TPU v7x, 256 devices: a whole 4x4x8 slice. The times are simulated.
256 devices in a mesh: fsdp: 64 (over z, x, core), dp: 4 (over y).
Axes of the slice: x: 4, y: 4, z: 8, core: 2. Of those that a mesh axis runs over, the one named last changes fastest.
Arguments:
- gradient: bfloat16 [8, 1024, 8, 1024], P(None, 'fsdp', None, 'dp'), may hold values from -2 to 2
- second_moment: float32 [8, 1024, 8, 1024], P(None, 'fsdp', None, 'dp'), may hold values from 1e-06 to 0.001
- stat_left: float32 [128, 1024, 1024], P('fsdp', 'dp'), may hold values from -6 to 6
- stat_right: float32 [128, 1024, 1024], P('fsdp', 'dp'), may hold values from -6 to 6
- root_left: bfloat16 [128, 1024, 1024], P('fsdp', 'dp'), may hold values from -0.1875 to 0.1875
- root_right: bfloat16 [128, 1024, 1024], P('fsdp', None, 'dp'), may hold values from -0.1875 to 0.1875
- block_slot: int32 [64], replicated, may hold values from 0 to 127, as said below
Outputs:
- new_left: float32 [128, 1024, 1024], P('fsdp', 'dp')
- new_right: float32 [128, 1024, 1024], P('fsdp', 'dp')
- new_second: float32 [8, 1024, 8, 1024], P(None, 'fsdp', None, 'dp')
- direction: bfloat16 [8, 1024, 8, 1024], P(None, 'fsdp', None, 'dp')
Inputs may be any that keep to these rules, and one draw needn't show every extreme that they name: `block_slot`: all entries differ; slot s belongs to owner s // 2; some owner holds 2 blocks.
All inputs are finite; a program needn't handle non-finite values.
Results may differ from a plain program's by a relative error of at most 0.0058.
Values may be sent and summed in bfloat16 or wider, within the bound.
No kernel may reach another device: no remote copies, remote signals or barrier semaphores. Data moves between devices by JAX's collectives and lax.ppermute only.
A program may use at most 64 MiB of HBM per device.

v0:
```python
import jax
import jax.numpy as jnp
from jax import lax
from jax.sharding import PartitionSpec as P


def body(gradient, second_moment, stat_left, stat_right, root_left, root_right, block_slot):
    fsdp_count = lax.axis_size("fsdp")
    row_blocks, piece_rows, column_blocks, quarter = gradient.shape
    blocks = row_blocks * column_blocks
    slot_count = stat_left.shape[0]
    total_slots = slot_count * fsdp_count
    column_start = lax.axis_index("dp") * quarter
    slot_block = (
        jnp.full((total_slots,), -1, jnp.int32)
        .at[block_slot]
        .set(jnp.arange(blocks, dtype=jnp.int32))
    )
    filled = slot_block >= 0
    picked = jnp.maximum(slot_block, 0)
    grad_values = gradient.astype(jnp.float32)
    new_second = 0.9 * second_moment + 0.1 * grad_values * grad_values
    adam = grad_values / (jnp.sqrt(new_second) + 1e-08)
    adam_part = jnp.sum(adam * adam, axis=(1, 3)).reshape(blocks)
    pieces = gradient.transpose(0, 2, 1, 3).reshape(blocks, gradient.shape[1], gradient.shape[3])
    column_part = lax.all_to_all(
        jnp.where(filled[:, None, None], pieces[picked], jnp.zeros((), gradient.dtype)),
        "fsdp",
        split_axis=0,
        concat_axis=1,
        tiled=True,
    )
    whole_block = lax.all_gather(column_part, "dp", axis=2, tiled=True)
    row_part = lax.dynamic_slice_in_dim(whole_block, column_start, quarter, 1)
    new_left = stat_left + jnp.einsum(
        "sik,sjk->sij", row_part, whole_block, preferred_element_type=jnp.float32
    )
    new_right = stat_right + jnp.einsum(
        "ski,skj->sij", column_part, whole_block, preferred_element_type=jnp.float32
    )
    mixed = jnp.einsum(
        "sik,skj->sij", whole_block, root_right, preferred_element_type=jnp.float32
    ).astype(jnp.bfloat16)
    left_whole = lax.all_gather(root_left, "dp", axis=1, tiled=True)
    update = jnp.einsum(
        "sik,skj->sij", left_whole, mixed, preferred_element_type=jnp.float32
    ).astype(jnp.bfloat16)
    returned_slots = lax.all_to_all(update, "fsdp", split_axis=1, concat_axis=0, tiled=True)
    returned = returned_slots[block_slot].astype(jnp.float32)
    update_part = jnp.sum(returned * returned, axis=(1, 2))
    adam_total, update_total = lax.psum((adam_part, update_part), ("fsdp", "dp"))
    scaling = jnp.sqrt(adam_total / (update_total + 1e-06))
    scaled = (scaling[:, None, None] * returned).astype(jnp.bfloat16)
    direction = scaled.reshape(row_blocks, column_blocks, piece_rows, quarter).transpose(0, 2, 1, 3)
    return (new_left, new_right, new_second, direction)


def solution(mesh):
    placed = (
        P(None, "fsdp", None, "dp"),
        P(None, "fsdp", None, "dp"),
        P("fsdp", "dp", None),
        P("fsdp", "dp", None),
        P("fsdp", "dp", None),
        P("fsdp", None, "dp"),
        P(),
    )
    return jax.shard_map(
        body,
        mesh=mesh,
        in_specs=placed,
        out_specs=(
            P("fsdp", "dp", None),
            P("fsdp", "dp", None),
            P(None, "fsdp", None, "dp"),
            P(None, "fsdp", None, "dp"),
        ),
        check_vma=False,
    )
```

profile of v0, /device:TPU:1, one launch (start us, length us, event | category | flops | bytes accessed | tf_op | source)
XLA Modules:
  0.0 252.8 jit_solution(8941037831152248848)
XLA Ops:
  7.2 0.7 all-gather.5.cloned.1.call-update
  8.0 1.1 copy.18
  9.1 0.7 compare_select_fusion
  9.8 0.8 scatter_custom_fusion
  10.6 0.6 gather_fusion
  11.2 0.2 broadcast_select_fusion
  11.5 40.8 %all_to_all.36 = bf16[128,16,256]{2,1,0:T(8,128)(2,1)S(1)} all-to-all(bf16[128,16,256]{2,1,0:T(8,128)(2,1)S(1)} %broadcast_select_fusion), channel_id=1, replica_groups=mesh['fsdp'=64,'dp'=4] {'fsdp'}, dimensions={0} | all-to-all | bytes 2097152 | tf_op jit(solution)/shard_map/all_to_all | solution.py:26
  52.2 1.1 copy.19
  53.3 11.2 %all-gather.5.cloned.1.call-done = bf16[2,1024,1024]{2,1,0:T(8,128)(2,1)} async-done(((bf16[2,256,1024]{2,1,0:T(8,128)(2,1)}), bf16[2,1024,1024]{2,1,0:T(8,128)(2,1)}) %all-gather.5.cloned.1.call-update) | async-done | bytes 4194320 | tf_op jit(solution)/shard_map/all_gather | solution.py:44
  64.5 56.5 %all-gather.3.cloned.1.call-done = bf16[2,1024,1024]{2,1,0:T(8,128)(2,1)} async-done(((bf16[2,1024,256]{2,1,0:T(8,128)(2,1)}), bf16[2,1024,1024]{2,1,0:T(8,128)(2,1)}) %all-gather.3.cloned.1.call-update) | async-done | bytes 4194320 | tf_op jit(solution)/shard_map/all_gather | solution.py:33
  121.0 5.9 %fusion = bf16[2,1024,256]{1,2,0:T(8,128)(2,1)S(1)} fusion(bf16[2,1024,1024]{2,1,0:T(8,128)(2,1)} %all-gather.5.cloned.1.call-done, bf16[2,1024,1024]{2,1,0:T(8,128)(2,1)} %all-gather.3.cloned.1.call-done, bf16[2,1024,256]{2,1,0:T(8,128)(2,1)S(1)} %copy-done), kind=kOutput, calls=%fused_computation.8 | convolution fusion | flops 2148532224 | bytes 10485760 | tf_op jit(solution)/shard_map/sik,skj->sij/dot_general | solution.py:45
  126.8 2.1 copy.22
  128.9 11.5 %all-to-all-start.1 = ((bf16[2,1024,256]{2,0,1:T(2,128)(2,1)}), bf16[2,1024,256]{2,0,1:T(2,128)(2,1)S(1)}, u32[]{:S(2)}, u32[]{:S(2)}) async-start(bf16[2,1024,256]{2,0,1:T(2,128)(2,1)} %copy.22), calls=%async_computation.1 | async-start | bytes 2097152 | tf_op jit(solution)/shard_map/all_to_all | solution.py:48
  140.5 2.8 %fusion.4 = (f32[8,8]{1,0:T(8,128)S(1)}, f32[8,16,8,256]{3,2,1,0:T(8,128)}) fusion(bf16[8,16,8,256]{3,2,1,0:T(8,128)(2,1)S(1)} %copy-done.3, f32[8,16,8,256]{3,2,1,0:T(8,128)} %param.8), kind=kLoop, calls=%fused_computation.15 | loop fusion | flops 2359232 | bytes 2621696 | tf_op jit(solution)/shard_map/reduce_sum | solution.py:24
  143.4 5.9 %convolution_add_fusion.1 = f32[2,256,1024]{2,1,0:T(8,128)} fusion(f32[2,256,1024]{2,1,0:T(8,128)} %param.9, bf16[2,1024,1024]{2,1,0:T(8,128)(2,1)} %all-gather.3.cloned.1.call-done, s32[]{:T(128)S(6)} %select_n.14), kind=kOutput, calls=%fused_computation.5 | convolution fusion | flops 1074266112 | bytes 9437188 | tf_op jit(solution)/shard_map/sik,sjk->sij/dot_general | solution.py:35
  149.3 2.6 %convolution_add_fusion = f32[2,256,1024]{2,1,0:T(8,128)} fusion(f32[2,256,1024]{2,1,0:T(8,128)S(1)} %copy-done.4, bf16[2,1024,256]{2,1,0:T(8,128)(2,1)S(1)} %bitcast.25, bf16[2,1024,1024]{2,1,0:T(8,128)(2,1)S(1)} %copy-done.1), kind=kOutput, calls=%fused_computation.4 | convolution fusion | flops 1074266112 | bytes 9437184 | tf_op jit(solution)/shard_map/ski,skj->sij/dot_general | solution.py:38
  151.9 16.5 %all-to-all-done.1 = bf16[2,1024,256]{2,0,1:T(2,128)(2,1)S(1)} async-done(((bf16[2,1024,256]{2,0,1:T(2,128)(2,1)}), bf16[2,1024,256]{2,0,1:T(2,128)(2,1)S(1)}, u32[]{:S(2)}, u32[]{:S(2)}) %all-to-all-start.1) | async-done | bytes 1048608 | tf_op jit(solution)/shard_map/all_to_all | solution.py:48
  168.4 0.1 copy.23
  168.6 0.1 copy.24
  168.7 0.6 gather_fusion.1
  169.3 0.6 multiply_reduce_fusion
  169.9 74.9 %all-reduce = (f32[64]{0:T(128)S(1)}, f32[64]{0:T(128)S(1)}) all-reduce(f32[64]{0:T(128)S(1)} %reshape.23, f32[64]{0:T(128)S(1)} %multiply_reduce_fusion), channel_id=1, replica_groups=mesh['fsdp'=64,'dp'=4] {'fsdp','dp'}, use_global_device_ids=true, to_apply=%region_2.3 | all-reduce | flops 128 | bytes 1024 | tf_op jit(solution)/shard_map/psum | solution.py:51
  244.8 0.2 fusion.5
  245.0 1.0 copy.25
  (21 shorter events, 0.3 us)
Async XLA Ops:
  7.2 113.8 %copy-start = (bf16[2,1024,256]{2,1,0:T(8,128)(2,1)S(1)}, bf16[2,1024,256]{2,1,0:T(8,128)(2,1)}, u32[]{:S(2)}) copy-start(bf16[2,1024,256]{2,1,0:T(8,128)(2,1)} %param.12) | copy-start | bytes 3145732
  7.2 57.3 %all-gather.5.cloned.1.call-start = ((), (), s32[]{:S(2)}) async-start(), calls=%async_computation.3 | async-start | bytes 5242880 | tf_op jit(solution)/shard_map/all_gather | solution.py:44
  7.9 113.0 %all-gather.3.cloned.1.call-start = ((), (), s32[]{:S(2)}) async-start(), calls=%async_computation.2 | async-start | bytes 5242880 | tf_op jit(solution)/shard_map/all_gather | solution.py:33
  126.8 13.6 %copy-start.3 = (bf16[8,16,8,256]{3,2,1,0:T(8,128)(2,1)S(1)}, bf16[8,16,8,256]{3,2,1,0:T(8,128)(2,1)}, u32[]{:S(2)}) copy-start(bf16[8,16,8,256]{3,2,1,0:T(8,128)(2,1)} %param.7) | copy-start | bytes 1572868
  128.9 39.5 %all-to-all-start.1 = ((bf16[2,1024,256]{2,0,1:T(2,128)(2,1)}), bf16[2,1024,256]{2,0,1:T(2,128)(2,1)S(1)}, u32[]{:S(2)}, u32[]{:S(2)}) async-start(bf16[2,1024,256]{2,0,1:T(2,128)(2,1)} %copy.22), calls=%async_computation.1 | async-start | bytes 2097152 | tf_op jit(solution)/shard_map/all_to_all | solution.py:48
  143.3 6.0 %copy-start.1 = (bf16[2,1024,1024]{2,1,0:T(8,128)(2,1)S(1)}, bf16[2,1024,1024]{2,1,0:T(8,128)(2,1)}, u32[]{:S(2)}) copy-start(bf16[2,1024,1024]{2,1,0:T(8,128)(2,1)} %all-gather.3.cloned.1.call-done) | copy-start | bytes 12582916
  143.3 5.9 %copy-start.2 = (bf16[2,64,16,256]{3,2,1,0:T(8,128)(2,1)S(1)}, bf16[2,64,16,256]{3,2,1,0:T(8,128)(2,1)}, u32[]{:S(2)}) copy-start(bf16[2,64,16,256]{3,2,1,0:T(8,128)(2,1)} %copy.19) | copy-start | bytes 3145732
  143.3 5.9 %copy-start.4 = (f32[2,256,1024]{2,1,0:T(8,128)S(1)}, f32[2,256,1024]{2,1,0:T(8,128)}, u32[]{:S(2)}) copy-start(f32[2,256,1024]{2,1,0:T(8,128)} %param.10) | copy-start | bytes 6291460
Sparse Core Ops, SparseCore 0:
  9.8 54.5 all-gather.4
  66.8 54.0 all-gather.2
where the time goes:
time: 253 us
  blocking collectives  116 us (46%)
  waiting for transfers between devices  84.9 us (34%)
  matrix products  14.4 us (6%)
  between operations  14.2 us (6%)
  starting transfers between devices  11.6 us (5%)
  local copies, waits for them, and re-layouts  7.72 us (3%)
  other arithmetic  4.4 us (2%)
    psum x1, blocking collectives, body(): lax.psum((adam_part, update_part), ('fsdp', 'dp'))  74.9 us
    all_gather x1, waiting for transfers between devices, body(): whole_block = lax.all_gather(column_part, 'dp', axis=2, tiled=True)  56.5 us
    all_to_all x1, blocking collectives, body(): lax.all_to_all(jnp.where(filled[:, None, None], pieces[picked], jnp.zeros...  40.8 us
    all_to_all x1, waiting for transfers between devices, body(): lax.all_to_all(update, 'fsdp', split_axis=1, concat_axis=0, tiled=True)  16.5 us
    all_to_all x1, starting transfers between devices, body(): lax.all_to_all(update, 'fsdp', split_axis=1, concat_axis=0, tiled=True)  11.5 us
    all_gather x1, waiting for transfers between devices, body(): left_whole = lax.all_gather(root_left, 'dp', axis=1, tiled=True)  11.2 us
    dot_general x1, matrix products, body(): jnp.einsum('sik,sjk->sij', row_part, whole_block, preferred_element_type=...  5.92 us
    dot_general x1, matrix products, body(): jnp.einsum('sik,skj->sij', left_whole, mixed, preferred_element_type=jnp....  5.86 us
  transfers between devices with their start and end apart: 3, of which 3 were waited for; matrix products, arithmetic and copies ran while one was open for 6% of the time, Pallas kernels for 0%

commit v1 on v0

v1 whole, which is shorter than its diff:
```python
import jax
import jax.numpy as jnp
from jax import lax
from jax.experimental import pallas as pl
from jax.experimental.pallas import tpu as pltpu
from jax.sharding import PartitionSpec as P

AXES = ("fsdp", "dp")
F32 = jnp.float32
BF16 = jnp.bfloat16
SMEM = pl.BlockSpec(memory_space=pltpu.SMEM)
VMEM = pl.BlockSpec(memory_space=pltpu.VMEM)
MIB = 1 << 20


def local(kernel, outs, inputs, scratch=(), limit=16, flops=0, moved=0):
    return pl.pallas_call(
        kernel,
        out_shape=outs,
        in_specs=[SMEM] + [VMEM] * (len(inputs) - 1),
        out_specs=jax.tree.map(lambda _: VMEM, outs),
        scratch_shapes=list(scratch),
        compiler_params=pltpu.CompilerParams(vmem_limit_bytes=limit * MIB),
        cost_estimate=pl.CostEstimate(flops=flops, bytes_accessed=moved, transcendentals=0),
    )(*inputs)


def shape(dims, dtype):
    return jax.ShapeDtypeStruct(dims, dtype)


def spread_row(slot):
    return ((slot >> 2) << 3) + (slot & 3)


def spread_kernel(slot_ref, grad_ref, after_ref, out_ref, wide):
    row_blocks, rows, column_blocks, quarter = grad_ref.shape
    half = quarter // 2
    out_ref[...] = jnp.zeros_like(out_ref)
    size = wide.shape[0] // 2
    for h in range(2):
        wide[h * size : (h + 1) * size, :] = grad_ref[..., h * half : (h + 1) * half].astype(F32).reshape(size, half)
    for b in range(row_blocks * column_blocks):
        start = (b // column_blocks) * rows * column_blocks + b % column_blocks
        at = spread_row(slot_ref[b])
        out_ref[at] = wide[pl.ds(start, rows, stride=column_blocks), :].astype(BF16)
        out_ref[at + 4] = wide[pl.ds(size + start, rows, stride=column_blocks), :].astype(BF16)


def moment_kernel(slot_ref, grad_ref, second_ref, new_ref, sent_ref, part):
    row_blocks, _, column_blocks, _ = grad_ref.shape
    sent_ref[...] = jnp.zeros_like(sent_ref)
    for r in range(row_blocks):
        g = grad_ref[r].astype(F32)
        new = 0.9 * second_ref[r] + 0.1 * g * g
        new_ref[r] = new
        adam = g / (jnp.sqrt(new) + 1e-08)
        sums = jnp.sum(jnp.sum(adam * adam, axis=0), axis=1, keepdims=True)
        part[r * column_blocks : (r + 1) * column_blocks, :] = jnp.broadcast_to(sums, (column_blocks, 128))
    for b in range(row_blocks * column_blocks):
        at = spread_row(slot_ref[b])
        sent_ref[at] = part[b : b + 1, :]
        sent_ref[at + 4] = part[b : b + 1, :]


def pack_kernel(spot_ref, left_ref, right_ref, *outs):
    half = left_ref.shape[1] // 2
    chips = len(outs) // 2
    for m in range(chips):
        to = spot_ref[0] ^ m
        part = pl.ds(pl.multiple_of((to >> 1) * half, half), half)
        outs[m][...] = left_ref[to & 1, part, :]
        outs[chips + m][...] = right_ref[to & 1, :, part]


def update_kernel(spot_ref, adam_ref, own_ref, other_ref, *refs):
    lefts, lefts2, rights = refs[0:4], refs[4:8], refs[8:12]
    grad, update_ref, norm_ref, note_ref, root, mixed, rows = refs[12:]
    core, lane = spot_ref[1], spot_ref[2]
    owners, chips, piece, half = own_ref.shape
    order = grad.shape[0]
    for d in range(chips):
        mine = pl.multiple_of((2 * d + core) * half, half)
        theirs = pl.multiple_of((2 * d + 1 - core) * half, half)
        grad[:, pl.ds(mine, half)] = own_ref[:, d].reshape(order, half)
        grad[:, pl.ds(theirs, half)] = other_ref[:, d].reshape(order, half)
        root[:, pl.ds(pl.multiple_of((lane ^ d) * half, half), half)] = rights[d][...]
    for t in range(0, order, 512):
        mixed[t : t + 512, :] = jnp.dot(grad[t : t + 512, :], root[...], preferred_element_type=F32).astype(BF16)
    total = jnp.zeros((8, 128), F32)
    count = half // piece
    for parts, which, first in ((lefts, core, lane), (lefts2, 1 - core, lane ^ 2)):
        for m in range(chips):
            rows[m * half : (m + 1) * half, :] = parts[m][...]
        part = jnp.dot(rows[...], mixed[...], preferred_element_type=F32).astype(BF16)
        wide = part.astype(F32)
        squares = jnp.sum((wide * wide).reshape(chips * half // 8, 8, chips * half), axis=0)
        for y in range(chips):
            total = total + squares[:, y * half : (y + 1) * half]
            for m in range(chips):
                block = part[m * half : (m + 1) * half, y * half : (y + 1) * half]
                spot = (first ^ m) * (2 * count) + which * count
                update_ref[pl.ds(spot, count), y] = block.reshape(count, piece, half)
    norm = jnp.sum(jnp.sum(total, axis=0, keepdims=True), axis=1, keepdims=True)
    norm_ref[...] = jnp.broadcast_to(norm, norm_ref.shape)
    note_ref[...] = jnp.broadcast_to(jnp.sum(adam_ref[...], axis=0), note_ref.shape)


def product_kernel(spot_ref, grad, *refs):
    outs, (rows, columns) = refs[:-2], refs[-2:]
    core, lane = spot_ref[1], spot_ref[2]
    order = grad.shape[0]
    half = rows.shape[0] // 4
    for m in range(4):
        d = lane ^ m
        rows[m * half : (m + 1) * half, :] = grad[pl.ds(pl.multiple_of(d * 2 * half + core * half, half), half), :]
        columns[m * half : (m + 1) * half, :] = grad[:, pl.ds(pl.multiple_of((2 * d + core) * half, half), half)].T
    for n in range(0, order, 256):
        left = lax.dot_general(rows[...], grad[n : n + 256, :], (((1,), (1,)), ((), ())), preferred_element_type=F32)
        right = jnp.dot(columns[...], grad[:, n : n + 256], preferred_element_type=F32)
        for m, out in enumerate(outs):
            out[:half, n : n + 256] = left[m * half : (m + 1) * half].astype(BF16)
            out[half:, n : n + 256] = right[m * half : (m + 1) * half].astype(BF16)


def graft_kernel(spot_ref, update_ref, norm_ref, norm2_ref, note_ref, after_ref, out_ref):
    scale = jnp.sqrt(note_ref[0:1, :] / (norm_ref[0:1, :] + norm2_ref[0:1, :] + 1e-06))
    out_ref[...] = (update_ref[...].astype(F32) * scale[None, None]).astype(BF16)


def stat_kernel(spot_ref, p0, p1, p2, p3, left_ref, right_ref, new_left_ref, new_right_ref):
    half = left_ref.shape[1]
    for m, ref in enumerate((p0, p1, p2, p3)):

        @pl.when(pl.program_id(0) == m)
        def _():
            new_left_ref[0] = left_ref[0] + ref[:half, :].astype(F32)
            new_right_ref[0] = right_ref[0] + ref[half:, :].astype(F32)


def direction_kernel(slot_ref, values_ref, out_ref, wide):
    row_blocks, rows, column_blocks, quarter = out_ref.shape
    half = quarter // 2
    size = wide.shape[0] // 2
    for b in range(row_blocks * column_blocks):
        at = spread_row(slot_ref[b])
        start = (b // column_blocks) * rows * column_blocks + b % column_blocks
        wide[pl.ds(start, rows, stride=column_blocks), :] = values_ref[at].astype(F32)
        wide[pl.ds(size + start, rows, stride=column_blocks), :] = values_ref[at + 4].astype(F32)
    for h in range(2):
        part = wide[h * size : (h + 1) * size, :].reshape(row_blocks, rows, column_blocks, half)
        out_ref[..., h * half : (h + 1) * half] = part.astype(out_ref.dtype)


def body(gradient, second_moment, stat_left, stat_right, root_left, root_right, block_slot):
    owners = lax.axis_size("fsdp")
    chips = lax.axis_size("dp")
    devices = owners * chips
    row_blocks, piece_rows, column_blocks, quarter = gradient.shape
    blocks = row_blocks * column_blocks
    order = stat_left.shape[2]
    half = quarter // 2
    core = lax.axis_index("fsdp") % 2
    chip = lax.axis_index("dp")
    spot = jnp.stack([chip, core, 2 * core + chip % 2]).astype(jnp.int32)

    def matching(m, back):
        pairs = []
        for k in range(owners // 2):
            for c in range(2):
                for d in range(chips):
                    c2, j = (d ^ m) >> 1, (d ^ m) & 1
                    here = (2 * k + c) * chips + d
                    there = (2 * k + c2) * chips + 2 * c + j
                    pairs.append((there, here) if back else (here, there))
        return pairs

    swap = [(i, i ^ 1) for i in range(owners)]

    packed = local(
        pack_kernel,
        [shape((half, order), BF16)] * chips + [shape((order, half), BF16)] * chips,
        (spot, root_left, root_right),
        moved=4 * MIB,
    )
    lefts = [lax.ppermute(packed[m], AXES, matching(m, False)) for m in range(chips)]
    rights = [lax.ppermute(packed[chips + m], AXES, matching(m, False)) for m in range(chips)]

    pieces = local(
        spread_kernel, shape((devices, piece_rows, half), BF16), (block_slot, gradient, packed[0]),
        scratch=[pltpu.VMEM((2 * blocks * piece_rows, half), F32)], moved=MIB * 3 // 2,
    )
    own = lax.all_to_all(pieces, AXES, split_axis=0, concat_axis=0, tiled=True)

    new_second, sent = local(
        moment_kernel,
        [shape(second_moment.shape, F32), shape((devices, 1, 128), F32)],
        (block_slot, gradient, second_moment),
        scratch=[pltpu.VMEM((blocks, 128), F32)], moved=MIB * 5 // 2,
    )
    adam = lax.all_to_all(sent, AXES, split_axis=0, concat_axis=0, tiled=True)

    own, adam = lax.optimization_barrier((own, adam))
    lefts2 = [lax.ppermute(part, "fsdp", swap) for part in lefts]
    other = lax.ppermute(own, "fsdp", swap)

    cut = (owners, chips, piece_rows, half)
    grad, update, norm, note = local(
        update_kernel,
        [shape((order, order), BF16), shape(cut, BF16), shape((8, 128), F32), shape((8, 128), F32)],
        (spot, adam, own.reshape(cut), other.reshape(cut), *lefts, *lefts2, *rights),
        scratch=[
            pltpu.VMEM((order, order // 2), BF16), pltpu.VMEM((order, order // 2), BF16),
            pltpu.VMEM((order // 2, order), BF16),
        ],
        limit=32, flops=2 * order * order * order, moved=8 * MIB,
    )
    norm2 = lax.ppermute(norm, "fsdp", swap)
    products = local(
        product_kernel, [shape((2 * half, order), BF16)] * chips, (spot, grad),
        scratch=[pltpu.VMEM((order // 2, order), BF16)] * 2,
        limit=24, flops=2 * order * order * order, moved=4 * MIB,
    )
    back = local(graft_kernel, shape(cut, BF16), (spot, update, norm, norm2, note, products[0]), moved=2 * MIB)
    products = [lax.ppermute(products[m], AXES, matching(m, True)) for m in range(chips)]
    returned = lax.all_to_all(back.reshape(devices, piece_rows, half), AXES, split_axis=0, concat_axis=0, tiled=True)

    whole = pl.BlockSpec((2 * half, order), lambda m, s: (0, 0))
    piece = pl.BlockSpec((1, half, order), lambda m, s: ((s[0] ^ m) & 1, (s[0] ^ m) >> 1, 0))
    new_left, new_right = pl.pallas_call(
        stat_kernel,
        out_shape=[shape(stat_left.shape, F32), shape(stat_right.shape, F32)],
        grid_spec=pltpu.PrefetchScalarGridSpec(
            num_scalar_prefetch=1, grid=(chips,), in_specs=[whole] * chips + [piece] * 2, out_specs=[piece] * 2
        ),
        compiler_params=pltpu.CompilerParams(vmem_limit_bytes=16 * MIB),
        cost_estimate=pl.CostEstimate(flops=0, bytes_accessed=10 * MIB, transcendentals=0),
    )(spot, *products, stat_left, stat_right)

    direction = local(
        direction_kernel, shape(gradient.shape, gradient.dtype), (block_slot, returned),
        scratch=[pltpu.VMEM((2 * blocks * piece_rows, half), F32)],
        moved=2 * MIB,
    )
    return (new_left, new_right, new_second, direction)


def solution(mesh):
    placed = (
        P(None, "fsdp", None, "dp"),
        P(None, "fsdp", None, "dp"),
        P("fsdp", "dp", None),
        P("fsdp", "dp", None),
        P("fsdp", "dp", None),
        P("fsdp", None, "dp"),
        P(),
    )
    return jax.shard_map(
        body,
        mesh=mesh,
        in_specs=placed,
        out_specs=(
            P("fsdp", "dp", None),
            P("fsdp", "dp", None),
            P(None, "fsdp", None, "dp"),
            P(None, "fsdp", None, "dp"),
        ),
        check_vma=False,
    )
```

time: 253 us -> 160 us (0.63)
  blocking collectives: 116 us -> 36.5 us
  starting transfers between devices: 11.6 us -> 52.7 us
  waiting for transfers between devices: 84.9 us -> 45.2 us
  Pallas kernels: 0 us -> 17.4 us
  matrix products: 14.4 us -> 0 us
  between operations: 14.2 us -> 0.86 us
  other arithmetic: 4.4 us -> 0.08 us
    psum x1 -> x0, blocking collectives: 74.9 us -> none  [body(): lax.psum((adam_part, update_part), ('fsdp', 'dp'))]
    all_gather x2 -> x0, waiting for transfers between devices: 67.7 us -> none  [the longest x1 56.5 us: body(): whole_block = lax.all_gather(column_part, 'dp', axis=2, tiled=True)]
    ppermute x0 -> x18, waiting for transfers between devices: none -> 36.3 us  [the longest x4 29.2 us: body(): lax.ppermute(products[m], AXES, matching(m, True))]
    ppermute x0 -> x18, starting transfers between devices: none -> 30.9 us  [the longest x4 10.1 us: body(): lax.ppermute(packed[chips + m], AXES, matching(m, False))]
    pallas_call x0 -> x8, Pallas kernels: none -> 17.4 us  [the longest x7 14.3 us: local(): pl.pallas_call(kernel, out_shape=outs, in_specs=[SMEM] + [VMEM] * (len(in...]
    dot_general x3 -> x0, matrix products: 14.4 us -> none  [the longest x1 5.92 us: body(): jnp.einsum('sik,sjk->sij', row_part, whole_block, preferred_element_type=...]
    all_to_all x1 -> x2, starting transfers between devices: 11.5 us -> 21.8 us  [the longest x1 15.7 us: body(): adam = lax.all_to_all(sent, AXES, split_axis=0, concat_axis=0, tiled=True)]
    all_to_all x1 -> x2, waiting for transfers between devices: 16.5 us -> 8.89 us  [the longest x1 8.89 us: body(): adam = lax.all_to_all(sent, AXES, split_axis=0, concat_axis=0, tiled=True)]
  transfers between devices with their start and end apart: 3 -> 20, of which waited for: 3 -> 9; matrix products, arithmetic and copies ran while one was open for 6% -> 0% of each run, Pallas kernels for 0% -> 5%
where the time goes in v1:
time: 160 us; the launch traced here: 159 us
  starting transfers between devices  52.7 us (33%)
  waiting for transfers between devices  45.2 us (28%)
  blocking collectives  36.5 us (23%)
  Pallas kernels  17.4 us (11%)
  local copies, waits for them, and re-layouts  6.48 us (4%)
    all_to_all x1, blocking collectives, body(): own = lax.all_to_all(pieces, AXES, split_axis=0, concat_axis=0, tiled=True)  36.5 us
    ppermute x4, waiting for transfers between devices, body(): lax.ppermute(products[m], AXES, matching(m, True))  29.2 us
    all_to_all x1, starting transfers between devices, body(): adam = lax.all_to_all(sent, AXES, split_axis=0, concat_axis=0, tiled=True)  15.7 us
    pallas_call x7, Pallas kernels, local(): pl.pallas_call(kernel, out_shape=outs, in_specs=[SMEM] + [VMEM] * (len(in...  14.3 us
    ppermute x4, starting transfers between devices, body(): lax.ppermute(packed[chips + m], AXES, matching(m, False))  10.1 us
    all_to_all x1, waiting for transfers between devices, body(): adam = lax.all_to_all(sent, AXES, split_axis=0, concat_axis=0, tiled=True)  8.89 us
    ppermute x4, starting transfers between devices, body(): lax.ppermute(products[m], AXES, matching(m, True))  8.66 us
    ppermute x4, starting transfers between devices, body(): lax.ppermute(packed[m], AXES, matching(m, False))  6.74 us
  transfers between devices with their start and end apart: 20, of which 9 were waited for; matrix products, arithmetic and copies ran while one was open for 0% of the time, Pallas kernels for 5%

profile of v1, /device:TPU:1, one launch (start us, length us, event | category | flops | bytes accessed | tf_op | source)
XLA Modules:
  0.0 159.1 jit_solution(14776084042915222656)
XLA Ops:
  3.6 2.3 %shard_map.104 = (f32[8,16,8,256]{3,2,1,0:T(8,128)}, f32[256,1,128]{2,1,0:T(1,128)}) custom-call(s32[64]{0:T(128)S(1)} %copy-done.8, bf16[8,16,8,256]{3,2,1,0:T(8,128)(2,1)S(1)} %copy-done.2, f32[8,16,8,256]{3,2,1,0:T(8,128)S(1)} %copy-done.6), custom_call_target="tpu_custom_call" | custom-call | bytes 2621440 | tf_op jit(solution)/shard_map/pallas_call | solution.py:17
  5.9 15.7 %all-to-all-start.1 = ((f32[256,1,128]{2,1,0:T(1,128)}), f32[256,1,128]{2,1,0:T(1,128)S(1)}, u32[]{:S(2)}, u32[]{:S(2)}) async-start(f32[256,1,128]{2,1,0:T(1,128)} %get-tuple-element.27), calls=%async_computation.1 | async-start | bytes 262144 | tf_op jit(solution)/shard_map/all_to_all | solution.py:201
  25.3 8.9 %all-to-all-done.1.adam_ref = f32[256,1,128]{2,1,0:T(1,128)S(1)} async-done(((f32[256,1,128]{2,1,0:T(1,128)}), f32[256,1,128]{2,1,0:T(1,128)S(1)}, u32[]{:S(2)}, u32[]{:S(2)}) %all-to-all-start.1) | async-done | bytes 131104 | tf_op jit(solution)/shard_map/all_to_all | solution.py:201
  34.2 36.5 %all_to_all.15 = bf16[256,16,128]{2,1,0:T(8,128)(2,1)S(1)} all-to-all(bf16[256,16,128]{2,1,0:T(8,128)(2,1)S(1)} %shard_map.103), channel_id=1, replica_groups=mesh['fsdp'=64,'dp'=4] {'fsdp','dp'}, dimensions={0} | all-to-all | bytes 2097152 | tf_op jit(solution)/shard_map/all_to_all | solution.py:193
  70.7 2.2 %collective-permute-start.2 = (bf16[128,1024]{1,0:T(8,128)(2,1)S(1)}, bf16[128,1024]{1,0:T(8,128)(2,1)S(1)}, u32[]{:S(2)}, u32[]{:S(2)}) collective-permute-start(bf16[128,1024]{1,0:T(8,128)(2,1)S(1)} %copy-done.14), channel_id=1, source_target_pairs={{0,1},{1,0},{2,5},{3,4},{4,3},{5,2},{6,7},{7,6},{8,9},{9,8},{10,13... | collective-permute-start | bytes 786440 | tf_op jit(solution)/shard_map/ppermute | solution.py:186
  73.8 3.4 %collective-permute-start.9 = (bf16[1024,128]{1,0:T(8,128)(2,1)S(1)}, bf16[1024,128]{1,0:T(8,128)(2,1)S(1)}, u32[]{:S(2)}, u32[]{:S(2)}) collective-permute-start(bf16[1024,128]{1,0:T(8,128)(2,1)S(1)} %get-tuple-element.33), channel_id=1, source_target_pairs={{0,0},{1,1},{2,4},{3,5},{4,2},{5,3},{6,6},{7,7},{8,8},{9,9},{10,12... | collective-permute-start | bytes 786440 | tf_op jit(solution)/shard_map/ppermute | solution.py:187
  77.2 2.2 %collective-permute-done.2.refs_1_ = bf16[128,1024]{1,0:T(8,128)(2,1)S(1)} collective-permute-done((bf16[128,1024]{1,0:T(8,128)(2,1)S(1)}, bf16[128,1024]{1,0:T(8,128)(2,1)S(1)}, u32[]{:S(2)}, u32[]{:S(2)}) %collective-permute-start.2) | collective-permute-done | bytes 262176 | tf_op jit(solution)/shard_map/ppermute | solution.py:186
  79.3 3.0 %collective-permute-start.10 = (bf16[1024,128]{1,0:T(8,128)(2,1)S(1)}, bf16[1024,128]{1,0:T(8,128)(2,1)S(1)}, u32[]{:S(2)}, u32[]{:S(2)}) collective-permute-start(bf16[1024,128]{1,0:T(8,128)(2,1)S(1)} %get-tuple-element.34), channel_id=1, source_target_pairs={{0,1},{1,0},{2,5},{3,4},{4,3},{5,2},{6,7},{7,6},{8,9},{9,8},{10,13... | collective-permute-start | bytes 786440 | tf_op jit(solution)/shard_map/ppermute | solution.py:187
  83.3 1.7 %collective-permute-done.4.refs_3_ = bf16[128,1024]{1,0:T(8,128)(2,1)S(1)} collective-permute-done((bf16[128,1024]{1,0:T(8,128)(2,1)S(1)}, bf16[128,1024]{1,0:T(8,128)(2,1)S(1)}, u32[]{:S(2)}, u32[]{:S(2)}) %collective-permute-start.4) | collective-permute-done | bytes 262176 | tf_op jit(solution)/shard_map/ppermute | solution.py:186
  84.9 2.8 %collective-permute-start.12 = (bf16[1024,128]{1,0:T(8,128)(2,1)S(1)}, bf16[1024,128]{1,0:T(8,128)(2,1)S(1)}, u32[]{:S(2)}, u32[]{:S(2)}) collective-permute-start(bf16[1024,128]{1,0:T(8,128)(2,1)S(1)} %get-tuple-element.36), channel_id=1, source_target_pairs={{0,5},{1,4},{2,1},{3,0},{4,7},{5,6},{6,3},{7,2},{8,13},{9,12},{10,... | collective-permute-start | bytes 786440 | tf_op jit(solution)/shard_map/ppermute | solution.py:187
  87.7 3.7 %collective-permute-start.1 = (bf16[128,1024]{1,0:T(8,128)(2,1)S(1)}, bf16[128,1024]{1,0:T(8,128)(2,1)S(1)}, u32[]{:S(2)}, u32[]{:S(2)}) collective-permute-start(bf16[128,1024]{1,0:T(8,128)(2,1)S(1)} %get-tuple-element.26.after_ref), channel_id=1, source_target_pairs={{0,0},{1,1},{2,4},{3,5},{4,2},{5,3},{6,6},{7,7},{8,8},{9,9},{10,12... | collective-permute-start | bytes 786440 | tf_op jit(solution)/shard_map/ppermute | solution.py:186
  91.5 2.4 %collective-permute-start.7 = (bf16[128,1024]{1,0:T(8,128)(2,1)S(1)}, bf16[128,1024]{1,0:T(8,128)(2,1)S(1)}, u32[]{:S(2)}, u32[]{:S(2)}) collective-permute-start(bf16[128,1024]{1,0:T(8,128)(2,1)S(1)} %collective-permute-done.3.refs_2_), channel_id=1, source_target_pairs={{0,4},{4,0},{8,12},{12,8},{16,20},{20,16},{24,28},{28,24},{32,36},... | collective-permute-start | bytes 786440 | tf_op jit(solution)/shard_map/ppermute | solution.py:204
  93.9 1.7 %collective-permute-done.12.refs_11_ = bf16[1024,128]{1,0:T(8,128)(2,1)S(1)} collective-permute-done((bf16[1024,128]{1,0:T(8,128)(2,1)S(1)}, bf16[1024,128]{1,0:T(8,128)(2,1)S(1)}, u32[]{:S(2)}, u32[]{:S(2)}) %collective-permute-start.12) | collective-permute-done | bytes 262176 | tf_op jit(solution)/shard_map/ppermute | solution.py:187
  95.6 2.4 %collective-permute-start.8 = (bf16[128,1024]{1,0:T(8,128)(2,1)S(1)}, bf16[128,1024]{1,0:T(8,128)(2,1)S(1)}, u32[]{:S(2)}, u32[]{:S(2)}) collective-permute-start(bf16[128,1024]{1,0:T(8,128)(2,1)S(1)} %collective-permute-done.4.refs_3_), channel_id=1, source_target_pairs={{0,4},{4,0},{8,12},{12,8},{16,20},{20,16},{24,28},{28,24},{32,36},... | collective-permute-start | bytes 786440 | tf_op jit(solution)/shard_map/ppermute | solution.py:204
  99.6 4.0 %shard_map.105 = (bf16[1024,1024]{1,0:T(8,128)(2,1)S(1)}, bf16[64,4,16,128]{3,2,1,0:T(8,128)(2,1)S(1)}, f32[8,128]{1,0:T(8,128)S(1)}, f32[8,128]{1,0:T(8,128)S(1)}) custom-call(s32[3]{0:T(128)S(1)} %pad_add_fusion.spot_ref, f32[256,1,128]{2,1,0:T(1,128)S(1)} %all-to-all-done.1.adam_ref, bf16[64,4,16,128]{3,2,1,0:T(8,128)(2,1)S(1)} %bitcast.6, ...), custom_call_target="tpu_custom_call" | custom-call | flops 2147483648 | bytes 8388608 | tf_op jit(solution)/shard_map/pallas_call | solution.py:17
  104.0 3.0 %shard_map.106 = (bf16[256,1024]{1,0:T(8,128)(2,1)S(1)}, bf16[256,1024]{1,0:T(8,128)(2,1)S(1)}, bf16[256,1024]{1,0:T(8,128)(2,1)S(1)}, bf16[256,1024]{1,0:T(8,128)(2,1)S(1)}) custom-call(s32[3]{0:T(128)S(1)} %pad_add_fusion.spot_ref, bf16[1024,1024]{1,0:T(8,128)(2,1)S(1)} %get-tuple-element.37.grad), custom_call_target="tpu_custom_call" | custom-call | flops 2147483648 | bytes 4194304 | tf_op jit(solution)/shard_map/pallas_call | solution.py:17
  107.1 1.7 %shard_map.108 = bf16[64,4,16,128]{3,2,1,0:T(8,128)(2,1)} custom-call(s32[3]{0:T(128)S(1)} %pad_add_fusion.spot_ref, bf16[64,4,16,128]{3,2,1,0:T(8,128)(2,1)S(1)} %get-tuple-element.45.update_ref, f32[8,128]{1,0:T(8,128)S(1)} %get-tuple-element.46.norm_ref, f32[8,128]{1,0:T(8,128)S(1)} %collective-permute-done.17.norm2_ref, ...), custom_call_target="tpu_custom_call" | custom-call | bytes 2097152 | tf_op jit(solution)/shard_map/pallas_call | solution.py:17
  108.8 6.1 %all-to-all-start.2 = ((bf16[256,16,128]{2,1,0:T(8,128)(2,1)}), bf16[256,16,128]{2,1,0:T(8,128)(2,1)S(1)}, u32[]{:S(2)}, u32[]{:S(2)}) async-start(bf16[256,16,128]{2,1,0:T(8,128)(2,1)} %bitcast.5), calls=%async_computation.2 | async-start | bytes 2097152 | tf_op jit(solution)/shard_map/all_to_all | solution.py:226
  114.9 3.0 %collective-permute-start.14 = (bf16[256,1024]{1,0:T(8,128)(2,1)}, bf16[256,1024]{1,0:T(8,128)(2,1)S(1)}, u32[]{:S(2)}, u32[]{:S(2)}) collective-permute-start(bf16[256,1024]{1,0:T(8,128)(2,1)} %copy-done.12), channel_id=1, source_target_pairs={{1,0},{0,1},{5,2},{4,3},{3,4},{2,5},{7,6},{6,7},{9,8},{8,9},{13,10... | collective-permute-start | bytes 1572872 | tf_op jit(solution)/shard_map/ppermute | solution.py:225
  118.9 4.7 %collective-permute-start.13 = (bf16[256,1024]{1,0:T(8,128)(2,1)}, bf16[256,1024]{1,0:T(8,128)(2,1)S(1)}, u32[]{:S(2)}, u32[]{:S(2)}) collective-permute-start(bf16[256,1024]{1,0:T(8,128)(2,1)} %copy-done.7), channel_id=1, source_target_pairs={{0,0},{1,1},{4,2},{5,3},{2,4},{3,5},{6,6},{7,7},{8,8},{9,9},{12,10... | collective-permute-start | bytes 1572872 | tf_op jit(solution)/shard_map/ppermute | solution.py:225
  123.6 15.2 %collective-permute-done.14.p1 = bf16[256,1024]{1,0:T(8,128)(2,1)S(1)} collective-permute-done((bf16[256,1024]{1,0:T(8,128)(2,1)}, bf16[256,1024]{1,0:T(8,128)(2,1)S(1)}, u32[]{:S(2)}, u32[]{:S(2)}) %collective-permute-start.14) | collective-permute-done | bytes 524320 | tf_op jit(solution)/shard_map/ppermute | solution.py:225
  138.8 11.9 %collective-permute-done.15.p2 = bf16[256,1024]{1,0:T(8,128)(2,1)S(1)} collective-permute-done((bf16[256,1024]{1,0:T(8,128)(2,1)}, bf16[256,1024]{1,0:T(8,128)(2,1)S(1)}, u32[]{:S(2)}, u32[]{:S(2)}) %collective-permute-start.15) | collective-permute-done | bytes 524320 | tf_op jit(solution)/shard_map/ppermute | solution.py:225
  150.7 2.1 %collective-permute-done.13.p0 = bf16[256,1024]{1,0:T(8,128)(2,1)S(1)} collective-permute-done((bf16[256,1024]{1,0:T(8,128)(2,1)}, bf16[256,1024]{1,0:T(8,128)(2,1)S(1)}, u32[]{:S(2)}, u32[]{:S(2)}) %collective-permute-start.13) | collective-permute-done | bytes 524320 | tf_op jit(solution)/shard_map/ppermute | solution.py:225
  154.4 3.1 %shard_map.107 = (f32[2,256,1024]{2,1,0:T(8,128)}, f32[2,256,1024]{2,1,0:T(8,128)}) custom-call(s32[3]{0:T(128)S(1)} %pad_add_fusion.spot_ref, bf16[256,1024]{1,0:T(8,128)(2,1)S(1)} %collective-permute-done.13.p0, bf16[256,1024]{1,0:T(8,128)(2,1)S(1)} %collective-permute-done.14.p1, bf16[256,1024]{1,0:T(8,128)(2,1)S(1)} %collective-permute-done.15.p2, ...), custom_call_target="tpu_custom_call" | custom-call | bytes 10485760 | tf_op jit(solution)/shard_map/pallas_call | solution.py:230
  (56 shorter events, 14.7 us)
Async XLA Ops:
  3.6 20.8 %copy-start.3 = (bf16[8,16,8,256]{3,2,1,0:T(8,128)(2,1)S(1)}, bf16[8,16,8,256]{3,2,1,0:T(8,128)(2,1)}, u32[]{:S(2)}) copy-start(bf16[8,16,8,256]{3,2,1,0:T(8,128)(2,1)} %grad_ref.3) | copy-start | bytes 1572868
  3.6 20.8 %copy-start.9 = (s32[64]{0:T(128)S(1)}, s32[64]{0:T(128)}, u32[]{:S(2)}) copy-start(s32[64]{0:T(128)} %slot_ref.5) | copy-start | bytes 772
  5.9 28.3 %all-to-all-start.1 = ((f32[256,1,128]{2,1,0:T(1,128)}), f32[256,1,128]{2,1,0:T(1,128)S(1)}, u32[]{:S(2)}, u32[]{:S(2)}) async-start(f32[256,1,128]{2,1,0:T(1,128)} %get-tuple-element.27), calls=%async_computation.1 | async-start | bytes 262144 | tf_op jit(solution)/shard_map/all_to_all | solution.py:201
  25.3 45.4 %copy-start.14 = (bf16[128,1024]{1,0:T(8,128)(2,1)S(1)}, bf16[128,1024]{1,0:T(8,128)(2,1)}, u32[]{:S(2)}) copy-start(bf16[128,1024]{1,0:T(8,128)(2,1)} %copy-done.13) | copy-start | bytes 786436
  70.7 28.9 %collective-permute-start = (bf16[256,16,128]{2,1,0:T(8,128)(2,1)S(1)}, bf16[256,16,128]{2,1,0:T(8,128)(2,1)S(1)}, u32[]{:S(2)}, u32[]{:S(2)}) collective-permute-start(bf16[256,16,128]{2,1,0:T(8,128)(2,1)S(1)} %all_to_all.15), channel_id=1, source_target_pairs={{0,4},{4,0},{8,12},{12,8},{16,20},{20,16},{24,28},{28,24},{32,36},... | collective-permute-start | bytes 3145736 | tf_op jit(solution)/shard_map/ppermute | solution.py:205
  70.7 8.6 %collective-permute-start.2 = (bf16[128,1024]{1,0:T(8,128)(2,1)S(1)}, bf16[128,1024]{1,0:T(8,128)(2,1)S(1)}, u32[]{:S(2)}, u32[]{:S(2)}) collective-permute-start(bf16[128,1024]{1,0:T(8,128)(2,1)S(1)} %copy-done.14), channel_id=1, source_target_pairs={{0,1},{1,0},{2,5},{3,4},{4,3},{5,2},{6,7},{7,6},{8,9},{9,8},{10,13... | collective-permute-start | bytes 786440 | tf_op jit(solution)/shard_map/ppermute | solution.py:186
  72.9 9.5 %collective-permute-start.3 = (bf16[128,1024]{1,0:T(8,128)(2,1)S(1)}, bf16[128,1024]{1,0:T(8,128)(2,1)S(1)}, u32[]{:S(2)}, u32[]{:S(2)}) collective-permute-start(bf16[128,1024]{1,0:T(8,128)(2,1)S(1)} %get-tuple-element.31), channel_id=1, source_target_pairs={{0,4},{1,5},{2,0},{3,1},{4,6},{5,7},{6,2},{7,3},{8,12},{9,13},{10,... | collective-permute-start | bytes 786440 | tf_op jit(solution)/shard_map/ppermute | solution.py:186
  73.7 11.3 %collective-permute-start.4 = (bf16[128,1024]{1,0:T(8,128)(2,1)S(1)}, bf16[128,1024]{1,0:T(8,128)(2,1)S(1)}, u32[]{:S(2)}, u32[]{:S(2)}) collective-permute-start(bf16[128,1024]{1,0:T(8,128)(2,1)S(1)} %get-tuple-element.32), channel_id=1, source_target_pairs={{0,5},{1,4},{2,1},{3,0},{4,7},{5,6},{6,3},{7,2},{8,13},{9,12},{10,... | collective-permute-start | bytes 786440 | tf_op jit(solution)/shard_map/ppermute | solution.py:186
  73.8 13.9 %collective-permute-start.9 = (bf16[1024,128]{1,0:T(8,128)(2,1)S(1)}, bf16[1024,128]{1,0:T(8,128)(2,1)S(1)}, u32[]{:S(2)}, u32[]{:S(2)}) collective-permute-start(bf16[1024,128]{1,0:T(8,128)(2,1)S(1)} %get-tuple-element.33), channel_id=1, source_target_pairs={{0,0},{1,1},{2,4},{3,5},{4,2},{5,3},{6,6},{7,7},{8,8},{9,9},{10,12... | collective-permute-start | bytes 786440 | tf_op jit(solution)/shard_map/ppermute | solution.py:187
  79.3 12.0 %collective-permute-start.10 = (bf16[1024,128]{1,0:T(8,128)(2,1)S(1)}, bf16[1024,128]{1,0:T(8,128)(2,1)S(1)}, u32[]{:S(2)}, u32[]{:S(2)}) collective-permute-start(bf16[1024,128]{1,0:T(8,128)(2,1)S(1)} %get-tuple-element.34), channel_id=1, source_target_pairs={{0,1},{1,0},{2,5},{3,4},{4,3},{5,2},{6,7},{7,6},{8,9},{9,8},{10,13... | collective-permute-start | bytes 786440 | tf_op jit(solution)/shard_map/ppermute | solution.py:187
  82.4 9.1 %collective-permute-start.11 = (bf16[1024,128]{1,0:T(8,128)(2,1)S(1)}, bf16[1024,128]{1,0:T(8,128)(2,1)S(1)}, u32[]{:S(2)}, u32[]{:S(2)}) collective-permute-start(bf16[1024,128]{1,0:T(8,128)(2,1)S(1)} %get-tuple-element.35), channel_id=1, source_target_pairs={{0,4},{1,5},{2,0},{3,1},{4,6},{5,7},{6,2},{7,3},{8,12},{9,13},{10,... | collective-permute-start | bytes 786440 | tf_op jit(solution)/shard_map/ppermute | solution.py:187
  84.9 10.7 %collective-permute-start.12 = (bf16[1024,128]{1,0:T(8,128)(2,1)S(1)}, bf16[1024,128]{1,0:T(8,128)(2,1)S(1)}, u32[]{:S(2)}, u32[]{:S(2)}) collective-permute-start(bf16[1024,128]{1,0:T(8,128)(2,1)S(1)} %get-tuple-element.36), channel_id=1, source_target_pairs={{0,5},{1,4},{2,1},{3,0},{4,7},{5,6},{6,3},{7,2},{8,13},{9,12},{10,... | collective-permute-start | bytes 786440 | tf_op jit(solution)/shard_map/ppermute | solution.py:187
  87.7 10.4 %collective-permute-start.1 = (bf16[128,1024]{1,0:T(8,128)(2,1)S(1)}, bf16[128,1024]{1,0:T(8,128)(2,1)S(1)}, u32[]{:S(2)}, u32[]{:S(2)}) collective-permute-start(bf16[128,1024]{1,0:T(8,128)(2,1)S(1)} %get-tuple-element.26.after_ref), channel_id=1, source_target_pairs={{0,0},{1,1},{2,4},{3,5},{4,2},{5,3},{6,6},{7,7},{8,8},{9,9},{10,12... | collective-permute-start | bytes 786440 | tf_op jit(solution)/shard_map/ppermute | solution.py:186
  91.4 6.7 %collective-permute-start.6 = (bf16[128,1024]{1,0:T(8,128)(2,1)S(1)}, bf16[128,1024]{1,0:T(8,128)(2,1)S(1)}, u32[]{:S(2)}, u32[]{:S(2)}) collective-permute-start(bf16[128,1024]{1,0:T(8,128)(2,1)S(1)} %collective-permute-done.2.refs_1_), channel_id=1, source_target_pairs={{0,4},{4,0},{8,12},{12,8},{16,20},{20,16},{24,28},{28,24},{32,36},... | collective-permute-start | bytes 786440 | tf_op jit(solution)/shard_map/ppermute | solution.py:204
  91.5 6.6 %collective-permute-start.7 = (bf16[128,1024]{1,0:T(8,128)(2,1)S(1)}, bf16[128,1024]{1,0:T(8,128)(2,1)S(1)}, u32[]{:S(2)}, u32[]{:S(2)}) collective-permute-start(bf16[128,1024]{1,0:T(8,128)(2,1)S(1)} %collective-permute-done.3.refs_2_), channel_id=1, source_target_pairs={{0,4},{4,0},{8,12},{12,8},{16,20},{20,16},{24,28},{28,24},{32,36},... | collective-permute-start | bytes 786440 | tf_op jit(solution)/shard_map/ppermute | solution.py:204
  95.6 3.6 %collective-permute-start.8 = (bf16[128,1024]{1,0:T(8,128)(2,1)S(1)}, bf16[128,1024]{1,0:T(8,128)(2,1)S(1)}, u32[]{:S(2)}, u32[]{:S(2)}) collective-permute-start(bf16[128,1024]{1,0:T(8,128)(2,1)S(1)} %collective-permute-done.4.refs_3_), channel_id=1, source_target_pairs={{0,4},{4,0},{8,12},{12,8},{16,20},{20,16},{24,28},{28,24},{32,36},... | collective-permute-start | bytes 786440 | tf_op jit(solution)/shard_map/ppermute | solution.py:204
  98.0 1.5 collective-permute-start.5
  103.6 3.5 %collective-permute-start.17 = (f32[8,128]{1,0:T(8,128)S(1)}, f32[8,128]{1,0:T(8,128)S(1)}, u32[]{:S(2)}, u32[]{:S(2)}) collective-permute-start(f32[8,128]{1,0:T(8,128)S(1)} %get-tuple-element.46.norm_ref), channel_id=1, source_target_pairs={{0,4},{4,0},{8,12},{12,8},{16,20},{20,16},{24,28},{28,24},{32,36},... | collective-permute-start | bytes 12296 | tf_op jit(solution)/shard_map/ppermute | solution.py:218
  107.0 45.7 %copy-start = (f32[2,256,1024]{2,1,0:T(8,128)S(1)}, f32[2,256,1024]{2,1,0:T(8,128)}, u32[]{:S(2)}) copy-start(f32[2,256,1024]{2,1,0:T(8,128)} %left_ref.3) | copy-start | bytes 6291460
  108.8 48.7 %all-to-all-start.2 = ((bf16[256,16,128]{2,1,0:T(8,128)(2,1)}), bf16[256,16,128]{2,1,0:T(8,128)(2,1)S(1)}, u32[]{:S(2)}, u32[]{:S(2)}) async-start(bf16[256,16,128]{2,1,0:T(8,128)(2,1)} %bitcast.5), calls=%async_computation.2 | async-start | bytes 2097152 | tf_op jit(solution)/shard_map/all_to_all | solution.py:226
  114.9 23.9 %collective-permute-start.14 = (bf16[256,1024]{1,0:T(8,128)(2,1)}, bf16[256,1024]{1,0:T(8,128)(2,1)S(1)}, u32[]{:S(2)}, u32[]{:S(2)}) collective-permute-start(bf16[256,1024]{1,0:T(8,128)(2,1)} %copy-done.12), channel_id=1, source_target_pairs={{1,0},{0,1},{5,2},{4,3},{3,4},{2,5},{7,6},{6,7},{9,8},{8,9},{13,10... | collective-permute-start | bytes 1572872 | tf_op jit(solution)/shard_map/ppermute | solution.py:225
  117.9 32.8 %collective-permute-start.15 = (bf16[256,1024]{1,0:T(8,128)(2,1)}, bf16[256,1024]{1,0:T(8,128)(2,1)S(1)}, u32[]{:S(2)}, u32[]{:S(2)}) collective-permute-start(bf16[256,1024]{1,0:T(8,128)(2,1)} %copy-done.11), channel_id=1, source_target_pairs={{4,0},{5,1},{0,2},{1,3},{6,4},{7,5},{2,6},{3,7},{12,8},{13,9},{8,1... | collective-permute-start | bytes 1572872 | tf_op jit(solution)/shard_map/ppermute | solution.py:225
  117.9 32.8 %collective-permute-start.16 = (bf16[256,1024]{1,0:T(8,128)(2,1)}, bf16[256,1024]{1,0:T(8,128)(2,1)S(1)}, u32[]{:S(2)}, u32[]{:S(2)}) collective-permute-start(bf16[256,1024]{1,0:T(8,128)(2,1)} %copy-done.10), channel_id=1, source_target_pairs={{5,0},{4,1},{1,2},{0,3},{7,4},{6,5},{3,6},{2,7},{13,8},{12,9},{9,1... | collective-permute-start | bytes 1572872 | tf_op jit(solution)/shard_map/ppermute | solution.py:225
  118.9 33.9 %collective-permute-start.13 = (bf16[256,1024]{1,0:T(8,128)(2,1)}, bf16[256,1024]{1,0:T(8,128)(2,1)S(1)}, u32[]{:S(2)}, u32[]{:S(2)}) collective-permute-start(bf16[256,1024]{1,0:T(8,128)(2,1)} %copy-done.7), channel_id=1, source_target_pairs={{0,0},{1,1},{4,2},{5,3},{2,4},{3,5},{6,6},{7,7},{8,8},{9,9},{12,10... | collective-permute-start | bytes 1572872 | tf_op jit(solution)/shard_map/ppermute | solution.py:225
  (11 other events, 31.6 us)

commit v2 on v1

--- a/solution.py
+++ b/solution.py
@@ -49,7 +49,7 @@
 
 def moment_kernel(slot_ref, grad_ref, second_ref, new_ref, sent_ref, part):
     row_blocks, _, column_blocks, _ = grad_ref.shape
-    sent_ref[...] = jnp.zeros_like(sent_ref)
+    part[...] = jnp.zeros_like(part)
     for r in range(row_blocks):
         g = grad_ref[r].astype(F32)
         new = 0.9 * second_ref[r] + 0.1 * g * g
@@ -57,25 +57,30 @@
         adam = g / (jnp.sqrt(new) + 1e-08)
         sums = jnp.sum(jnp.sum(adam * adam, axis=0), axis=1, keepdims=True)
         part[r * column_blocks : (r + 1) * column_blocks, :] = jnp.broadcast_to(sums, (column_blocks, 128))
-    for b in range(row_blocks * column_blocks):
-        at = spread_row(slot_ref[b])
-        sent_ref[at] = part[b : b + 1, :]
-        sent_ref[at + 4] = part[b : b + 1, :]
+    sent_ref[...] = part[...].T[0:8, :]
 
 
 def pack_kernel(spot_ref, left_ref, right_ref, *outs):
     half = left_ref.shape[1] // 2
-    chips = len(outs) // 2
-    for m in range(chips):
+    order = left_ref.shape[2]
+    for m, out in enumerate(outs):
         to = spot_ref[0] ^ m
         part = pl.ds(pl.multiple_of((to >> 1) * half, half), half)
-        outs[m][...] = left_ref[to & 1, part, :]
-        outs[chips + m][...] = right_ref[to & 1, :, part]
-
-
-def update_kernel(spot_ref, adam_ref, own_ref, other_ref, *refs):
-    lefts, lefts2, rights = refs[0:4], refs[4:8], refs[8:12]
-    grad, update_ref, norm_ref, note_ref, root, mixed, rows = refs[12:]
+        out[:half, :] = left_ref[to & 1, part, :]
+        for t in range(0, order, half):
+            out[half:, t : t + half] = right_ref[to & 1, t : t + half, part]
+
+
+def unpack_kernel(spot_ref, *refs):
+    got, out = refs[:-1], refs[-1]
+    half = out.shape[0] // len(got)
+    for m, ref in enumerate(got):
+        out[m * half : (m + 1) * half, :] = ref[:half, :]
+
+
+def update_kernel(spot_ref, own_ref, other_ref, left_ref, left2_ref, *refs):
+    rights = refs[0:4]
+    grad, update_ref, norm_ref, root, mixed = refs[4:]
     core, lane = spot_ref[1], spot_ref[2]
     owners, chips, piece, half = own_ref.shape
     order = grad.shape[0]
@@ -84,14 +89,14 @@
         theirs = pl.multiple_of((2 * d + 1 - core) * half, half)
         grad[:, pl.ds(mine, half)] = own_ref[:, d].reshape(order, half)
         grad[:, pl.ds(theirs, half)] = other_ref[:, d].reshape(order, half)
-        root[:, pl.ds(pl.multiple_of((lane ^ d) * half, half), half)] = rights[d][...]
+        to = pl.ds(pl.multiple_of((lane ^ d) * half, half), half)
+        for t in range(0, order, half):
+            root[t : t + half, to] = rights[d][half:, t : t + half]
     for t in range(0, order, 512):
         mixed[t : t + 512, :] = jnp.dot(grad[t : t + 512, :], root[...], preferred_element_type=F32).astype(BF16)
     total = jnp.zeros((8, 128), F32)
     count = half // piece
-    for parts, which, first in ((lefts, core, lane), (lefts2, 1 - core, lane ^ 2)):
-        for m in range(chips):
-            rows[m * half : (m + 1) * half, :] = parts[m][...]
+    for rows, which, first in ((left_ref, core, lane), (left2_ref, 1 - core, lane ^ 2)):
         part = jnp.dot(rows[...], mixed[...], preferred_element_type=F32).astype(BF16)
         wide = part.astype(F32)
         squares = jnp.sum((wide * wide).reshape(chips * half // 8, 8, chips * half), axis=0)
@@ -103,7 +108,6 @@
                 update_ref[pl.ds(spot, count), y] = block.reshape(count, piece, half)
     norm = jnp.sum(jnp.sum(total, axis=0, keepdims=True), axis=1, keepdims=True)
     norm_ref[...] = jnp.broadcast_to(norm, norm_ref.shape)
-    note_ref[...] = jnp.broadcast_to(jnp.sum(adam_ref[...], axis=0), note_ref.shape)
 
 
 def product_kernel(spot_ref, grad, *refs):
@@ -123,8 +127,8 @@
             out[half:, n : n + 256] = right[m * half : (m + 1) * half].astype(BF16)
 
 
-def graft_kernel(spot_ref, update_ref, norm_ref, norm2_ref, note_ref, after_ref, out_ref):
-    scale = jnp.sqrt(note_ref[0:1, :] / (norm_ref[0:1, :] + norm2_ref[0:1, :] + 1e-06))
+def graft_kernel(spot_ref, update_ref, norm_ref, norm2_ref, after_ref, out_ref):
+    scale = 1.0 / jnp.sqrt(norm_ref[0:1, :] + norm2_ref[0:1, :] + 1e-06)
     out_ref[...] = (update_ref[...].astype(F32) * scale[None, None]).astype(BF16)
 
 
@@ -138,15 +142,19 @@
             new_right_ref[0] = right_ref[0] + ref[half:, :].astype(F32)
 
 
-def direction_kernel(slot_ref, values_ref, out_ref, wide):
+def direction_kernel(slot_ref, values_ref, adam_ref, out_ref, wide, scales):
     row_blocks, rows, column_blocks, quarter = out_ref.shape
     half = quarter // 2
     size = wide.shape[0] // 2
+    copies = jnp.sum(adam_ref[...].reshape(-1, 8, 128), axis=0)
+    total = jnp.sqrt(copies[0:1, :])
+    scales[...] = jnp.broadcast_to(total, scales.shape).T
     for b in range(row_blocks * column_blocks):
         at = spread_row(slot_ref[b])
         start = (b // column_blocks) * rows * column_blocks + b % column_blocks
-        wide[pl.ds(start, rows, stride=column_blocks), :] = values_ref[at].astype(F32)
-        wide[pl.ds(size + start, rows, stride=column_blocks), :] = values_ref[at + 4].astype(F32)
+        scale = scales[b : b + 1, :]
+        wide[pl.ds(start, rows, stride=column_blocks), :] = values_ref[at].astype(F32) * scale
+        wide[pl.ds(size + start, rows, stride=column_blocks), :] = values_ref[at + 4].astype(F32) * scale
     for h in range(2):
         part = wide[h * size : (h + 1) * size, :].reshape(row_blocks, rows, column_blocks, half)
         out_ref[..., h * half : (h + 1) * half] = part.astype(out_ref.dtype)
@@ -178,50 +186,46 @@
     swap = [(i, i ^ 1) for i in range(owners)]
 
     packed = local(
-        pack_kernel,
-        [shape((half, order), BF16)] * chips + [shape((order, half), BF16)] * chips,
-        (spot, root_left, root_right),
-        moved=4 * MIB,
-    )
-    lefts = [lax.ppermute(packed[m], AXES, matching(m, False)) for m in range(chips)]
-    rights = [lax.ppermute(packed[chips + m], AXES, matching(m, False)) for m in range(chips)]
+        pack_kernel, [shape((2 * half, order), BF16)] * chips, (spot, root_left, root_right),
+        limit=5, moved=4 * MIB,
+    )
+    roots = [lax.ppermute(packed[m], AXES, matching(m, False)) for m in range(chips)]
 
     pieces = local(
         spread_kernel, shape((devices, piece_rows, half), BF16), (block_slot, gradient, packed[0]),
-        scratch=[pltpu.VMEM((2 * blocks * piece_rows, half), F32)], moved=MIB * 3 // 2,
+        scratch=[pltpu.VMEM((2 * blocks * piece_rows, half), F32)], limit=6, moved=MIB * 3 // 2,
     )
     own = lax.all_to_all(pieces, AXES, split_axis=0, concat_axis=0, tiled=True)
 
     new_second, sent = local(
         moment_kernel,
-        [shape(second_moment.shape, F32), shape((devices, 1, 128), F32)],
+        [shape(second_moment.shape, F32), shape((8, 128), F32)],
         (block_slot, gradient, second_moment),
-        scratch=[pltpu.VMEM((blocks, 128), F32)], moved=MIB * 5 // 2,
-    )
-    adam = lax.all_to_all(sent, AXES, split_axis=0, concat_axis=0, tiled=True)
-
-    own, adam = lax.optimization_barrier((own, adam))
-    lefts2 = [lax.ppermute(part, "fsdp", swap) for part in lefts]
+        scratch=[pltpu.VMEM((128, 128), F32)], limit=6, moved=MIB * 5 // 2,
+    )
+    adam = lax.all_gather(sent, AXES, axis=0, tiled=True)
+
+    own, *roots = lax.optimization_barrier((own, *roots))
+    left = local(unpack_kernel, shape((order // 2, order), BF16), (spot, *roots), limit=4, moved=2 * MIB)
+    left2 = lax.ppermute(left, "fsdp", swap)
     other = lax.ppermute(own, "fsdp", swap)
 
     cut = (owners, chips, piece_rows, half)
-    grad, update, norm, note = local(
+    grad, update, norm = local(
         update_kernel,
-        [shape((order, order), BF16), shape(cut, BF16), shape((8, 128), F32), shape((8, 128), F32)],
-        (spot, adam, own.reshape(cut), other.reshape(cut), *lefts, *lefts2, *rights),
-        scratch=[
-            pltpu.VMEM((order, order // 2), BF16), pltpu.VMEM((order, order // 2), BF16),
-            pltpu.VMEM((order // 2, order), BF16),
-        ],
-        limit=32, flops=2 * order * order * order, moved=8 * MIB,
+        [shape((order, order), BF16), shape(cut, BF16), shape((8, 128), F32)],
+        (spot, own.reshape(cut), other.reshape(cut), left, left2, *roots),
+        scratch=[pltpu.VMEM((order, order // 2), BF16)] * 2,
+        flops=2 * order * order * order, limit=18, moved=8 * MIB,
     )
     norm2 = lax.ppermute(norm, "fsdp", swap)
     products = local(
         product_kernel, [shape((2 * half, order), BF16)] * chips, (spot, grad),
         scratch=[pltpu.VMEM((order // 2, order), BF16)] * 2,
-        limit=24, flops=2 * order * order * order, moved=4 * MIB,
-    )
-    back = local(graft_kernel, shape(cut, BF16), (spot, update, norm, norm2, note, products[0]), moved=2 * MIB)
+        flops=2 * order * order * order, limit=11, moved=4 * MIB,
+    )
+    update, adam = lax.optimization_barrier((update, adam))
+    back = local(graft_kernel, shape(cut, BF16), (spot, update, norm, norm2, products[0]), limit=5, moved=2 * MIB)
     products = [lax.ppermute(products[m], AXES, matching(m, True)) for m in range(chips)]
     returned = lax.all_to_all(back.reshape(devices, piece_rows, half), AXES, split_axis=0, concat_axis=0, tiled=True)
 
@@ -233,14 +237,14 @@
         grid_spec=pltpu.PrefetchScalarGridSpec(
             num_scalar_prefetch=1, grid=(chips,), in_specs=[whole] * chips + [piece] * 2, out_specs=[piece] * 2
         ),
-        compiler_params=pltpu.CompilerParams(vmem_limit_bytes=16 * MIB),
+        compiler_params=pltpu.CompilerParams(vmem_limit_bytes=10 * MIB),
         cost_estimate=pl.CostEstimate(flops=0, bytes_accessed=10 * MIB, transcendentals=0),
     )(spot, *products, stat_left, stat_right)
 
     direction = local(
-        direction_kernel, shape(gradient.shape, gradient.dtype), (block_slot, returned),
-        scratch=[pltpu.VMEM((2 * blocks * piece_rows, half), F32)],
-        moved=2 * MIB,
+        direction_kernel, shape(gradient.shape, gradient.dtype), (block_slot, returned, adam),
+        scratch=[pltpu.VMEM((2 * blocks * piece_rows, half), F32), pltpu.VMEM((128, 128), F32)],
+        limit=7, moved=2 * MIB,
     )
     return (new_left, new_right, new_second, direction)
 

time: 160 us -> 208 us (1.30)
  waiting for transfers between devices: 45.2 us -> 112 us
  blocking collectives: 36.5 us -> 0 us
  between operations: 0.86 us -> 14.2 us
  local copies, waits for them, and re-layouts: 6.48 us -> 15.9 us
  starting transfers between devices: 52.7 us -> 46.4 us
    all_gather x0 -> x1, waiting for transfers between devices: none -> 48.5 us  [body(): adam = lax.all_gather(sent, AXES, axis=0, tiled=True)]
    all_to_all x1 -> x0, blocking collectives: 36.5 us -> none  [body(): own = lax.all_to_all(pieces, AXES, split_axis=0, concat_axis=0, tiled=True)]
    ppermute x4, waiting for transfers between devices: 3.85 us -> 28.8 us  [body(): lax.ppermute(packed[m], AXES, matching(m, False))]
    ppermute x8 -> x1, starting transfers between devices: 15 us -> 2.64 us  [body(): left2 = lax.ppermute(left, 'fsdp', swap)]
    unnamed x30 -> x46, local copies, waits for them, and re-layouts: 6.48 us -> 15.9 us
    all_to_all x1, waiting for transfers between devices: 8.89 us -> 0.01 us  [body(): own = lax.all_to_all(pieces, AXES, split_axis=0, concat_axis=0, tiled=True)]
    all_to_all x1, starting transfers between devices: 6.14 us -> 10.4 us  [body(): lax.all_to_all(back.reshape(devices, piece_rows, half), AXES, split_axis=...]
    pallas_call x7 -> x8, Pallas kernels: 14.3 us -> 16 us  [local(): pl.pallas_call(kernel, out_shape=outs, in_specs=[SMEM] + [VMEM] * (len(in...]
  transfers between devices with their start and end apart: 20 -> 14, of which waited for: 9 -> 10; matrix products, arithmetic and copies ran while one was open for 0% -> 0% of each run, Pallas kernels for 5% -> 6%
where the time goes in v2:
time: 208 us; the launch traced here: 207 us
  waiting for transfers between devices  112 us (54%)
  starting transfers between devices  46.4 us (22%)
  Pallas kernels  19.1 us (9%)
  local copies, waits for them, and re-layouts  15.9 us (8%)
  between operations  14.2 us (7%)
    all_gather x1, waiting for transfers between devices, body(): adam = lax.all_gather(sent, AXES, axis=0, tiled=True)  48.5 us
    ppermute x4, waiting for transfers between devices, body(): lax.ppermute(products[m], AXES, matching(m, True))  30.6 us
    ppermute x4, waiting for transfers between devices, body(): lax.ppermute(packed[m], AXES, matching(m, False))  28.8 us
    pallas_call x8, Pallas kernels, local(): pl.pallas_call(kernel, out_shape=outs, in_specs=[SMEM] + [VMEM] * (len(in...  16 us
    unnamed x46, local copies, waits for them, and re-layouts  15.9 us
    all_to_all x1, starting transfers between devices, body(): own = lax.all_to_all(pieces, AXES, split_axis=0, concat_axis=0, tiled=True)  15.7 us
    all_to_all x1, starting transfers between devices, body(): lax.all_to_all(back.reshape(devices, piece_rows, half), AXES, split_axis=...  10.4 us
    ppermute x4, starting transfers between devices, body(): lax.ppermute(products[m], AXES, matching(m, True))  8.95 us
  transfers between devices with their start and end apart: 14, of which 10 were waited for; matrix products, arithmetic and copies ran while one was open for 0% of the time, Pallas kernels for 6%

profile of v2, /device:TPU:1, one launch (start us, length us, event | category | flops | bytes accessed | tf_op | source)
XLA Modules:
  0.0 207.1 jit_solution(3278938663653048474)
XLA Ops:
  13.1 1.9 shard_map.103
  15.0 15.7 %all-to-all-start = ((bf16[256,16,128]{2,1,0:T(8,128)(2,1)}), bf16[256,16,128]{2,1,0:T(8,128)(2,1)S(1)}, u32[]{:S(2)}, u32[]{:S(2)}) async-start(bf16[256,16,128]{2,1,0:T(8,128)(2,1)} %shard_map.103), calls=%async_computation | async-start | bytes 2097152 | tf_op jit(solution)/shard_map/all_to_all | solution.py:198
  30.7 2.1 %shard_map.108 = (f32[8,16,8,256]{3,2,1,0:T(8,128)}, f32[8,128]{1,0:T(8,128)}) custom-call(s32[64]{0:T(128)S(1)} %copy-done.16, bf16[8,16,8,256]{3,2,1,0:T(8,128)(2,1)S(1)} %copy-done.2, f32[8,16,8,256]{3,2,1,0:T(8,128)S(1)} %copy-done.5), custom_call_target="tpu_custom_call" | custom-call | bytes 2621440 | tf_op jit(solution)/shard_map/pallas_call | solution.py:17
  32.8 5.1 %collective-permute-start = (bf16[256,1024]{1,0:T(8,128)(2,1)S(1)}, bf16[256,1024]{1,0:T(8,128)(2,1)S(1)}, u32[]{:S(2)}, u32[]{:S(2)}) collective-permute-start(bf16[256,1024]{1,0:T(8,128)(2,1)S(1)} %get-tuple-element.26.after_ref), channel_id=1, source_target_pairs={{0,0},{1,1},{2,4},{3,5},{4,2},{5,3},{6,6},{7,7},{8,8},{9,9},{10,12... | collective-permute-start | bytes 1572872 | tf_op jit(solution)/shard_map/ppermute | solution.py:192
  38.9 2.2 %collective-permute-start.3 = (bf16[256,1024]{1,0:T(8,128)(2,1)}, bf16[256,1024]{1,0:T(8,128)(2,1)S(1)}, u32[]{:S(2)}, u32[]{:S(2)}) collective-permute-start(bf16[256,1024]{1,0:T(8,128)(2,1)} %copy-done.17), channel_id=1, source_target_pairs={{0,5},{1,4},{2,1},{3,0},{4,7},{5,6},{6,3},{7,2},{8,13},{9,12},{10,... | collective-permute-start | bytes 1572872 | tf_op jit(solution)/shard_map/ppermute | solution.py:192
  41.0 18.4 %collective-permute-done.refs_0_ = bf16[256,1024]{1,0:T(8,128)(2,1)S(1)} collective-permute-done((bf16[256,1024]{1,0:T(8,128)(2,1)S(1)}, bf16[256,1024]{1,0:T(8,128)(2,1)S(1)}, u32[]{:S(2)}, u32[]{:S(2)}) %collective-permute-start) | collective-permute-done | bytes 524320 | tf_op jit(solution)/shard_map/ppermute | solution.py:192
  59.4 2.3 %collective-permute-done.1.refs_1_ = bf16[256,1024]{1,0:T(8,128)(2,1)S(1)} collective-permute-done((bf16[256,1024]{1,0:T(8,128)(2,1)}, bf16[256,1024]{1,0:T(8,128)(2,1)S(1)}, u32[]{:S(2)}, u32[]{:S(2)}) %collective-permute-start.1) | collective-permute-done | bytes 524320 | tf_op jit(solution)/shard_map/ppermute | solution.py:192
  61.6 6.5 %collective-permute-done.2.refs_2_ = bf16[256,1024]{1,0:T(8,128)(2,1)S(1)} collective-permute-done((bf16[256,1024]{1,0:T(8,128)(2,1)}, bf16[256,1024]{1,0:T(8,128)(2,1)S(1)}, u32[]{:S(2)}, u32[]{:S(2)}) %collective-permute-start.2) | collective-permute-done | bytes 524320 | tf_op jit(solution)/shard_map/ppermute | solution.py:192
  68.1 1.7 collective-permute-done.3.refs_3_
  72.2 2.6 %collective-permute-start.5 = (bf16[512,1024]{1,0:T(8,128)(2,1)S(1)}, bf16[512,1024]{1,0:T(8,128)(2,1)S(1)}, u32[]{:S(2)}, u32[]{:S(2)}) collective-permute-start(bf16[512,1024]{1,0:T(8,128)(2,1)S(1)} %shard_map.104.left_ref), channel_id=1, source_target_pairs={{0,4},{4,0},{8,12},{12,8},{16,20},{20,16},{24,28},{28,24},{32,36},... | collective-permute-start | bytes 3145736 | tf_op jit(solution)/shard_map/ppermute | solution.py:210
  75.0 2.2 %collective-permute-done.5.left2_ref = bf16[512,1024]{1,0:T(8,128)(2,1)S(1)} collective-permute-done((bf16[512,1024]{1,0:T(8,128)(2,1)S(1)}, bf16[512,1024]{1,0:T(8,128)(2,1)S(1)}, u32[]{:S(2)}, u32[]{:S(2)}) %collective-permute-start.5) | collective-permute-done | bytes 1048608 | tf_op jit(solution)/shard_map/ppermute | solution.py:210
  77.2 1.5 collective-permute-done.4
  80.8 3.9 %shard_map.105 = (bf16[1024,1024]{1,0:T(8,128)(2,1)S(1)}, bf16[64,4,16,128]{3,2,1,0:T(8,128)(2,1)S(1)}, f32[8,128]{1,0:T(8,128)S(1)}) custom-call(s32[3]{0:T(128)S(1)} %pad_add_fusion.spot_ref, bf16[64,4,16,128]{3,2,1,0:T(8,128)(2,1)S(1)} %bitcast.6, bf16[64,4,16,128]{3,2,1,0:T(8,128)(2,1)S(1)} %bitcast.7, bf16[512,1024]{1,0:T(8,128)(2,1)S(1)} %shard_map.104.left_ref, ...), custom_call_target="tpu_custom_call" | custom-call | flops 2147483648 | bytes 8388608 | tf_op jit(solution)/shard_map/pallas_call | solution.py:17
  85.1 3.0 %shard_map.106 = (bf16[256,1024]{1,0:T(8,128)(2,1)S(1)}, bf16[256,1024]{1,0:T(8,128)(2,1)S(1)}, bf16[256,1024]{1,0:T(8,128)(2,1)S(1)}, bf16[256,1024]{1,0:T(8,128)(2,1)S(1)}) custom-call(s32[3]{0:T(128)S(1)} %pad_add_fusion.spot_ref, bf16[1024,1024]{1,0:T(8,128)(2,1)S(1)} %get-tuple-element.35.grad), custom_call_target="tpu_custom_call" | custom-call | flops 2147483648 | bytes 4194304 | tf_op jit(solution)/shard_map/pallas_call | solution.py:17
  91.2 48.5 %all-gather.2.cloned.1.call-done.adam_ref = f32[2048,128]{1,0:T(8,128)} async-done(((f32[8,128]{1,0:T(8,128)}), f32[2048,128]{1,0:T(8,128)}) %all-gather.2.cloned.1.call-update) | async-done | bytes 1048592 | tf_op jit(solution)/shard_map/all_gather | solution.py:206
  140.8 1.7 shard_map.109
  142.5 10.4 %all-to-all-start.1 = ((bf16[256,16,128]{2,1,0:T(8,128)(2,1)}), bf16[256,16,128]{2,1,0:T(8,128)(2,1)S(1)}, u32[]{:S(2)}, u32[]{:S(2)}) async-start(bf16[256,16,128]{2,1,0:T(8,128)(2,1)} %bitcast.5), calls=%async_computation.1 | async-start | bytes 2097152 | tf_op jit(solution)/shard_map/all_to_all | solution.py:230
  152.9 5.1 %collective-permute-start.6 = (bf16[256,1024]{1,0:T(8,128)(2,1)}, bf16[256,1024]{1,0:T(8,128)(2,1)S(1)}, u32[]{:S(2)}, u32[]{:S(2)}) collective-permute-start(bf16[256,1024]{1,0:T(8,128)(2,1)} %copy-done.14), channel_id=1, source_target_pairs={{0,0},{1,1},{4,2},{5,3},{2,4},{3,5},{6,6},{7,7},{8,8},{9,9},{12,10... | collective-permute-start | bytes 1572872 | tf_op jit(solution)/shard_map/ppermute | solution.py:229
  158.9 2.9 %collective-permute-start.9 = (bf16[256,1024]{1,0:T(8,128)(2,1)}, bf16[256,1024]{1,0:T(8,128)(2,1)S(1)}, u32[]{:S(2)}, u32[]{:S(2)}) collective-permute-start(bf16[256,1024]{1,0:T(8,128)(2,1)} %copy-done.18), channel_id=1, source_target_pairs={{5,0},{4,1},{1,2},{0,3},{7,4},{6,5},{3,6},{2,7},{13,8},{12,9},{9,1... | collective-permute-start | bytes 1572872 | tf_op jit(solution)/shard_map/ppermute | solution.py:229
  161.8 17.0 %collective-permute-done.6.p0 = bf16[256,1024]{1,0:T(8,128)(2,1)S(1)} collective-permute-done((bf16[256,1024]{1,0:T(8,128)(2,1)}, bf16[256,1024]{1,0:T(8,128)(2,1)S(1)}, u32[]{:S(2)}, u32[]{:S(2)}) %collective-permute-start.6) | collective-permute-done | bytes 524320 | tf_op jit(solution)/shard_map/ppermute | solution.py:229
  178.9 13.5 %collective-permute-done.7.p1 = bf16[256,1024]{1,0:T(8,128)(2,1)S(1)} collective-permute-done((bf16[256,1024]{1,0:T(8,128)(2,1)}, bf16[256,1024]{1,0:T(8,128)(2,1)S(1)}, u32[]{:S(2)}, u32[]{:S(2)}) %collective-permute-start.7) | collective-permute-done | bytes 524320 | tf_op jit(solution)/shard_map/ppermute | solution.py:229
  192.4 1.6 copy-done.1
  194.0 3.1 %shard_map.107 = (f32[2,256,1024]{2,1,0:T(8,128)}, f32[2,256,1024]{2,1,0:T(8,128)}) custom-call(s32[3]{0:T(128)S(1)} %pad_add_fusion.spot_ref, bf16[256,1024]{1,0:T(8,128)(2,1)S(1)} %collective-permute-done.6.p0, bf16[256,1024]{1,0:T(8,128)(2,1)S(1)} %collective-permute-done.7.p1, bf16[256,1024]{1,0:T(8,128)(2,1)S(1)} %collective-permute-done.8.p2, ...), custom_call_target="tpu_custom_call" | custom-call | bytes 10485760 | tf_op jit(solution)/shard_map/pallas_call | solution.py:234
  198.3 1.9 shard_map.110
  (61 shorter events, 18.5 us)
Async XLA Ops:
  7.2 5.9 %copy-start.2 = (bf16[8,16,8,256]{3,2,1,0:T(8,128)(2,1)S(1)}, bf16[8,16,8,256]{3,2,1,0:T(8,128)(2,1)}, u32[]{:S(2)}) copy-start(bf16[8,16,8,256]{3,2,1,0:T(8,128)(2,1)} %grad_ref.3) | copy-start | bytes 1572868
  7.3 1.3 copy-start.3
  9.8 3.3 %copy-start.16 = (s32[64]{0:T(128)S(1)}, s32[64]{0:T(128)}, u32[]{:S(2)}) copy-start(s32[64]{0:T(128)} %slot_ref.5) | copy-start | bytes 772
  13.1 17.6 %copy-start.5 = (f32[8,16,8,256]{3,2,1,0:T(8,128)S(1)}, f32[8,16,8,256]{3,2,1,0:T(8,128)}, u32[]{:S(2)}) copy-start(f32[8,16,8,256]{3,2,1,0:T(8,128)} %second_ref.1) | copy-start | bytes 3145732
  15.0 55.6 %all-to-all-start = ((bf16[256,16,128]{2,1,0:T(8,128)(2,1)}), bf16[256,16,128]{2,1,0:T(8,128)(2,1)S(1)}, u32[]{:S(2)}, u32[]{:S(2)}) async-start(bf16[256,16,128]{2,1,0:T(8,128)(2,1)} %shard_map.103), calls=%async_computation | async-start | bytes 2097152 | tf_op jit(solution)/shard_map/all_to_all | solution.py:198
  30.6 109.1 %all-gather.2.cloned.1.call-start = ((), (), s32[]{:S(2)}) async-start(), calls=%async_computation.2 | async-start | bytes 1052672 | tf_op jit(solution)/shard_map/all_gather | solution.py:206
  32.8 26.6 %collective-permute-start = (bf16[256,1024]{1,0:T(8,128)(2,1)S(1)}, bf16[256,1024]{1,0:T(8,128)(2,1)S(1)}, u32[]{:S(2)}, u32[]{:S(2)}) collective-permute-start(bf16[256,1024]{1,0:T(8,128)(2,1)S(1)} %get-tuple-element.26.after_ref), channel_id=1, source_target_pairs={{0,0},{1,1},{2,4},{3,5},{4,2},{5,3},{6,6},{7,7},{8,8},{9,9},{10,12... | collective-permute-start | bytes 1572872 | tf_op jit(solution)/shard_map/ppermute | solution.py:192
  37.8 23.8 %collective-permute-start.1 = (bf16[256,1024]{1,0:T(8,128)(2,1)}, bf16[256,1024]{1,0:T(8,128)(2,1)S(1)}, u32[]{:S(2)}, u32[]{:S(2)}) collective-permute-start(bf16[256,1024]{1,0:T(8,128)(2,1)} %copy-done.21), channel_id=1, source_target_pairs={{0,1},{1,0},{2,5},{3,4},{4,3},{5,2},{6,7},{7,6},{8,9},{9,8},{10,13... | collective-permute-start | bytes 1572872 | tf_op jit(solution)/shard_map/ppermute | solution.py:192
  38.9 29.2 %collective-permute-start.2 = (bf16[256,1024]{1,0:T(8,128)(2,1)}, bf16[256,1024]{1,0:T(8,128)(2,1)S(1)}, u32[]{:S(2)}, u32[]{:S(2)}) collective-permute-start(bf16[256,1024]{1,0:T(8,128)(2,1)} %copy-done.19), channel_id=1, source_target_pairs={{0,4},{1,5},{2,0},{3,1},{4,6},{5,7},{6,2},{7,3},{8,12},{9,13},{10,... | collective-permute-start | bytes 1572872 | tf_op jit(solution)/shard_map/ppermute | solution.py:192
  38.9 30.9 %collective-permute-start.3 = (bf16[256,1024]{1,0:T(8,128)(2,1)}, bf16[256,1024]{1,0:T(8,128)(2,1)S(1)}, u32[]{:S(2)}, u32[]{:S(2)}) collective-permute-start(bf16[256,1024]{1,0:T(8,128)(2,1)} %copy-done.17), channel_id=1, source_target_pairs={{0,5},{1,4},{2,1},{3,0},{4,7},{5,6},{6,3},{7,2},{8,13},{9,12},{10,... | collective-permute-start | bytes 1572872 | tf_op jit(solution)/shard_map/ppermute | solution.py:192
  61.6 17.1 %copy-start.7 = (bf16[256,1024]{1,0:T(8,128)(2,1)}, bf16[256,1024]{1,0:T(8,128)(2,1)S(1)}, u32[]{:S(2)}) copy-start(bf16[256,1024]{1,0:T(8,128)(2,1)S(1)} %collective-permute-done.1.refs_1_) | copy-start | bytes 1572868
  68.1 10.6 %copy-start.9 = (bf16[256,1024]{1,0:T(8,128)(2,1)}, bf16[256,1024]{1,0:T(8,128)(2,1)S(1)}, u32[]{:S(2)}) copy-start(bf16[256,1024]{1,0:T(8,128)(2,1)S(1)} %collective-permute-done.2.refs_2_) | copy-start | bytes 1572868
  71.6 7.1 %copy-start.13 = (bf16[256,1024]{1,0:T(8,128)(2,1)S(1)}, bf16[256,1024]{1,0:T(8,128)(2,1)}, u32[]{:S(2)}) copy-start(bf16[256,1024]{1,0:T(8,128)(2,1)} %copy-done.11) | copy-start | bytes 1572868
  72.2 4.9 %collective-permute-start.5 = (bf16[512,1024]{1,0:T(8,128)(2,1)S(1)}, bf16[512,1024]{1,0:T(8,128)(2,1)S(1)}, u32[]{:S(2)}, u32[]{:S(2)}) collective-permute-start(bf16[512,1024]{1,0:T(8,128)(2,1)S(1)} %shard_map.104.left_ref), channel_id=1, source_target_pairs={{0,4},{4,0},{8,12},{12,8},{16,20},{20,16},{24,28},{28,24},{32,36},... | collective-permute-start | bytes 3145736 | tf_op jit(solution)/shard_map/ppermute | solution.py:210
  74.9 3.8 %collective-permute-start.4 = (bf16[256,16,128]{2,1,0:T(8,128)(2,1)S(1)}, bf16[256,16,128]{2,1,0:T(8,128)(2,1)S(1)}, u32[]{:S(2)}, u32[]{:S(2)}) collective-permute-start(bf16[256,16,128]{2,1,0:T(8,128)(2,1)S(1)} %all-to-all-done), channel_id=1, source_target_pairs={{0,4},{4,0},{8,12},{12,8},{16,20},{20,16},{24,28},{28,24},{32,36},... | collective-permute-start | bytes 3145736 | tf_op jit(solution)/shard_map/ppermute | solution.py:211
  84.7 55.1 %collective-permute-start.10 = (f32[8,128]{1,0:T(8,128)S(1)}, f32[8,128]{1,0:T(8,128)S(1)}, u32[]{:S(2)}, u32[]{:S(2)}) collective-permute-start(f32[8,128]{1,0:T(8,128)S(1)} %get-tuple-element.46.norm_ref), channel_id=1, source_target_pairs={{0,4},{4,0},{8,12},{12,8},{16,20},{20,16},{24,28},{28,24},{32,36},... | collective-permute-start | bytes 12296 | tf_op jit(solution)/shard_map/ppermute | solution.py:221
  140.8 51.7 %copy-start = (f32[2,256,1024]{2,1,0:T(8,128)S(1)}, f32[2,256,1024]{2,1,0:T(8,128)}, u32[]{:S(2)}) copy-start(f32[2,256,1024]{2,1,0:T(8,128)} %left_ref.3) | copy-start | bytes 6291460
  142.5 54.6 %all-to-all-start.1 = ((bf16[256,16,128]{2,1,0:T(8,128)(2,1)}), bf16[256,16,128]{2,1,0:T(8,128)(2,1)S(1)}, u32[]{:S(2)}, u32[]{:S(2)}) async-start(bf16[256,16,128]{2,1,0:T(8,128)(2,1)} %bitcast.5), calls=%async_computation.1 | async-start | bytes 2097152 | tf_op jit(solution)/shard_map/all_to_all | solution.py:230
  152.9 26.0 %collective-permute-start.6 = (bf16[256,1024]{1,0:T(8,128)(2,1)}, bf16[256,1024]{1,0:T(8,128)(2,1)S(1)}, u32[]{:S(2)}, u32[]{:S(2)}) collective-permute-start(bf16[256,1024]{1,0:T(8,128)(2,1)} %copy-done.14), channel_id=1, source_target_pairs={{0,0},{1,1},{4,2},{5,3},{2,4},{3,5},{6,6},{7,7},{8,8},{9,9},{12,10... | collective-permute-start | bytes 1572872 | tf_op jit(solution)/shard_map/ppermute | solution.py:229
  157.9 34.4 %collective-permute-start.7 = (bf16[256,1024]{1,0:T(8,128)(2,1)}, bf16[256,1024]{1,0:T(8,128)(2,1)S(1)}, u32[]{:S(2)}, u32[]{:S(2)}) collective-permute-start(bf16[256,1024]{1,0:T(8,128)(2,1)} %copy-done.22), channel_id=1, source_target_pairs={{1,0},{0,1},{5,2},{4,3},{3,4},{2,5},{7,6},{6,7},{9,8},{8,9},{13,10... | collective-permute-start | bytes 1572872 | tf_op jit(solution)/shard_map/ppermute | solution.py:229
  158.9 33.4 %collective-permute-start.8 = (bf16[256,1024]{1,0:T(8,128)(2,1)}, bf16[256,1024]{1,0:T(8,128)(2,1)S(1)}, u32[]{:S(2)}, u32[]{:S(2)}) collective-permute-start(bf16[256,1024]{1,0:T(8,128)(2,1)} %copy-done.20), channel_id=1, source_target_pairs={{4,0},{5,1},{0,2},{1,3},{6,4},{7,5},{2,6},{3,7},{12,8},{13,9},{8,1... | collective-permute-start | bytes 1572872 | tf_op jit(solution)/shard_map/ppermute | solution.py:229
  158.9 33.5 %collective-permute-start.9 = (bf16[256,1024]{1,0:T(8,128)(2,1)}, bf16[256,1024]{1,0:T(8,128)(2,1)S(1)}, u32[]{:S(2)}, u32[]{:S(2)}) collective-permute-start(bf16[256,1024]{1,0:T(8,128)(2,1)} %copy-done.18), channel_id=1, source_target_pairs={{5,0},{4,1},{1,2},{0,3},{7,4},{6,5},{3,6},{2,7},{13,8},{12,9},{9,1... | collective-permute-start | bytes 1572872 | tf_op jit(solution)/shard_map/ppermute | solution.py:229
  192.4 1.6 copy-start.1
  197.1 1.2 copy-start.6
  (13 other events, 11.8 us)
Sparse Core Ops, SparseCore 0:
  35.2 104.4 all-gather.1

commit v3 on v2

--- a/solution.py
+++ b/solution.py
@@ -33,7 +33,7 @@
     return ((slot >> 2) << 3) + (slot & 3)
 
 
-def spread_kernel(slot_ref, grad_ref, after_ref, out_ref, wide):
+def spread_kernel(slot_ref, grad_ref, out_ref, wide):
     row_blocks, rows, column_blocks, quarter = grad_ref.shape
     half = quarter // 2
     out_ref[...] = jnp.zeros_like(out_ref)
@@ -78,7 +78,7 @@
         out[m * half : (m + 1) * half, :] = ref[:half, :]
 
 
-def update_kernel(spot_ref, own_ref, other_ref, left_ref, left2_ref, *refs):
+def update_kernel(spot_ref, slots_ref, own_ref, other_ref, left_ref, left2_ref, *refs):
     rights = refs[0:4]
     grad, update_ref, norm_ref, root, mixed = refs[4:]
     core, lane = spot_ref[1], spot_ref[2]
@@ -107,7 +107,7 @@
                 spot = (first ^ m) * (2 * count) + which * count
                 update_ref[pl.ds(spot, count), y] = block.reshape(count, piece, half)
     norm = jnp.sum(jnp.sum(total, axis=0, keepdims=True), axis=1, keepdims=True)
-    norm_ref[...] = jnp.broadcast_to(norm, norm_ref.shape)
+    norm_ref[...] = jnp.broadcast_to(jnp.where(slots_ref[...] == spot_ref[3], norm, 0.0), norm_ref.shape)
 
 
 def product_kernel(spot_ref, grad, *refs):
@@ -127,11 +127,6 @@
             out[half:, n : n + 256] = right[m * half : (m + 1) * half].astype(BF16)
 
 
-def graft_kernel(spot_ref, update_ref, norm_ref, norm2_ref, after_ref, out_ref):
-    scale = 1.0 / jnp.sqrt(norm_ref[0:1, :] + norm2_ref[0:1, :] + 1e-06)
-    out_ref[...] = (update_ref[...].astype(F32) * scale[None, None]).astype(BF16)
-
-
 def stat_kernel(spot_ref, p0, p1, p2, p3, left_ref, right_ref, new_left_ref, new_right_ref):
     half = left_ref.shape[1]
     for m, ref in enumerate((p0, p1, p2, p3)):
@@ -146,9 +141,10 @@
     row_blocks, rows, column_blocks, quarter = out_ref.shape
     half = quarter // 2
     size = wide.shape[0] // 2
-    copies = jnp.sum(adam_ref[...].reshape(-1, 8, 128), axis=0)
-    total = jnp.sqrt(copies[0:1, :])
+    blocks = row_blocks * column_blocks
+    total = jnp.sum(adam_ref[...].reshape(-1, 8, 128), axis=0)[0:1, :]
     scales[...] = jnp.broadcast_to(total, scales.shape).T
+    scales[:blocks, :] = jnp.sqrt(scales[:blocks, :] / (scales[blocks : 2 * blocks, :] + 1e-06))
     for b in range(row_blocks * column_blocks):
         at = spread_row(slot_ref[b])
         start = (b // column_blocks) * rows * column_blocks + b % column_blocks
@@ -170,7 +166,9 @@
     half = quarter // 2
     core = lax.axis_index("fsdp") % 2
     chip = lax.axis_index("dp")
-    spot = jnp.stack([chip, core, 2 * core + chip % 2]).astype(jnp.int32)
+    slot = 4 * (lax.axis_index("fsdp") // 2) + chip
+    spot = jnp.stack([chip, core, 2 * core + chip % 2, slot]).astype(jnp.int32)
+    slots = jnp.concatenate([jnp.full((128 - blocks,), -1, jnp.int32), block_slot])[None]
 
     def matching(m, back):
         pairs = []
@@ -192,10 +190,15 @@
     roots = [lax.ppermute(packed[m], AXES, matching(m, False)) for m in range(chips)]
 
     pieces = local(
-        spread_kernel, shape((devices, piece_rows, half), BF16), (block_slot, gradient, packed[0]),
+        spread_kernel, shape((devices, piece_rows, half), BF16), (block_slot, gradient),
         scratch=[pltpu.VMEM((2 * blocks * piece_rows, half), F32)], limit=6, moved=MIB * 3 // 2,
     )
-    own = lax.all_to_all(pieces, AXES, split_axis=0, concat_axis=0, tiled=True)
+    own = lax.cond(
+        block_slot[0] >= 0,
+        lambda x: lax.all_to_all(x, AXES, split_axis=0, concat_axis=0, tiled=True),
+        lambda x: x,
+        pieces,
+    )
 
     new_second, sent = local(
         moment_kernel,
@@ -203,8 +206,6 @@
         (block_slot, gradient, second_moment),
         scratch=[pltpu.VMEM((128, 128), F32)], limit=6, moved=MIB * 5 // 2,
     )
-    adam = lax.all_gather(sent, AXES, axis=0, tiled=True)
-
     own, *roots = lax.optimization_barrier((own, *roots))
     left = local(unpack_kernel, shape((order // 2, order), BF16), (spot, *roots), limit=4, moved=2 * MIB)
     left2 = lax.ppermute(left, "fsdp", swap)
@@ -214,20 +215,28 @@
     grad, update, norm = local(
         update_kernel,
         [shape((order, order), BF16), shape(cut, BF16), shape((8, 128), F32)],
-        (spot, own.reshape(cut), other.reshape(cut), left, left2, *roots),
+        (spot, slots, own.reshape(cut), other.reshape(cut), left, left2, *roots),
         scratch=[pltpu.VMEM((order, order // 2), BF16)] * 2,
         flops=2 * order * order * order, limit=18, moved=8 * MIB,
     )
-    norm2 = lax.ppermute(norm, "fsdp", swap)
     products = local(
         product_kernel, [shape((2 * half, order), BF16)] * chips, (spot, grad),
         scratch=[pltpu.VMEM((order // 2, order), BF16)] * 2,
         flops=2 * order * order * order, limit=11, moved=4 * MIB,
     )
-    update, adam = lax.optimization_barrier((update, adam))
-    back = local(graft_kernel, shape(cut, BF16), (spot, update, norm, norm2, products[0]), limit=5, moved=2 * MIB)
+    update, *products = lax.optimization_barrier((update, *products))
     products = [lax.ppermute(products[m], AXES, matching(m, True)) for m in range(chips)]
-    returned = lax.all_to_all(back.reshape(devices, piece_rows, half), AXES, split_axis=0, concat_axis=0, tiled=True)
+    returned = lax.all_to_all(update.reshape(devices, piece_rows, half), AXES, split_axis=0, concat_axis=0, tiled=True)
+
+    near = owners // 8
+    groups = [
+        [[near_at * 8 + i for i in range(8)] for near_at in range(near)],
+        [[i + 8 * z for z in range(near)] for i in range(8)],
+    ]
+    adam = lax.all_gather(sent + norm, "dp", axis=0, tiled=False).sum(axis=0)
+    adam = lax.all_gather(adam, "fsdp", axis_index_groups=groups[0], axis=0, tiled=False).sum(axis=0)
+    adam = lax.all_gather(adam, "fsdp", axis_index_groups=groups[1], axis=0, tiled=True)
+
 
     whole = pl.BlockSpec((2 * half, order), lambda m, s: (0, 0))
     piece = pl.BlockSpec((1, half, order), lambda m, s: ((s[0] ^ m) & 1, (s[0] ^ m) >> 1, 0))

time: 208 us -> 173 us (0.83)
  the two profiles are of different devices: /device:TPU:1 before, /device:TPU:2 now
where the time goes in v3:
time: 173 us; the launch traced here: 172 us
  blocking collectives  116 us (67%)
  starting transfers between devices  22.6 us (13%)
  Pallas kernels  18.2 us (11%)
  local copies, waits for them, and re-layouts  10.8 us (6%)
  waiting for transfers between devices  3.25 us (2%)
    all_to_all x1, blocking collectives, body(): lax.all_to_all(x, AXES, split_axis=0, concat_axis=0, tiled=True)  44.5 us
    all_gather x1, blocking collectives, body(): adam = lax.all_gather(sent + norm, 'dp', axis=0, tiled=False).sum(axis=0)  33.6 us
    all_gather x1, blocking collectives, body(): lax.all_gather(adam, 'fsdp', axis_index_groups=groups[1], axis=0, tiled=T...  25.3 us
    pallas_call x7, Pallas kernels, local(): pl.pallas_call(kernel, out_shape=outs, in_specs=[SMEM] + [VMEM] * (len(in...  15.2 us
    all_gather x1, blocking collectives, body(): lax.all_gather(adam, 'fsdp', axis_index_groups=groups[0], axis=0, tiled=F...  13 us
    unnamed x28, local copies, waits for them, and re-layouts  9.53 us
    ppermute x4, starting transfers between devices, body(): lax.ppermute(products[m], AXES, matching(m, True))  7.94 us
    all_to_all x1, starting transfers between devices, body(): lax.all_to_all(update.reshape(devices, piece_rows, half), AXES, split_axi...  7.09 us
  transfers between devices with their start and end apart: 11, of which 2 were waited for; matrix products, arithmetic and copies ran while one was open for 0% of the time, Pallas kernels for 4%

profile of v3, /device:TPU:2, one launch (start us, length us, event | category | flops | bytes accessed | tf_op | source)
XLA Modules:
  0.0 172.2 jit_solution(11312502072391078478)
XLA Ops:
  0.7 1.3 copy-done.4
  3.2 1.9 %shard_map.103 = (bf16[256,1024]{1,0:T(8,128)(2,1)}, bf16[256,1024]{1,0:T(8,128)(2,1)}, bf16[256,1024]{1,0:T(8,128)(2,1)}, bf16[256,1024]{1,0:T(8,128)(2,1)S(1)}) custom-call(s32[4]{0:T(128)S(1)} %pad_add_fusion.spot_ref, bf16[2,256,1024]{2,1,0:T(8,128)(2,1)S(1)} %copy-done.4, bf16[2,1024,256]{2,1,0:T(8,128)(2,1)S(1)} %copy-done.5), custom_call_target="tpu_custom_call" | custom-call | bytes 4194304 | tf_op jit(solution)/shard_map/pallas_call | solution.py:17
  5.2 1.7 collective-permute-start
  6.9 1.6 collective-permute-start.1
  8.4 2.5 %collective-permute-start.2 = (bf16[256,1024]{1,0:T(8,128)(2,1)}, bf16[256,1024]{1,0:T(8,128)(2,1)S(1)}, u32[]{:S(2)}, u32[]{:S(2)}) collective-permute-start(bf16[256,1024]{1,0:T(8,128)(2,1)} %get-tuple-element.36), channel_id=1, source_target_pairs={{0,4},{1,5},{2,0},{3,1},{4,6},{5,7},{6,2},{7,3},{8,12},{9,13},{10,... | collective-permute-start | bytes 1572872 | tf_op jit(solution)/shard_map/ppermute | solution.py:190
  11.0 1.9 %shard_map.102 = bf16[256,16,128]{2,1,0:T(8,128)(2,1)} custom-call(s32[64]{0:T(128)S(1)} %copy-done.8, bf16[8,16,8,256]{3,2,1,0:T(8,128)(2,1)S(1)} %copy-done.2), custom_call_target="tpu_custom_call" | custom-call | bytes 1572864 | tf_op jit(solution)/shard_map/pallas_call | solution.py:17
  13.0 45.7 %conditional.1 = (bf16[256,16,128]{2,1,0:T(8,128)(2,1)}) conditional(s32[]{:T(128)} %bitcast.5, bf16[256,16,128]{2,1,0:T(8,128)(2,1)} %shard_map.102, bf16[256,16,128]{2,1,0:T(8,128)(2,1)} %shard_map.102), branch_computations={%region_0.1_spmd, %region_1.2_spmd} | conditional | bytes 6291492 | solution.py:196
  14.2 44.5 %all_to_all.9 = bf16[256,16,128]{2,1,0:T(8,128)(2,1)} all-to-all(bf16[256,16,128]{2,1,0:T(8,128)(2,1)S(1)} %copy-done.14), channel_id=1, replica_groups=mesh['fsdp'=64,'dp'=4] {'fsdp','dp'}, dimensions={0} | all-to-all | bytes 2097152 | tf_op jit(solution)/shard_map/cond/branch_1_fun/all_to_all | solution.py:198
  59.3 1.3 collective-permute-start.5
  61.2 1.7 %collective-permute-done.5.left2_ref = bf16[512,1024]{1,0:T(8,128)(2,1)S(1)} collective-permute-done((bf16[512,1024]{1,0:T(8,128)(2,1)S(1)}, bf16[512,1024]{1,0:T(8,128)(2,1)S(1)}, u32[]{:S(2)}, u32[]{:S(2)}) %collective-permute-start.5) | collective-permute-done | bytes 1048608 | tf_op jit(solution)/shard_map/ppermute | solution.py:211
  62.9 1.5 collective-permute-done.4
  64.4 3.9 %shard_map.105 = (bf16[1024,1024]{1,0:T(8,128)(2,1)S(1)}, bf16[64,4,16,128]{3,2,1,0:T(8,128)(2,1)S(1)}, f32[8,128]{1,0:T(8,128)S(1)}) custom-call(s32[4]{0:T(128)S(1)} %pad_add_fusion.spot_ref, s32[1,128]{1,0:T(1,128)S(1)} %pad_bitcast_fusion.slots_ref, bf16[64,4,16,128]{3,2,1,0:T(8,128)(2,1)S(1)} %bitcast.18, bf16[64,4,16,128]{3,2,1,0:T(8,128)(2,1)S(1)} %bitcast.17, ...), custom_call_target="tpu_custom_call" | custom-call | flops 2147483648 | bytes 8388608 | tf_op jit(solution)/shard_map/pallas_call | solution.py:17
  68.3 3.0 %shard_map.106 = (bf16[256,1024]{1,0:T(8,128)(2,1)S(1)}, bf16[256,1024]{1,0:T(8,128)(2,1)S(1)}, bf16[256,1024]{1,0:T(8,128)(2,1)S(1)}, bf16[256,1024]{1,0:T(8,128)(2,1)S(1)}) custom-call(s32[4]{0:T(128)S(1)} %pad_add_fusion.spot_ref, bf16[1024,1024]{1,0:T(8,128)(2,1)S(1)} %get-tuple-element.44.grad), custom_call_target="tpu_custom_call" | custom-call | flops 2147483648 | bytes 4194304 | tf_op jit(solution)/shard_map/pallas_call | solution.py:17
  74.5 7.1 %all-to-all-start.1 = ((bf16[256,16,128]{2,1,0:T(8,128)(2,1)}), bf16[256,16,128]{2,1,0:T(8,128)(2,1)S(1)}, u32[]{:S(2)}, u32[]{:S(2)}) async-start(bf16[256,16,128]{2,1,0:T(8,128)(2,1)} %bitcast.15), calls=%async_computation.1 | async-start | bytes 2097152 | tf_op jit(solution)/shard_map/all_to_all | solution.py:229
  81.6 1.7 collective-permute-start.6
  83.3 1.5 collective-permute-start.7
  84.8 4.2 %collective-permute-start.8 = (bf16[256,1024]{1,0:T(8,128)(2,1)}, bf16[256,1024]{1,0:T(8,128)(2,1)S(1)}, u32[]{:S(2)}, u32[]{:S(2)}) collective-permute-start(bf16[256,1024]{1,0:T(8,128)(2,1)} %copy-done.10), channel_id=1, source_target_pairs={{4,0},{5,1},{0,2},{1,3},{6,4},{7,5},{2,6},{3,7},{12,8},{13,9},{8,1... | collective-permute-start | bytes 1572872 | tf_op jit(solution)/shard_map/ppermute | solution.py:228
  91.8 2.1 %shard_map.108 = (f32[8,16,8,256]{3,2,1,0:T(8,128)}, f32[8,128]{1,0:T(8,128)S(1)}) custom-call(s32[64]{0:T(128)S(1)} %copy-done.8, bf16[8,16,8,256]{3,2,1,0:T(8,128)(2,1)S(1)} %copy-done.3, f32[8,16,8,256]{3,2,1,0:T(8,128)S(1)} %copy-done.6), custom_call_target="tpu_custom_call" | custom-call | bytes 2621440 | tf_op jit(solution)/shard_map/pallas_call | solution.py:17
  93.9 33.6 %all-gather = f32[32,128]{1,0:T(8,128)S(1)} all-gather(f32[8,128]{1,0:T(8,128)S(1)} %add.23), channel_id=2, replica_groups=mesh['fsdp'=64,'dp'=4] {'dp'}, dimensions={0}, use_global_device_ids=true | all-gather | bytes 20480 | tf_op jit(solution)/shard_map/all_gather | solution.py:236
  127.5 13.0 %all-gather.1 = f32[64,128]{1,0:T(8,128)S(1)} all-gather(f32[8,128]{1,0:T(8,128)S(1)} %bitcast_reduce_fusion.1), channel_id=3, replica_groups={{0,4,8,12,16,20,24,28},{32,36,40,44,48,52,56,60},{64,68,72,76,80,84,88,..., dimensions={0}, use_global_device_ids=true | all-gather | bytes 36864 | tf_op jit(solution)/shard_map/all_gather | solution.py:237
  140.5 25.3 %all_gather.19.adam_ref = f32[64,128]{1,0:T(8,128)S(1)} all-gather(f32[8,128]{1,0:T(8,128)S(1)} %bitcast_reduce_fusion), channel_id=1, replica_groups={{0,32,64,96,128,160,192,224},{4,36,68,100,132,164,196,228},{8,40,72,104..., dimensions={0}, use_global_device_ids=true | all-gather | bytes 36864 | tf_op jit(solution)/shard_map/all_gather | solution.py:238
  165.8 1.6 copy-done.1
  167.4 3.1 %shard_map.107 = (f32[2,256,1024]{2,1,0:T(8,128)}, f32[2,256,1024]{2,1,0:T(8,128)}) custom-call(s32[4]{0:T(128)S(1)} %pad_add_fusion.spot_ref, bf16[256,1024]{1,0:T(8,128)(2,1)S(1)} %collective-permute-done.6.p0, bf16[256,1024]{1,0:T(8,128)(2,1)S(1)} %collective-permute-done.7.p1, bf16[256,1024]{1,0:T(8,128)(2,1)S(1)} %collective-permute-done.8.p2, ...), custom_call_target="tpu_custom_call" | custom-call | bytes 10485760 | tf_op jit(solution)/shard_map/pallas_call | solution.py:243
  170.5 1.7 shard_map.109
  (46 shorter events, 9.7 us)
Async XLA Ops:
  0.6 10.4 %copy-start.2 = (bf16[8,16,8,256]{3,2,1,0:T(8,128)(2,1)S(1)}, bf16[8,16,8,256]{3,2,1,0:T(8,128)(2,1)}, u32[]{:S(2)}) copy-start(bf16[8,16,8,256]{3,2,1,0:T(8,128)(2,1)} %grad_ref.3) | copy-start | bytes 1572868
  0.7 1.3 copy-start.4
  2.0 1.2 copy-start.5
  3.2 7.7 %copy-start.8 = (s32[64]{0:T(128)S(1)}, s32[64]{0:T(128)}, u32[]{:S(2)}) copy-start(s32[64]{0:T(128)} %slot_ref.5) | copy-start | bytes 772
  5.2 53.5 %collective-permute-start = (bf16[256,1024]{1,0:T(8,128)(2,1)}, bf16[256,1024]{1,0:T(8,128)(2,1)S(1)}, u32[]{:S(2)}, u32[]{:S(2)}) collective-permute-start(bf16[256,1024]{1,0:T(8,128)(2,1)} %get-tuple-element.34), channel_id=1, source_target_pairs={{0,0},{1,1},{2,4},{3,5},{4,2},{5,3},{6,6},{7,7},{8,8},{9,9},{10,12... | collective-permute-start | bytes 1572872 | tf_op jit(solution)/shard_map/ppermute | solution.py:190
  6.9 51.8 %collective-permute-start.1 = (bf16[256,1024]{1,0:T(8,128)(2,1)}, bf16[256,1024]{1,0:T(8,128)(2,1)S(1)}, u32[]{:S(2)}, u32[]{:S(2)}) collective-permute-start(bf16[256,1024]{1,0:T(8,128)(2,1)} %get-tuple-element.35), channel_id=1, source_target_pairs={{0,1},{1,0},{2,5},{3,4},{4,3},{5,2},{6,7},{7,6},{8,9},{9,8},{10,13... | collective-permute-start | bytes 1572872 | tf_op jit(solution)/shard_map/ppermute | solution.py:190
  8.4 50.3 %collective-permute-start.2 = (bf16[256,1024]{1,0:T(8,128)(2,1)}, bf16[256,1024]{1,0:T(8,128)(2,1)S(1)}, u32[]{:S(2)}, u32[]{:S(2)}) collective-permute-start(bf16[256,1024]{1,0:T(8,128)(2,1)} %get-tuple-element.36), channel_id=1, source_target_pairs={{0,4},{1,5},{2,0},{3,1},{4,6},{5,7},{6,2},{7,3},{8,12},{9,13},{10,... | collective-permute-start | bytes 1572872 | tf_op jit(solution)/shard_map/ppermute | solution.py:190
  11.0 47.7 %collective-permute-start.3 = (bf16[256,1024]{1,0:T(8,128)(2,1)S(1)}, bf16[256,1024]{1,0:T(8,128)(2,1)S(1)}, u32[]{:S(2)}, u32[]{:S(2)}) collective-permute-start(bf16[256,1024]{1,0:T(8,128)(2,1)S(1)} %get-tuple-element.37), channel_id=1, source_target_pairs={{0,5},{1,4},{2,1},{3,0},{4,7},{5,6},{6,3},{7,2},{8,13},{9,12},{10,... | collective-permute-start | bytes 1572872 | tf_op jit(solution)/shard_map/ppermute | solution.py:190
  13.0 1.2 copy-start.14
  58.7 2.0 %copy-start.13 = (bf16[256,16,128]{2,1,0:T(8,128)(2,1)S(1)}, bf16[256,16,128]{2,1,0:T(8,128)(2,1)}, u32[]{:S(2)}) copy-start(bf16[256,16,128]{2,1,0:T(8,128)(2,1)} %get-tuple-element.59) | copy-start | bytes 3145732
  59.3 3.6 %collective-permute-start.5 = (bf16[512,1024]{1,0:T(8,128)(2,1)S(1)}, bf16[512,1024]{1,0:T(8,128)(2,1)S(1)}, u32[]{:S(2)}, u32[]{:S(2)}) collective-permute-start(bf16[512,1024]{1,0:T(8,128)(2,1)S(1)} %shard_map.104.left_ref), channel_id=1, source_target_pairs={{0,4},{4,0},{8,12},{12,8},{16,20},{20,16},{24,28},{28,24},{32,36},... | collective-permute-start | bytes 3145736 | tf_op jit(solution)/shard_map/ppermute | solution.py:211
  60.7 3.8 %collective-permute-start.4 = (bf16[256,16,128]{2,1,0:T(8,128)(2,1)S(1)}, bf16[256,16,128]{2,1,0:T(8,128)(2,1)S(1)}, u32[]{:S(2)}, u32[]{:S(2)}) collective-permute-start(bf16[256,16,128]{2,1,0:T(8,128)(2,1)S(1)} %copy-done.13), channel_id=1, source_target_pairs={{0,4},{4,0},{8,12},{12,8},{16,20},{20,16},{24,28},{28,24},{32,36},... | collective-permute-start | bytes 3145736 | tf_op jit(solution)/shard_map/ppermute | solution.py:212
  68.3 3.0 %copy-start.7 = (bf16[64,4,16,128]{3,2,1,0:T(8,128)(2,1)}, bf16[64,4,16,128]{3,2,1,0:T(8,128)(2,1)S(1)}, u32[]{:S(2)}) copy-start(bf16[64,4,16,128]{3,2,1,0:T(8,128)(2,1)S(1)} %get-tuple-element.56) | copy-start | bytes 3145732
  71.3 0.8 copy-start.9
  72.1 0.8 copy-start.10
  74.5 91.3 %copy-start = (f32[2,256,1024]{2,1,0:T(8,128)S(1)}, f32[2,256,1024]{2,1,0:T(8,128)}, u32[]{:S(2)}) copy-start(f32[2,256,1024]{2,1,0:T(8,128)} %left_ref.3) | copy-start | bytes 6291460
  74.5 96.0 %all-to-all-start.1 = ((bf16[256,16,128]{2,1,0:T(8,128)(2,1)}), bf16[256,16,128]{2,1,0:T(8,128)(2,1)S(1)}, u32[]{:S(2)}, u32[]{:S(2)}) async-start(bf16[256,16,128]{2,1,0:T(8,128)(2,1)} %bitcast.15), calls=%async_computation.1 | async-start | bytes 2097152 | tf_op jit(solution)/shard_map/all_to_all | solution.py:229
  81.6 84.2 %collective-permute-start.6 = (bf16[256,1024]{1,0:T(8,128)(2,1)}, bf16[256,1024]{1,0:T(8,128)(2,1)S(1)}, u32[]{:S(2)}, u32[]{:S(2)}) collective-permute-start(bf16[256,1024]{1,0:T(8,128)(2,1)} %copy-done.12), channel_id=1, source_target_pairs={{0,0},{1,1},{4,2},{5,3},{2,4},{3,5},{6,6},{7,7},{8,8},{9,9},{12,10... | collective-permute-start | bytes 1572872 | tf_op jit(solution)/shard_map/ppermute | solution.py:228
  83.3 82.5 %collective-permute-start.7 = (bf16[256,1024]{1,0:T(8,128)(2,1)}, bf16[256,1024]{1,0:T(8,128)(2,1)S(1)}, u32[]{:S(2)}, u32[]{:S(2)}) collective-permute-start(bf16[256,1024]{1,0:T(8,128)(2,1)} %copy-done.11), channel_id=1, source_target_pairs={{1,0},{0,1},{5,2},{4,3},{3,4},{2,5},{7,6},{6,7},{9,8},{8,9},{13,10... | collective-permute-start | bytes 1572872 | tf_op jit(solution)/shard_map/ppermute | solution.py:228
  84.8 81.0 %collective-permute-start.8 = (bf16[256,1024]{1,0:T(8,128)(2,1)}, bf16[256,1024]{1,0:T(8,128)(2,1)S(1)}, u32[]{:S(2)}, u32[]{:S(2)}) collective-permute-start(bf16[256,1024]{1,0:T(8,128)(2,1)} %copy-done.10), channel_id=1, source_target_pairs={{4,0},{5,1},{0,2},{1,3},{6,4},{7,5},{2,6},{3,7},{12,8},{13,9},{8,1... | collective-permute-start | bytes 1572872 | tf_op jit(solution)/shard_map/ppermute | solution.py:228
  89.0 76.8 %collective-permute-start.9 = (bf16[256,1024]{1,0:T(8,128)(2,1)}, bf16[256,1024]{1,0:T(8,128)(2,1)S(1)}, u32[]{:S(2)}, u32[]{:S(2)}) collective-permute-start(bf16[256,1024]{1,0:T(8,128)(2,1)} %copy-done.9), channel_id=1, source_target_pairs={{5,0},{4,1},{1,2},{0,3},{7,4},{6,5},{3,6},{2,7},{13,8},{12,9},{9,1... | collective-permute-start | bytes 1572872 | tf_op jit(solution)/shard_map/ppermute | solution.py:228
  89.6 1.0 copy-start.3
  90.6 1.2 copy-start.6
  165.8 1.6 copy-start.1
  (2 other events, 1.6 us)

commit v4 on v2

--- a/solution.py
+++ b/solution.py
@@ -33,7 +33,7 @@
     return ((slot >> 2) << 3) + (slot & 3)
 
 
-def spread_kernel(slot_ref, grad_ref, after_ref, out_ref, wide):
+def spread_kernel(slot_ref, grad_ref, out_ref, wide):
     row_blocks, rows, column_blocks, quarter = grad_ref.shape
     half = quarter // 2
     out_ref[...] = jnp.zeros_like(out_ref)
@@ -49,7 +49,7 @@
 
 def moment_kernel(slot_ref, grad_ref, second_ref, new_ref, sent_ref, part):
     row_blocks, _, column_blocks, _ = grad_ref.shape
-    part[...] = jnp.zeros_like(part)
+    sent_ref[...] = jnp.zeros_like(sent_ref)
     for r in range(row_blocks):
         g = grad_ref[r].astype(F32)
         new = 0.9 * second_ref[r] + 0.1 * g * g
@@ -57,7 +57,10 @@
         adam = g / (jnp.sqrt(new) + 1e-08)
         sums = jnp.sum(jnp.sum(adam * adam, axis=0), axis=1, keepdims=True)
         part[r * column_blocks : (r + 1) * column_blocks, :] = jnp.broadcast_to(sums, (column_blocks, 128))
-    sent_ref[...] = part[...].T[0:8, :]
+    for b in range(row_blocks * column_blocks):
+        at = spread_row(slot_ref[b])
+        sent_ref[at] = part[b : b + 1, :]
+        sent_ref[at + 4] = part[b : b + 1, :]
 
 
 def pack_kernel(spot_ref, left_ref, right_ref, *outs):
@@ -72,15 +75,15 @@
 
 
 def unpack_kernel(spot_ref, *refs):
-    got, out = refs[:-1], refs[-1]
-    half = out.shape[0] // len(got)
+    got, (left_ref, right_ref) = refs[:-2], refs[-2:]
+    half = right_ref.shape[1]
     for m, ref in enumerate(got):
-        out[m * half : (m + 1) * half, :] = ref[:half, :]
-
-
-def update_kernel(spot_ref, own_ref, other_ref, left_ref, left2_ref, *refs):
-    rights = refs[0:4]
-    grad, update_ref, norm_ref, root, mixed = refs[4:]
+        left_ref[m * half : (m + 1) * half, :] = ref[:half, :]
+        right_ref[m] = ref[half:, :]
+
+
+def update_kernel(spot_ref, own_ref, other_ref, left_ref, left2_ref, right_ref, *refs):
+    grad, update_ref, norm_ref, root, mixed = refs
     core, lane = spot_ref[1], spot_ref[2]
     owners, chips, piece, half = own_ref.shape
     order = grad.shape[0]
@@ -91,7 +94,7 @@
         grad[:, pl.ds(theirs, half)] = other_ref[:, d].reshape(order, half)
         to = pl.ds(pl.multiple_of((lane ^ d) * half, half), half)
         for t in range(0, order, half):
-            root[t : t + half, to] = rights[d][half:, t : t + half]
+            root[t : t + half, to] = right_ref[d, :, t : t + half]
     for t in range(0, order, 512):
         mixed[t : t + 512, :] = jnp.dot(grad[t : t + 512, :], root[...], preferred_element_type=F32).astype(BF16)
     total = jnp.zeros((8, 128), F32)
@@ -127,8 +130,9 @@
             out[half:, n : n + 256] = right[m * half : (m + 1) * half].astype(BF16)
 
 
-def graft_kernel(spot_ref, update_ref, norm_ref, norm2_ref, after_ref, out_ref):
-    scale = 1.0 / jnp.sqrt(norm_ref[0:1, :] + norm2_ref[0:1, :] + 1e-06)
+def graft_kernel(spot_ref, update_ref, norm_ref, norm2_ref, adam_ref, out_ref):
+    adam = jnp.sum(adam_ref[...], axis=0)
+    scale = jnp.sqrt(adam / (norm_ref[0:1, :] + norm2_ref[0:1, :] + 1e-06))
     out_ref[...] = (update_ref[...].astype(F32) * scale[None, None]).astype(BF16)
 
 
@@ -142,19 +146,15 @@
             new_right_ref[0] = right_ref[0] + ref[half:, :].astype(F32)
 
 
-def direction_kernel(slot_ref, values_ref, adam_ref, out_ref, wide, scales):
+def direction_kernel(slot_ref, values_ref, out_ref, wide):
     row_blocks, rows, column_blocks, quarter = out_ref.shape
     half = quarter // 2
     size = wide.shape[0] // 2
-    copies = jnp.sum(adam_ref[...].reshape(-1, 8, 128), axis=0)
-    total = jnp.sqrt(copies[0:1, :])
-    scales[...] = jnp.broadcast_to(total, scales.shape).T
     for b in range(row_blocks * column_blocks):
         at = spread_row(slot_ref[b])
         start = (b // column_blocks) * rows * column_blocks + b % column_blocks
-        scale = scales[b : b + 1, :]
-        wide[pl.ds(start, rows, stride=column_blocks), :] = values_ref[at].astype(F32) * scale
-        wide[pl.ds(size + start, rows, stride=column_blocks), :] = values_ref[at + 4].astype(F32) * scale
+        wide[pl.ds(start, rows, stride=column_blocks), :] = values_ref[at].astype(F32)
+        wide[pl.ds(size + start, rows, stride=column_blocks), :] = values_ref[at + 4].astype(F32)
     for h in range(2):
         part = wide[h * size : (h + 1) * size, :].reshape(row_blocks, rows, column_blocks, half)
         out_ref[..., h * half : (h + 1) * half] = part.astype(out_ref.dtype)
@@ -191,22 +191,30 @@
     )
     roots = [lax.ppermute(packed[m], AXES, matching(m, False)) for m in range(chips)]
 
-    pieces = local(
-        spread_kernel, shape((devices, piece_rows, half), BF16), (block_slot, gradient, packed[0]),
-        scratch=[pltpu.VMEM((2 * blocks * piece_rows, half), F32)], limit=6, moved=MIB * 3 // 2,
-    )
-    own = lax.all_to_all(pieces, AXES, split_axis=0, concat_axis=0, tiled=True)
-
     new_second, sent = local(
         moment_kernel,
-        [shape(second_moment.shape, F32), shape((8, 128), F32)],
+        [shape(second_moment.shape, F32), shape((devices, 1, 128), F32)],
         (block_slot, gradient, second_moment),
-        scratch=[pltpu.VMEM((128, 128), F32)], limit=6, moved=MIB * 5 // 2,
-    )
-    adam = lax.all_gather(sent, AXES, axis=0, tiled=True)
+        scratch=[pltpu.VMEM((blocks, 128), F32)], limit=6, moved=MIB * 5 // 2,
+    )
+    adam = lax.all_to_all(sent, AXES, split_axis=0, concat_axis=0, tiled=True)
+
+    pieces = local(
+        spread_kernel, shape((devices, piece_rows, half), BF16), (block_slot, gradient),
+        scratch=[pltpu.VMEM((2 * blocks * piece_rows, half), F32)], limit=6, moved=MIB * 3 // 2,
+    )
+    own = lax.cond(
+        block_slot[0] >= 0,
+        lambda x: lax.all_to_all(x, AXES, split_axis=0, concat_axis=0, tiled=True),
+        lambda x: x,
+        pieces,
+    )
 
     own, *roots = lax.optimization_barrier((own, *roots))
-    left = local(unpack_kernel, shape((order // 2, order), BF16), (spot, *roots), limit=4, moved=2 * MIB)
+    left, right = local(
+        unpack_kernel, [shape((order // 2, order), BF16), shape((chips, half, order), BF16)], (spot, *roots),
+        limit=5, moved=4 * MIB,
+    )
     left2 = lax.ppermute(left, "fsdp", swap)
     other = lax.ppermute(own, "fsdp", swap)
 
@@ -214,7 +222,7 @@
     grad, update, norm = local(
         update_kernel,
         [shape((order, order), BF16), shape(cut, BF16), shape((8, 128), F32)],
-        (spot, own.reshape(cut), other.reshape(cut), left, left2, *roots),
+        (spot, own.reshape(cut), other.reshape(cut), left, left2, right),
         scratch=[pltpu.VMEM((order, order // 2), BF16)] * 2,
         flops=2 * order * order * order, limit=18, moved=8 * MIB,
     )
@@ -224,8 +232,8 @@
         scratch=[pltpu.VMEM((order // 2, order), BF16)] * 2,
         flops=2 * order * order * order, limit=11, moved=4 * MIB,
     )
-    update, adam = lax.optimization_barrier((update, adam))
-    back = local(graft_kernel, shape(cut, BF16), (spot, update, norm, norm2, products[0]), limit=5, moved=2 * MIB)
+    update, *products = lax.optimization_barrier((update, *products))
+    back = local(graft_kernel, shape(cut, BF16), (spot, update, norm, norm2, adam), limit=5, moved=2 * MIB)
     products = [lax.ppermute(products[m], AXES, matching(m, True)) for m in range(chips)]
     returned = lax.all_to_all(back.reshape(devices, piece_rows, half), AXES, split_axis=0, concat_axis=0, tiled=True)
 
@@ -242,8 +250,8 @@
     )(spot, *products, stat_left, stat_right)
 
     direction = local(
-        direction_kernel, shape(gradient.shape, gradient.dtype), (block_slot, returned, adam),
-        scratch=[pltpu.VMEM((2 * blocks * piece_rows, half), F32), pltpu.VMEM((128, 128), F32)],
+        direction_kernel, shape(gradient.shape, gradient.dtype), (block_slot, returned),
+        scratch=[pltpu.VMEM((2 * blocks * piece_rows, half), F32)],
         limit=7, moved=2 * MIB,
     )
     return (new_left, new_right, new_second, direction)

time: 208 us -> 147 us (0.71)
  waiting for transfers between devices: 112 us -> 30.6 us
  blocking collectives: 0 us -> 43.3 us
  between operations: 14.2 us -> 0.84 us
  local copies, waits for them, and re-layouts: 15.9 us -> 8.8 us
  starting transfers between devices: 46.4 us -> 39.5 us
  Pallas kernels: 19.1 us -> 23.4 us
    all_gather x1 -> x0, waiting for transfers between devices: 48.5 us -> none  [body(): adam = lax.all_gather(sent, AXES, axis=0, tiled=True)]
    all_to_all x0 -> x1, blocking collectives: none -> 43.3 us  [body(): lax.all_to_all(x, AXES, split_axis=0, concat_axis=0, tiled=True)]
    ppermute x4, waiting for transfers between devices: 28.8 us -> 0.01 us  [body(): lax.ppermute(packed[m], AXES, matching(m, False))]
    all_to_all x1, starting transfers between devices: 15.7 us -> 6.56 us  [body(): adam = lax.all_to_all(sent, AXES, split_axis=0, concat_axis=0, tiled=True)]
    unnamed x46 -> x26, local copies, waits for them, and re-layouts: 15.9 us -> 7.57 us
    pallas_call x8, Pallas kernels: 16 us -> 20.4 us  [local(): pl.pallas_call(kernel, out_shape=outs, in_specs=[SMEM] + [VMEM] * (len(in...]
    ppermute x1, starting transfers between devices: 2.64 us -> 0.01 us  [body(): left2 = lax.ppermute(left, 'fsdp', swap)]
    ppermute x1, waiting for transfers between devices: 2.19 us -> 0.01 us  [body(): left2 = lax.ppermute(left, 'fsdp', swap)]
  transfers between devices with their start and end apart: 14 -> 13, of which waited for: 10 -> 3; matrix products, arithmetic and copies ran while one was open for 0% -> 1% of each run, Pallas kernels for 6% -> 11%
where the time goes in v4:
time: 147 us
  blocking collectives  43.3 us (29%)
  starting transfers between devices  39.5 us (27%)
  waiting for transfers between devices  30.6 us (21%)
  Pallas kernels  23.4 us (16%)
  local copies, waits for them, and re-layouts  8.8 us (6%)
    all_to_all x1, blocking collectives, body(): lax.all_to_all(x, AXES, split_axis=0, concat_axis=0, tiled=True)  43.3 us
    ppermute x4, waiting for transfers between devices, body(): lax.ppermute(products[m], AXES, matching(m, True))  30.6 us
    pallas_call x8, Pallas kernels, local(): pl.pallas_call(kernel, out_shape=outs, in_specs=[SMEM] + [VMEM] * (len(in...  20.4 us
    all_to_all x1, starting transfers between devices, body(): lax.all_to_all(back.reshape(devices, piece_rows, half), AXES, split_axis=...  11.7 us
    ppermute x4, starting transfers between devices, body(): lax.ppermute(packed[m], AXES, matching(m, False))  9.36 us
    ppermute x4, starting transfers between devices, body(): lax.ppermute(products[m], AXES, matching(m, True))  8.95 us
    unnamed x26, local copies, waits for them, and re-layouts  7.57 us
    all_to_all x1, starting transfers between devices, body(): adam = lax.all_to_all(sent, AXES, split_axis=0, concat_axis=0, tiled=True)  6.56 us
  transfers between devices with their start and end apart: 13, of which 3 were waited for; matrix products, arithmetic and copies ran while one was open for 1% of the time, Pallas kernels for 11%

profile of v4, /device:TPU:1, one launch (start us, length us, event | category | flops | bytes accessed | tf_op | source)
XLA Modules:
  0.0 146.5 jit_solution(11125046647342366499)
XLA Ops:
  0.7 1.3 copy-done.3
  2.0 1.2 copy-done.4
  3.2 2.2 %shard_map.103 = (bf16[256,1024]{1,0:T(8,128)(2,1)}, bf16[256,1024]{1,0:T(8,128)(2,1)}, bf16[256,1024]{1,0:T(8,128)(2,1)}, bf16[256,1024]{1,0:T(8,128)(2,1)}) custom-call(s32[3]{0:T(128)S(1)} %pad_add_fusion.spot_ref, bf16[2,256,1024]{2,1,0:T(8,128)(2,1)S(1)} %copy-done.3, bf16[2,1024,256]{2,1,0:T(8,128)(2,1)S(1)} %copy-done.4), custom_call_target="tpu_custom_call" | custom-call | bytes 4194304 | tf_op jit(solution)/shard_map/pallas_call | solution.py:17
  5.4 6.2 %collective-permute-start = (bf16[256,1024]{1,0:T(8,128)(2,1)}, bf16[256,1024]{1,0:T(8,128)(2,1)S(1)}, u32[]{:S(2)}, u32[]{:S(2)}) collective-permute-start(bf16[256,1024]{1,0:T(8,128)(2,1)} %get-tuple-element.36), channel_id=1, source_target_pairs={{0,0},{1,1},{2,4},{3,5},{4,2},{5,3},{6,6},{7,7},{8,8},{9,9},{10,12... | collective-permute-start | bytes 1572872 | tf_op jit(solution)/shard_map/ppermute | solution.py:192
  12.2 2.6 %collective-permute-start.3 = (bf16[256,1024]{1,0:T(8,128)(2,1)}, bf16[256,1024]{1,0:T(8,128)(2,1)}, u32[]{:S(2)}, u32[]{:S(2)}) collective-permute-start(bf16[256,1024]{1,0:T(8,128)(2,1)} %get-tuple-element.39), channel_id=1, source_target_pairs={{0,5},{1,4},{2,1},{3,0},{4,7},{5,6},{6,3},{7,2},{8,13},{9,12},{10,... | collective-permute-start | bytes 1572872 | tf_op jit(solution)/shard_map/ppermute | solution.py:192
  14.8 1.9 %shard_map.102 = bf16[256,16,128]{2,1,0:T(8,128)(2,1)} custom-call(s32[64]{0:T(128)S(1)} %copy-done.6, bf16[8,16,8,256]{3,2,1,0:T(8,128)(2,1)S(1)} %copy-done.2), custom_call_target="tpu_custom_call" | custom-call | bytes 1572864 | tf_op jit(solution)/shard_map/pallas_call | solution.py:17
  16.8 44.5 %conditional.1 = (bf16[256,16,128]{2,1,0:T(8,128)(2,1)}) conditional(s32[]{:T(128)} %bitcast.3, bf16[256,16,128]{2,1,0:T(8,128)(2,1)} %shard_map.102, bf16[256,16,128]{2,1,0:T(8,128)(2,1)} %shard_map.102), branch_computations={%region_0.1_spmd, %region_1.2_spmd} | conditional | bytes 4194312 | solution.py:206
  16.8 1.2 copy.13
  18.0 43.3 %all_to_all.14 = bf16[256,16,128]{2,1,0:T(8,128)(2,1)} all-to-all(bf16[256,16,128]{2,1,0:T(8,128)(2,1)S(1)} %copy.13), channel_id=1, replica_groups=mesh['fsdp'=64,'dp'=4] {'fsdp','dp'}, dimensions={0} | all-to-all | bytes 2097152 | tf_op jit(solution)/shard_map/cond/branch_1_fun/all_to_all | solution.py:208
  61.3 2.2 %shard_map.104 = (bf16[512,1024]{1,0:T(8,128)(2,1)}, bf16[4,128,1024]{2,1,0:T(8,128)(2,1)S(1)}) custom-call(s32[3]{0:T(128)S(1)} %pad_add_fusion.spot_ref, bf16[256,1024]{1,0:T(8,128)(2,1)S(1)} %collective-permute-done.refs_0_, bf16[256,1024]{1,0:T(8,128)(2,1)S(1)} %collective-permute-done.1.refs_1_, bf16[256,1024]{1,0:T(8,128)(2,1)S(1)} %collective-permute-done.2.refs_2_, ...), custom_call_target="tpu_custom_call" | custom-call | bytes 4194304 | tf_op jit(solution)/shard_map/pallas_call | solution.py:17
  65.0 2.3 %shard_map.108 = (f32[8,16,8,256]{3,2,1,0:T(8,128)}, f32[256,1,128]{2,1,0:T(1,128)}) custom-call(s32[64]{0:T(128)S(1)} %copy-done.6, bf16[8,16,8,256]{3,2,1,0:T(8,128)(2,1)S(1)} %copy-done.2, f32[8,16,8,256]{3,2,1,0:T(8,128)S(1)} %copy-done.5), custom_call_target="tpu_custom_call" | custom-call | bytes 2621440 | tf_op jit(solution)/shard_map/pallas_call | solution.py:17
  67.3 6.6 %all-to-all-start.1 = ((f32[256,1,128]{2,1,0:T(1,128)}), f32[256,1,128]{2,1,0:T(1,128)S(1)}, u32[]{:S(2)}, u32[]{:S(2)}) async-start(f32[256,1,128]{2,1,0:T(1,128)} %get-tuple-element.62), calls=%async_computation.1 | async-start | bytes 262144 | tf_op jit(solution)/shard_map/all_to_all | solution.py:200
  75.1 5.2 %shard_map.105 = (bf16[1024,1024]{1,0:T(8,128)(2,1)S(1)}, bf16[64,4,16,128]{3,2,1,0:T(8,128)(2,1)S(1)}, f32[8,128]{1,0:T(8,128)S(1)}) custom-call(s32[3]{0:T(128)S(1)} %pad_add_fusion.spot_ref, bf16[64,4,16,128]{3,2,1,0:T(8,128)(2,1)} %bitcast.4.own_ref, bf16[64,4,16,128]{3,2,1,0:T(8,128)(2,1)} %bitcast.5.other_ref, ...), custom_call_target="tpu_custom_call" | custom-call | flops 2147483648 | bytes 8388608 | tf_op jit(solution)/shard_map/pallas_call | solution.py:17
  80.3 2.4 %collective-permute-start.10 = (f32[8,128]{1,0:T(8,128)S(1)}, f32[8,128]{1,0:T(8,128)S(1)}, u32[]{:S(2)}, u32[]{:S(2)}) collective-permute-start(f32[8,128]{1,0:T(8,128)S(1)} %get-tuple-element.61.norm_ref), channel_id=1, source_target_pairs={{0,4},{4,0},{8,12},{12,8},{16,20},{20,16},{24,28},{28,24},{32,36},... | collective-permute-start | bytes 12296 | tf_op jit(solution)/shard_map/ppermute | solution.py:229
  82.6 3.0 %shard_map.106 = (bf16[256,1024]{1,0:T(8,128)(2,1)S(1)}, bf16[256,1024]{1,0:T(8,128)(2,1)S(1)}, bf16[256,1024]{1,0:T(8,128)(2,1)S(1)}, bf16[256,1024]{1,0:T(8,128)(2,1)S(1)}) custom-call(s32[3]{0:T(128)S(1)} %pad_add_fusion.spot_ref, bf16[1024,1024]{1,0:T(8,128)(2,1)S(1)} %get-tuple-element.48.grad), custom_call_target="tpu_custom_call" | custom-call | flops 2147483648 | bytes 4194304 | tf_op jit(solution)/shard_map/pallas_call | solution.py:17
  86.9 2.0 %shard_map.109 = bf16[64,4,16,128]{3,2,1,0:T(8,128)(2,1)} custom-call(s32[3]{0:T(128)S(1)} %pad_add_fusion.spot_ref, bf16[64,4,16,128]{3,2,1,0:T(8,128)(2,1)S(1)} %get-tuple-element.60.update_ref, f32[8,128]{1,0:T(8,128)S(1)} %get-tuple-element.61.norm_ref, f32[8,128]{1,0:T(8,128)S(1)} %collective-permute-done.10.norm2_ref, ...), custom_call_target="tpu_custom_call" | custom-call | bytes 2097152 | tf_op jit(solution)/shard_map/pallas_call | solution.py:17
  88.9 11.7 %all-to-all-start.2 = ((bf16[256,16,128]{2,1,0:T(8,128)(2,1)}), bf16[256,16,128]{2,1,0:T(8,128)(2,1)S(1)}, u32[]{:S(2)}, u32[]{:S(2)}) async-start(bf16[256,16,128]{2,1,0:T(8,128)(2,1)} %bitcast.6), calls=%async_computation.2 | async-start | bytes 2097152 | tf_op jit(solution)/shard_map/all_to_all | solution.py:238
  100.7 5.1 %collective-permute-start.6 = (bf16[256,1024]{1,0:T(8,128)(2,1)}, bf16[256,1024]{1,0:T(8,128)(2,1)S(1)}, u32[]{:S(2)}, u32[]{:S(2)}) collective-permute-start(bf16[256,1024]{1,0:T(8,128)(2,1)} %copy-done.12), channel_id=1, source_target_pairs={{0,0},{1,1},{4,2},{5,3},{2,4},{3,5},{6,6},{7,7},{8,8},{9,9},{12,10... | collective-permute-start | bytes 1572872 | tf_op jit(solution)/shard_map/ppermute | solution.py:237
  106.7 2.9 %collective-permute-start.9 = (bf16[256,1024]{1,0:T(8,128)(2,1)}, bf16[256,1024]{1,0:T(8,128)(2,1)S(1)}, u32[]{:S(2)}, u32[]{:S(2)}) collective-permute-start(bf16[256,1024]{1,0:T(8,128)(2,1)} %copy-done.9), channel_id=1, source_target_pairs={{5,0},{4,1},{1,2},{0,3},{7,4},{6,5},{3,6},{2,7},{13,8},{12,9},{9,1... | collective-permute-start | bytes 1572872 | tf_op jit(solution)/shard_map/ppermute | solution.py:237
  109.6 17.0 %collective-permute-done.6.p0 = bf16[256,1024]{1,0:T(8,128)(2,1)S(1)} collective-permute-done((bf16[256,1024]{1,0:T(8,128)(2,1)}, bf16[256,1024]{1,0:T(8,128)(2,1)S(1)}, u32[]{:S(2)}, u32[]{:S(2)}) %collective-permute-start.6) | collective-permute-done | bytes 524320 | tf_op jit(solution)/shard_map/ppermute | solution.py:237
  126.6 13.5 %collective-permute-done.7.p1 = bf16[256,1024]{1,0:T(8,128)(2,1)S(1)} collective-permute-done((bf16[256,1024]{1,0:T(8,128)(2,1)}, bf16[256,1024]{1,0:T(8,128)(2,1)S(1)}, u32[]{:S(2)}, u32[]{:S(2)}) %collective-permute-start.7) | collective-permute-done | bytes 524320 | tf_op jit(solution)/shard_map/ppermute | solution.py:237
  140.2 1.6 %copy-done.1 = f32[2,256,1024]{2,1,0:T(8,128)S(1)} copy-done((f32[2,256,1024]{2,1,0:T(8,128)S(1)}, f32[2,256,1024]{2,1,0:T(8,128)}, u32[]{:S(2)}) %copy-start.1) | copy-done | bytes 2097176
  141.8 3.1 %shard_map.107 = (f32[2,256,1024]{2,1,0:T(8,128)}, f32[2,256,1024]{2,1,0:T(8,128)}) custom-call(s32[3]{0:T(128)S(1)} %pad_add_fusion.spot_ref, bf16[256,1024]{1,0:T(8,128)(2,1)S(1)} %collective-permute-done.6.p0, bf16[256,1024]{1,0:T(8,128)(2,1)S(1)} %collective-permute-done.7.p1, bf16[256,1024]{1,0:T(8,128)(2,1)S(1)} %collective-permute-done.8.p2, ...), custom_call_target="tpu_custom_call" | custom-call | bytes 10485760 | tf_op jit(solution)/shard_map/pallas_call | solution.py:242
  144.9 1.6 %shard_map.110 = bf16[8,16,8,256]{3,2,1,0:T(8,128)(2,1)} custom-call(s32[64]{0:T(128)S(1)} %copy-done.6, bf16[256,16,128]{2,1,0:T(8,128)(2,1)S(1)} %all-to-all-done.2.values_ref), custom_call_target="tpu_custom_call" | custom-call | bytes 2097152 | tf_op jit(solution)/shard_map/pallas_call | solution.py:17
  (41 shorter events, 5.8 us)
Async XLA Ops:
  0.6 14.2 %copy-start.2 = (bf16[8,16,8,256]{3,2,1,0:T(8,128)(2,1)S(1)}, bf16[8,16,8,256]{3,2,1,0:T(8,128)(2,1)}, u32[]{:S(2)}) copy-start(bf16[8,16,8,256]{3,2,1,0:T(8,128)(2,1)} %grad_ref.3) | copy-start | bytes 1572868
  0.7 1.3 copy-start.3
  2.0 1.2 copy-start.4
  3.2 11.6 %copy-start.6 = (s32[64]{0:T(128)S(1)}, s32[64]{0:T(128)}, u32[]{:S(2)}) copy-start(s32[64]{0:T(128)} %slot_ref.5) | copy-start | bytes 772
  5.4 55.8 %collective-permute-start = (bf16[256,1024]{1,0:T(8,128)(2,1)}, bf16[256,1024]{1,0:T(8,128)(2,1)S(1)}, u32[]{:S(2)}, u32[]{:S(2)}) collective-permute-start(bf16[256,1024]{1,0:T(8,128)(2,1)} %get-tuple-element.36), channel_id=1, source_target_pairs={{0,0},{1,1},{2,4},{3,5},{4,2},{5,3},{6,6},{7,7},{8,8},{9,9},{10,12... | collective-permute-start | bytes 1572872 | tf_op jit(solution)/shard_map/ppermute | solution.py:192
  11.6 49.6 %collective-permute-start.1 = (bf16[256,1024]{1,0:T(8,128)(2,1)}, bf16[256,1024]{1,0:T(8,128)(2,1)S(1)}, u32[]{:S(2)}, u32[]{:S(2)}) collective-permute-start(bf16[256,1024]{1,0:T(8,128)(2,1)} %get-tuple-element.37), channel_id=1, source_target_pairs={{0,1},{1,0},{2,5},{3,4},{4,3},{5,2},{6,7},{7,6},{8,9},{9,8},{10,13... | collective-permute-start | bytes 1572872 | tf_op jit(solution)/shard_map/ppermute | solution.py:192
  12.2 49.1 %collective-permute-start.2 = (bf16[256,1024]{1,0:T(8,128)(2,1)}, bf16[256,1024]{1,0:T(8,128)(2,1)S(1)}, u32[]{:S(2)}, u32[]{:S(2)}) collective-permute-start(bf16[256,1024]{1,0:T(8,128)(2,1)} %get-tuple-element.38), channel_id=1, source_target_pairs={{0,4},{1,5},{2,0},{3,1},{4,6},{5,7},{6,2},{7,3},{8,12},{9,13},{10,... | collective-permute-start | bytes 1572872 | tf_op jit(solution)/shard_map/ppermute | solution.py:192
  12.2 49.1 %collective-permute-start.3 = (bf16[256,1024]{1,0:T(8,128)(2,1)}, bf16[256,1024]{1,0:T(8,128)(2,1)}, u32[]{:S(2)}, u32[]{:S(2)}) collective-permute-start(bf16[256,1024]{1,0:T(8,128)(2,1)} %get-tuple-element.39), channel_id=1, source_target_pairs={{0,5},{1,4},{2,1},{3,0},{4,7},{5,6},{6,3},{7,2},{8,13},{9,12},{10,... | collective-permute-start | bytes 1572872 | tf_op jit(solution)/shard_map/ppermute | solution.py:192
  61.3 3.7 %copy-start.5 = (f32[8,16,8,256]{3,2,1,0:T(8,128)S(1)}, f32[8,16,8,256]{3,2,1,0:T(8,128)}, u32[]{:S(2)}) copy-start(f32[8,16,8,256]{3,2,1,0:T(8,128)} %second_ref.1) | copy-start | bytes 3145732
  63.5 1.0 copy-start.7
  64.5 9.4 %collective-permute-start.5 = (bf16[512,1024]{1,0:T(8,128)(2,1)}, bf16[512,1024]{1,0:T(8,128)(2,1)S(1)}, u32[]{:S(2)}, u32[]{:S(2)}) collective-permute-start(bf16[512,1024]{1,0:T(8,128)(2,1)} %get-tuple-element.45.left_ref), channel_id=1, source_target_pairs={{0,4},{4,0},{8,12},{12,8},{16,20},{20,16},{24,28},{28,24},{32,36},... | collective-permute-start | bytes 3145736 | tf_op jit(solution)/shard_map/ppermute | solution.py:218
  64.5 9.4 %collective-permute-start.4 = (bf16[256,16,128]{2,1,0:T(8,128)(2,1)}, bf16[256,16,128]{2,1,0:T(8,128)(2,1)}, u32[]{:S(2)}, u32[]{:S(2)}) collective-permute-start(bf16[256,16,128]{2,1,0:T(8,128)(2,1)} %get-tuple-element.63), channel_id=1, source_target_pairs={{0,4},{4,0},{8,12},{12,8},{16,20},{20,16},{24,28},{28,24},{32,36},... | collective-permute-start | bytes 3145736 | tf_op jit(solution)/shard_map/ppermute | solution.py:219
  67.3 19.6 %all-to-all-start.1 = ((f32[256,1,128]{2,1,0:T(1,128)}), f32[256,1,128]{2,1,0:T(1,128)S(1)}, u32[]{:S(2)}, u32[]{:S(2)}) async-start(f32[256,1,128]{2,1,0:T(1,128)} %get-tuple-element.62), calls=%async_computation.1 | async-start | bytes 262144 | tf_op jit(solution)/shard_map/all_to_all | solution.py:200
  73.9 1.2 copy-start.8
  80.3 6.7 %collective-permute-start.10 = (f32[8,128]{1,0:T(8,128)S(1)}, f32[8,128]{1,0:T(8,128)S(1)}, u32[]{:S(2)}, u32[]{:S(2)}) collective-permute-start(f32[8,128]{1,0:T(8,128)S(1)} %get-tuple-element.61.norm_ref), channel_id=1, source_target_pairs={{0,4},{4,0},{8,12},{12,8},{16,20},{20,16},{24,28},{28,24},{32,36},... | collective-permute-start | bytes 12296 | tf_op jit(solution)/shard_map/ppermute | solution.py:229
  85.6 1.1 copy-start.11
  85.7 1.3 copy-start.12
  86.9 53.3 %copy-start = (f32[2,256,1024]{2,1,0:T(8,128)S(1)}, f32[2,256,1024]{2,1,0:T(8,128)}, u32[]{:S(2)}) copy-start(f32[2,256,1024]{2,1,0:T(8,128)} %left_ref.3) | copy-start | bytes 6291460
  88.9 56.0 %all-to-all-start.2 = ((bf16[256,16,128]{2,1,0:T(8,128)(2,1)}), bf16[256,16,128]{2,1,0:T(8,128)(2,1)S(1)}, u32[]{:S(2)}, u32[]{:S(2)}) async-start(bf16[256,16,128]{2,1,0:T(8,128)(2,1)} %bitcast.6), calls=%async_computation.2 | async-start | bytes 2097152 | tf_op jit(solution)/shard_map/all_to_all | solution.py:238
  100.7 26.0 %collective-permute-start.6 = (bf16[256,1024]{1,0:T(8,128)(2,1)}, bf16[256,1024]{1,0:T(8,128)(2,1)S(1)}, u32[]{:S(2)}, u32[]{:S(2)}) collective-permute-start(bf16[256,1024]{1,0:T(8,128)(2,1)} %copy-done.12), channel_id=1, source_target_pairs={{0,0},{1,1},{4,2},{5,3},{2,4},{3,5},{6,6},{7,7},{8,8},{9,9},{12,10... | collective-permute-start | bytes 1572872 | tf_op jit(solution)/shard_map/ppermute | solution.py:237
  105.7 34.4 %collective-permute-start.7 = (bf16[256,1024]{1,0:T(8,128)(2,1)}, bf16[256,1024]{1,0:T(8,128)(2,1)S(1)}, u32[]{:S(2)}, u32[]{:S(2)}) collective-permute-start(bf16[256,1024]{1,0:T(8,128)(2,1)} %copy-done.11), channel_id=1, source_target_pairs={{1,0},{0,1},{5,2},{4,3},{3,4},{2,5},{7,6},{6,7},{9,8},{8,9},{13,10... | collective-permute-start | bytes 1572872 | tf_op jit(solution)/shard_map/ppermute | solution.py:237
  106.7 33.4 %collective-permute-start.8 = (bf16[256,1024]{1,0:T(8,128)(2,1)}, bf16[256,1024]{1,0:T(8,128)(2,1)S(1)}, u32[]{:S(2)}, u32[]{:S(2)}) collective-permute-start(bf16[256,1024]{1,0:T(8,128)(2,1)} %copy-done.10), channel_id=1, source_target_pairs={{4,0},{5,1},{0,2},{1,3},{6,4},{7,5},{2,6},{3,7},{12,8},{13,9},{8,1... | collective-permute-start | bytes 1572872 | tf_op jit(solution)/shard_map/ppermute | solution.py:237
  106.7 33.5 %collective-permute-start.9 = (bf16[256,1024]{1,0:T(8,128)(2,1)}, bf16[256,1024]{1,0:T(8,128)(2,1)S(1)}, u32[]{:S(2)}, u32[]{:S(2)}) collective-permute-start(bf16[256,1024]{1,0:T(8,128)(2,1)} %copy-done.9), channel_id=1, source_target_pairs={{5,0},{4,1},{1,2},{0,3},{7,4},{6,5},{3,6},{2,7},{13,8},{12,9},{9,1... | collective-permute-start | bytes 1572872 | tf_op jit(solution)/shard_map/ppermute | solution.py:237
  140.2 1.6 %copy-start.1 = (f32[2,256,1024]{2,1,0:T(8,128)S(1)}, f32[2,256,1024]{2,1,0:T(8,128)}, u32[]{:S(2)}) copy-start(f32[2,256,1024]{2,1,0:T(8,128)} %right_ref.3) | copy-start | bytes 6291460
  (2 other events, 1.8 us)

commit v5 on v2

--- a/solution.py
+++ b/solution.py
@@ -33,7 +33,7 @@
     return ((slot >> 2) << 3) + (slot & 3)
 
 
-def spread_kernel(slot_ref, grad_ref, after_ref, out_ref, wide):
+def spread_kernel(slot_ref, grad_ref, out_ref, wide):
     row_blocks, rows, column_blocks, quarter = grad_ref.shape
     half = quarter // 2
     out_ref[...] = jnp.zeros_like(out_ref)
@@ -47,7 +47,7 @@
         out_ref[at + 4] = wide[pl.ds(size + start, rows, stride=column_blocks), :].astype(BF16)
 
 
-def moment_kernel(slot_ref, grad_ref, second_ref, new_ref, sent_ref, part):
+def moment_kernel(slot_ref, grad_ref, second_ref, after_ref, new_ref, sent_ref, part):
     row_blocks, _, column_blocks, _ = grad_ref.shape
     part[...] = jnp.zeros_like(part)
     for r in range(row_blocks):
@@ -127,7 +127,7 @@
             out[half:, n : n + 256] = right[m * half : (m + 1) * half].astype(BF16)
 
 
-def graft_kernel(spot_ref, update_ref, norm_ref, norm2_ref, after_ref, out_ref):
+def graft_kernel(spot_ref, update_ref, norm_ref, norm2_ref, out_ref):
     scale = 1.0 / jnp.sqrt(norm_ref[0:1, :] + norm2_ref[0:1, :] + 1e-06)
     out_ref[...] = (update_ref[...].astype(F32) * scale[None, None]).astype(BF16)
 
@@ -147,7 +147,7 @@
     half = quarter // 2
     size = wide.shape[0] // 2
     copies = jnp.sum(adam_ref[...].reshape(-1, 8, 128), axis=0)
-    total = jnp.sqrt(copies[0:1, :])
+    total = jnp.sqrt(jnp.sum(copies, axis=0, keepdims=True) * (1.0 / 8))
     scales[...] = jnp.broadcast_to(total, scales.shape).T
     for b in range(row_blocks * column_blocks):
         at = spread_row(slot_ref[b])
@@ -191,19 +191,24 @@
     )
     roots = [lax.ppermute(packed[m], AXES, matching(m, False)) for m in range(chips)]
 
-    pieces = local(
-        spread_kernel, shape((devices, piece_rows, half), BF16), (block_slot, gradient, packed[0]),
-        scratch=[pltpu.VMEM((2 * blocks * piece_rows, half), F32)], limit=6, moved=MIB * 3 // 2,
-    )
-    own = lax.all_to_all(pieces, AXES, split_axis=0, concat_axis=0, tiled=True)
-
     new_second, sent = local(
         moment_kernel,
         [shape(second_moment.shape, F32), shape((8, 128), F32)],
-        (block_slot, gradient, second_moment),
+        (block_slot, gradient, second_moment, packed[0]),
         scratch=[pltpu.VMEM((128, 128), F32)], limit=6, moved=MIB * 5 // 2,
     )
     adam = lax.all_gather(sent, AXES, axis=0, tiled=True)
+
+    pieces = local(
+        spread_kernel, shape((devices, piece_rows, half), BF16), (block_slot, gradient),
+        scratch=[pltpu.VMEM((2 * blocks * piece_rows, half), F32)], limit=6, moved=MIB * 3 // 2,
+    )
+    own = lax.cond(
+        block_slot[0] >= 0,
+        lambda x: lax.all_to_all(x, AXES, split_axis=0, concat_axis=0, tiled=True),
+        lambda x: x,
+        pieces,
+    )
 
     own, *roots = lax.optimization_barrier((own, *roots))
     left = local(unpack_kernel, shape((order // 2, order), BF16), (spot, *roots), limit=4, moved=2 * MIB)
@@ -224,10 +229,16 @@
         scratch=[pltpu.VMEM((order // 2, order), BF16)] * 2,
         flops=2 * order * order * order, limit=11, moved=4 * MIB,
     )
-    update, adam = lax.optimization_barrier((update, adam))
-    back = local(graft_kernel, shape(cut, BF16), (spot, update, norm, norm2, products[0]), limit=5, moved=2 * MIB)
-    products = [lax.ppermute(products[m], AXES, matching(m, True)) for m in range(chips)]
-    returned = lax.all_to_all(back.reshape(devices, piece_rows, half), AXES, split_axis=0, concat_axis=0, tiled=True)
+    update, *products = lax.optimization_barrier((update, *products))
+    back = local(graft_kernel, shape(cut, BF16), (spot, update, norm, norm2), limit=5, moved=2 * MIB)
+
+    def home(x, parts):
+        parts = [lax.ppermute(part, AXES, matching(m, True)) for m, part in enumerate(parts)]
+        return lax.all_to_all(x, AXES, split_axis=0, concat_axis=0, tiled=True), parts
+
+    returned, products = lax.cond(
+        block_slot[0] >= 0, home, lambda x, parts: (x, parts), back.reshape(devices, piece_rows, half), products
+    )
 
     whole = pl.BlockSpec((2 * half, order), lambda m, s: (0, 0))
     piece = pl.BlockSpec((1, half, order), lambda m, s: ((s[0] ^ m) & 1, (s[0] ^ m) >> 1, 0))

time: 208 us -> 152 us (0.73)
  waiting for transfers between devices: 112 us -> 34.3 us
  blocking collectives: 0 us -> 43.3 us
  starting transfers between devices: 46.4 us -> 25.3 us
  local copies, waits for them, and re-layouts: 15.9 us -> 11.2 us
  Pallas kernels: 19.1 us -> 23.5 us
    all_gather x1, waiting for transfers between devices: 48.5 us -> 0.01 us  [body(): adam = lax.all_gather(sent, AXES, axis=0, tiled=True)]
    all_to_all x0 -> x1, blocking collectives: none -> 43.3 us  [body(): lax.all_to_all(x, AXES, split_axis=0, concat_axis=0, tiled=True)]
    ppermute x4, waiting for transfers between devices: 28.8 us -> 0.01 us  [body(): lax.ppermute(packed[m], AXES, matching(m, False))]
    all_to_all x2 -> x1, starting transfers between devices: 26.1 us -> 6.59 us  [home(): lax.all_to_all(x, AXES, split_axis=0, concat_axis=0, tiled=True)]
    unnamed x46 -> x20, local copies, waits for them, and re-layouts: 15.9 us -> 5.79 us
    cond x0 -> x7, local copies, waits for them, and re-layouts: none -> 5.37 us
    pallas_call x8, Pallas kernels: 16 us -> 18.9 us  [local(): pl.pallas_call(kernel, out_shape=outs, in_specs=[SMEM] + [VMEM] * (len(in...]
    ppermute x1, starting transfers between devices: 2.64 us -> 0.09 us  [body(): left2 = lax.ppermute(left, 'fsdp', swap)]
  transfers between devices with their start and end apart: 14 -> 13, of which waited for: 10 -> 4; matrix products, arithmetic and copies ran while one was open for 0% -> 3% of each run, Pallas kernels for 6% -> 11%
where the time goes in v5:
time: 152 us
  blocking collectives  43.3 us (28%)
  waiting for transfers between devices  34.3 us (23%)
  starting transfers between devices  25.3 us (17%)
  Pallas kernels  23.5 us (15%)
  between operations  14.2 us (9%)
  local copies, waits for them, and re-layouts  11.2 us (7%)
    all_to_all x1, blocking collectives, body(): lax.all_to_all(x, AXES, split_axis=0, concat_axis=0, tiled=True)  43.3 us
    ppermute x4, waiting for transfers between devices, home(): lax.ppermute(part, AXES, matching(m, True))  30.6 us
    pallas_call x8, Pallas kernels, local(): pl.pallas_call(kernel, out_shape=outs, in_specs=[SMEM] + [VMEM] * (len(in...  18.9 us
    ppermute x4, starting transfers between devices, body(): lax.ppermute(packed[m], AXES, matching(m, False))  9.38 us
    ppermute x4, starting transfers between devices, home(): lax.ppermute(part, AXES, matching(m, True))  8.95 us
    all_to_all x1, starting transfers between devices, home(): lax.all_to_all(x, AXES, split_axis=0, concat_axis=0, tiled=True)  6.59 us
    unnamed x20, local copies, waits for them, and re-layouts  5.79 us
    cond x7, local copies, waits for them, and re-layouts  5.37 us
  transfers between devices with their start and end apart: 13, of which 4 were waited for; matrix products, arithmetic and copies ran while one was open for 3% of the time, Pallas kernels for 11%

profile of v5, /device:TPU:1, one launch (start us, length us, event | category | flops | bytes accessed | tf_op | source)
XLA Modules:
  0.0 151.8 jit_solution(7801634329104531843)
XLA Ops:
  7.3 1.3 copy-done.3
  8.6 1.2 copy-done.4
  9.8 1.9 %shard_map.103 = (bf16[256,1024]{1,0:T(8,128)(2,1)S(1)}, bf16[256,1024]{1,0:T(8,128)(2,1)}, bf16[256,1024]{1,0:T(8,128)(2,1)}, bf16[256,1024]{1,0:T(8,128)(2,1)S(1)}) custom-call(s32[3]{0:T(128)S(1)} %pad_add_fusion.spot_ref, bf16[2,256,1024]{2,1,0:T(8,128)(2,1)S(1)} %copy-done.3, bf16[2,1024,256]{2,1,0:T(8,128)(2,1)S(1)} %copy-done.4), custom_call_target="tpu_custom_call" | custom-call | bytes 4194304 | tf_op jit(solution)/shard_map/pallas_call | solution.py:17
  11.7 2.1 %shard_map.109 = (f32[8,16,8,256]{3,2,1,0:T(8,128)}, f32[8,128]{1,0:T(8,128)}) custom-call(s32[64]{0:T(128)S(1)} %copy-done.7, bf16[8,16,8,256]{3,2,1,0:T(8,128)(2,1)S(1)} %copy-done.2, f32[8,16,8,256]{3,2,1,0:T(8,128)S(1)} %copy-done.5, bf16[256,1024]{1,0:T(8,128)(2,1)S(1)} %get-tuple-element.64.after_ref), custom_call_target="tpu_custom_call" | custom-call | bytes 2621440 | tf_op jit(solution)/shard_map/pallas_call | solution.py:17
  13.8 6.2 %collective-permute-start.4 = (bf16[256,1024]{1,0:T(8,128)(2,1)S(1)}, bf16[256,1024]{1,0:T(8,128)(2,1)S(1)}, u32[]{:S(2)}, u32[]{:S(2)}) collective-permute-start(bf16[256,1024]{1,0:T(8,128)(2,1)S(1)} %get-tuple-element.64.after_ref), channel_id=1, source_target_pairs={{0,0},{1,1},{2,4},{3,5},{4,2},{5,3},{6,6},{7,7},{8,8},{9,9},{10,12... | collective-permute-start | bytes 1572872 | tf_op jit(solution)/shard_map/ppermute | solution.py:192
  20.6 2.6 %collective-permute-start.7 = (bf16[256,1024]{1,0:T(8,128)(2,1)}, bf16[256,1024]{1,0:T(8,128)(2,1)S(1)}, u32[]{:S(2)}, u32[]{:S(2)}) collective-permute-start(bf16[256,1024]{1,0:T(8,128)(2,1)} %copy-done.8), channel_id=1, source_target_pairs={{0,5},{1,4},{2,1},{3,0},{4,7},{5,6},{6,3},{7,2},{8,13},{9,12},{10,... | collective-permute-start | bytes 1572872 | tf_op jit(solution)/shard_map/ppermute | solution.py:192
  23.2 1.9 %shard_map.102 = bf16[256,16,128]{2,1,0:T(8,128)(2,1)} custom-call(s32[64]{0:T(128)S(1)} %copy-done.7, bf16[8,16,8,256]{3,2,1,0:T(8,128)(2,1)S(1)} %copy-done.2), custom_call_target="tpu_custom_call" | custom-call | bytes 1572864 | tf_op jit(solution)/shard_map/pallas_call | solution.py:17
  25.1 44.5 %conditional.2 = (bf16[256,16,128]{2,1,0:T(8,128)(2,1)}) conditional(s32[]{:T(128)} %bitcast.3, bf16[256,16,128]{2,1,0:T(8,128)(2,1)} %shard_map.102, bf16[256,16,128]{2,1,0:T(8,128)(2,1)} %shard_map.102), branch_computations={%region_0.1_spmd, %region_1.2_spmd} | conditional | bytes 6291492 | solution.py:206
  26.3 43.3 %all_to_all.8 = bf16[256,16,128]{2,1,0:T(8,128)(2,1)} all-to-all(bf16[256,16,128]{2,1,0:T(8,128)(2,1)S(1)} %copy-done.10), channel_id=1, replica_groups=mesh['fsdp'=64,'dp'=4] {'fsdp','dp'}, dimensions={0} | all-to-all | bytes 2097152 | tf_op jit(solution)/shard_map/cond/branch_1_fun/all_to_all | solution.py:208
  70.9 2.1 %collective-permute-done.9.left2_ref = bf16[512,1024]{1,0:T(8,128)(2,1)S(1)} collective-permute-done((bf16[512,1024]{1,0:T(8,128)(2,1)S(1)}, bf16[512,1024]{1,0:T(8,128)(2,1)S(1)}, u32[]{:S(2)}, u32[]{:S(2)}) %collective-permute-start.9) | collective-permute-done | bytes 1048608 | tf_op jit(solution)/shard_map/ppermute | solution.py:215
  73.0 1.5 collective-permute-done.8
  74.5 3.9 %shard_map.105 = (bf16[1024,1024]{1,0:T(8,128)(2,1)S(1)}, bf16[64,4,16,128]{3,2,1,0:T(8,128)(2,1)S(1)}, f32[8,128]{1,0:T(8,128)S(1)}) custom-call(s32[3]{0:T(128)S(1)} %pad_add_fusion.spot_ref, bf16[64,4,16,128]{3,2,1,0:T(8,128)(2,1)S(1)} %bitcast.10, bf16[64,4,16,128]{3,2,1,0:T(8,128)(2,1)S(1)} %bitcast.9, bf16[512,1024]{1,0:T(8,128)(2,1)S(1)} %shard_map.104.left_ref, ...), custom_call_target="tpu_custom_call" | custom-call | flops 2147483648 | bytes 8388608 | tf_op jit(solution)/shard_map/pallas_call | solution.py:17
  78.6 4.2 %shard_map.106 = (bf16[256,1024]{1,0:T(8,128)(2,1)}, bf16[256,1024]{1,0:T(8,128)(2,1)}, bf16[256,1024]{1,0:T(8,128)(2,1)}, bf16[256,1024]{1,0:T(8,128)(2,1)}) custom-call(s32[3]{0:T(128)S(1)} %pad_add_fusion.spot_ref, bf16[1024,1024]{1,0:T(8,128)(2,1)S(1)} %get-tuple-element.74.grad), custom_call_target="tpu_custom_call" | custom-call | flops 2147483648 | bytes 4194304 | tf_op jit(solution)/shard_map/pallas_call | solution.py:17
  82.8 1.7 %shard_map.107 = bf16[64,4,16,128]{3,2,1,0:T(8,128)(2,1)} custom-call(s32[3]{0:T(128)S(1)} %pad_add_fusion.spot_ref, bf16[64,4,16,128]{3,2,1,0:T(8,128)(2,1)S(1)} %get-tuple-element.79.update_ref, f32[8,128]{1,0:T(8,128)S(1)} %get-tuple-element.80.norm_ref, f32[8,128]{1,0:T(8,128)S(1)} %collective-permute-done.10.norm2_ref), custom_call_target="tpu_custom_call" | custom-call | bytes 2097152 | tf_op jit(solution)/shard_map/pallas_call | solution.py:17
  84.5 50.3 %conditional.3 = ((bf16[256,16,128]{2,1,0:T(8,128)(2,1)}, bf16[256,1024]{1,0:T(8,128)(2,1)}, bf16[256,1024]{1,0:T(8,128)(2,1)}, bf16[256,1024]{1,0:T(8,128)(2,1)}, bf16[256,1024]{1,0:T(8,128)(2,1)})) conditional(s32[]{:T(128)} %bitcast.3, (bf16[256,16,128]{2,1,0:T(8,128)(2,1)}, bf16[256,1024]{1,0:T(8,128)(2,1)}, bf16[256,1024]{1,0:T(8,128)(2,1)}, ...), branch_computations={%region_2.3_spmd, %region_3.4_spmd} | conditional | bytes 17826032 | solution.py:239
  84.5 6.6 %all-to-all-start.1 = ((bf16[256,16,128]{2,1,0:T(8,128)(2,1)}), bf16[256,16,128]{2,1,0:T(8,128)(2,1)S(1)}, u32[]{:S(2)}, u32[]{:S(2)}) async-start(bf16[256,16,128]{2,1,0:T(8,128)(2,1)} %get-tuple-element.25), calls=%async_computation.1 | async-start | bytes 2097152 | tf_op jit(solution)/shard_map/cond/branch_1_fun/all_to_all | solution.py:237
  91.1 5.1 %collective-permute-start = (bf16[256,1024]{1,0:T(8,128)(2,1)}, bf16[256,1024]{1,0:T(8,128)(2,1)S(1)}, u32[]{:S(2)}, u32[]{:S(2)}) collective-permute-start(bf16[256,1024]{1,0:T(8,128)(2,1)} %get-tuple-element.26), channel_id=1, source_target_pairs={{0,0},{1,1},{4,2},{5,3},{2,4},{3,5},{6,6},{7,7},{8,8},{9,9},{12,10... | collective-permute-start | bytes 1572872 | tf_op jit(solution)/shard_map/cond/branch_1_fun/ppermute | solution.py:236
  97.2 2.9 %collective-permute-start.3 = (bf16[256,1024]{1,0:T(8,128)(2,1)}, bf16[256,1024]{1,0:T(8,128)(2,1)S(1)}, u32[]{:S(2)}, u32[]{:S(2)}) collective-permute-start(bf16[256,1024]{1,0:T(8,128)(2,1)} %get-tuple-element.29), channel_id=1, source_target_pairs={{5,0},{4,1},{1,2},{0,3},{7,4},{6,5},{3,6},{2,7},{13,8},{12,9},{9,1... | collective-permute-start | bytes 1572872 | tf_op jit(solution)/shard_map/cond/branch_1_fun/ppermute | solution.py:236
  100.1 17.9 %collective-permute-done = bf16[256,1024]{1,0:T(8,128)(2,1)S(1)} collective-permute-done((bf16[256,1024]{1,0:T(8,128)(2,1)}, bf16[256,1024]{1,0:T(8,128)(2,1)S(1)}, u32[]{:S(2)}, u32[]{:S(2)}) %collective-permute-start) | collective-permute-done | bytes 524320 | tf_op jit(solution)/shard_map/cond/branch_1_fun/ppermute | solution.py:236
  118.8 12.7 %collective-permute-done.1 = bf16[256,1024]{1,0:T(8,128)(2,1)S(1)} collective-permute-done((bf16[256,1024]{1,0:T(8,128)(2,1)}, bf16[256,1024]{1,0:T(8,128)(2,1)S(1)}, u32[]{:S(2)}, u32[]{:S(2)}) %collective-permute-start.1) | collective-permute-done | bytes 524320 | tf_op jit(solution)/shard_map/cond/branch_1_fun/ppermute | solution.py:236
  134.8 1.6 %copy-done.1 = f32[2,256,1024]{2,1,0:T(8,128)S(1)} copy-done((f32[2,256,1024]{2,1,0:T(8,128)S(1)}, f32[2,256,1024]{2,1,0:T(8,128)}, u32[]{:S(2)}) %copy-start.1) | copy-done | bytes 2097176
  136.4 4.6 %shard_map.108 = (f32[2,256,1024]{2,1,0:T(8,128)}, f32[2,256,1024]{2,1,0:T(8,128)}) custom-call(s32[3]{0:T(128)S(1)} %pad_add_fusion.spot_ref, bf16[256,1024]{1,0:T(8,128)(2,1)} %get-tuple-element.85.p0, bf16[256,1024]{1,0:T(8,128)(2,1)} %get-tuple-element.86.p1, bf16[256,1024]{1,0:T(8,128)(2,1)} %get-tuple-element.87.p2, ...), custom_call_target="tpu_custom_call" | custom-call | bytes 10485760 | tf_op jit(solution)/shard_map/pallas_call | solution.py:245
  141.1 1.2 copy-done.6
  142.3 2.6 %shard_map.110 = bf16[8,16,8,256]{3,2,1,0:T(8,128)(2,1)} custom-call(s32[64]{0:T(128)S(1)} %copy-done.7, bf16[256,16,128]{2,1,0:T(8,128)(2,1)} %get-tuple-element.92.values_ref, f32[2048,128]{1,0:T(8,128)S(1)} %copy-done.6), custom_call_target="tpu_custom_call" | custom-call | bytes 2097152 | tf_op jit(solution)/shard_map/pallas_call | solution.py:17
  (43 shorter events, 8.5 us)
Async XLA Ops:
  7.2 4.5 %copy-start.2 = (bf16[8,16,8,256]{3,2,1,0:T(8,128)(2,1)S(1)}, bf16[8,16,8,256]{3,2,1,0:T(8,128)(2,1)}, u32[]{:S(2)}) copy-start(bf16[8,16,8,256]{3,2,1,0:T(8,128)(2,1)} %grad_ref.3) | copy-start | bytes 1572868
  7.2 133.9 %all-gather.2.cloned.1.call-start = ((), (), s32[]{:S(2)}) async-start(), calls=%async_computation.2 | async-start | bytes 1052672 | tf_op jit(solution)/shard_map/all_gather | solution.py:200
  7.3 1.3 copy-start.3
  8.6 1.2 copy-start.4
  9.8 1.9 %copy-start.5 = (f32[8,16,8,256]{3,2,1,0:T(8,128)S(1)}, f32[8,16,8,256]{3,2,1,0:T(8,128)}, u32[]{:S(2)}) copy-start(f32[8,16,8,256]{3,2,1,0:T(8,128)} %second_ref.1) | copy-start | bytes 3145732
  9.8 1.9 %copy-start.7 = (s32[64]{0:T(128)S(1)}, s32[64]{0:T(128)}, u32[]{:S(2)}) copy-start(s32[64]{0:T(128)} %slot_ref.5) | copy-start | bytes 772
  11.7 2.1 %copy-start.8 = (bf16[256,1024]{1,0:T(8,128)(2,1)}, bf16[256,1024]{1,0:T(8,128)(2,1)S(1)}, u32[]{:S(2)}) copy-start(bf16[256,1024]{1,0:T(8,128)(2,1)S(1)} %get-tuple-element.67) | copy-start | bytes 1572868
  13.8 55.9 %collective-permute-start.4 = (bf16[256,1024]{1,0:T(8,128)(2,1)S(1)}, bf16[256,1024]{1,0:T(8,128)(2,1)S(1)}, u32[]{:S(2)}, u32[]{:S(2)}) collective-permute-start(bf16[256,1024]{1,0:T(8,128)(2,1)S(1)} %get-tuple-element.64.after_ref), channel_id=1, source_target_pairs={{0,0},{1,1},{2,4},{3,5},{4,2},{5,3},{6,6},{7,7},{8,8},{9,9},{10,12... | collective-permute-start | bytes 1572872 | tf_op jit(solution)/shard_map/ppermute | solution.py:192
  20.0 49.6 %collective-permute-start.5 = (bf16[256,1024]{1,0:T(8,128)(2,1)}, bf16[256,1024]{1,0:T(8,128)(2,1)S(1)}, u32[]{:S(2)}, u32[]{:S(2)}) collective-permute-start(bf16[256,1024]{1,0:T(8,128)(2,1)} %get-tuple-element.65), channel_id=1, source_target_pairs={{0,1},{1,0},{2,5},{3,4},{4,3},{5,2},{6,7},{7,6},{8,9},{9,8},{10,13... | collective-permute-start | bytes 1572872 | tf_op jit(solution)/shard_map/ppermute | solution.py:192
  20.6 49.1 %collective-permute-start.6 = (bf16[256,1024]{1,0:T(8,128)(2,1)}, bf16[256,1024]{1,0:T(8,128)(2,1)S(1)}, u32[]{:S(2)}, u32[]{:S(2)}) collective-permute-start(bf16[256,1024]{1,0:T(8,128)(2,1)} %get-tuple-element.66), channel_id=1, source_target_pairs={{0,4},{1,5},{2,0},{3,1},{4,6},{5,7},{6,2},{7,3},{8,12},{9,13},{10,... | collective-permute-start | bytes 1572872 | tf_op jit(solution)/shard_map/ppermute | solution.py:192
  20.6 49.1 %collective-permute-start.7 = (bf16[256,1024]{1,0:T(8,128)(2,1)}, bf16[256,1024]{1,0:T(8,128)(2,1)S(1)}, u32[]{:S(2)}, u32[]{:S(2)}) collective-permute-start(bf16[256,1024]{1,0:T(8,128)(2,1)} %copy-done.8), channel_id=1, source_target_pairs={{0,5},{1,4},{2,1},{3,0},{4,7},{5,6},{6,3},{7,2},{8,13},{9,12},{10,... | collective-permute-start | bytes 1572872 | tf_op jit(solution)/shard_map/ppermute | solution.py:192
  25.1 1.2 copy-start.10
  69.6 1.2 copy-start.9
  70.3 2.7 %collective-permute-start.9 = (bf16[512,1024]{1,0:T(8,128)(2,1)S(1)}, bf16[512,1024]{1,0:T(8,128)(2,1)S(1)}, u32[]{:S(2)}, u32[]{:S(2)}) collective-permute-start(bf16[512,1024]{1,0:T(8,128)(2,1)S(1)} %shard_map.104.left_ref), channel_id=1, source_target_pairs={{0,4},{4,0},{8,12},{12,8},{16,20},{20,16},{24,28},{28,24},{32,36},... | collective-permute-start | bytes 3145736 | tf_op jit(solution)/shard_map/ppermute | solution.py:215
  70.9 3.7 %collective-permute-start.8 = (bf16[256,16,128]{2,1,0:T(8,128)(2,1)S(1)}, bf16[256,16,128]{2,1,0:T(8,128)(2,1)S(1)}, u32[]{:S(2)}, u32[]{:S(2)}) collective-permute-start(bf16[256,16,128]{2,1,0:T(8,128)(2,1)S(1)} %copy-done.9), channel_id=1, source_target_pairs={{0,4},{4,0},{8,12},{12,8},{16,20},{20,16},{24,28},{28,24},{32,36},... | collective-permute-start | bytes 3145736 | tf_op jit(solution)/shard_map/ppermute | solution.py:216
  78.4 4.3 %collective-permute-start.10 = (f32[8,128]{1,0:T(8,128)S(1)}, f32[8,128]{1,0:T(8,128)S(1)}, u32[]{:S(2)}, u32[]{:S(2)}) collective-permute-start(f32[8,128]{1,0:T(8,128)S(1)} %get-tuple-element.80.norm_ref), channel_id=1, source_target_pairs={{0,4},{4,0},{8,12},{12,8},{16,20},{20,16},{24,28},{28,24},{32,36},... | collective-permute-start | bytes 12296 | tf_op jit(solution)/shard_map/ppermute | solution.py:226
  84.5 50.3 %copy-start = (f32[2,256,1024]{2,1,0:T(8,128)S(1)}, f32[2,256,1024]{2,1,0:T(8,128)}, u32[]{:S(2)}) copy-start(f32[2,256,1024]{2,1,0:T(8,128)} %left_ref.3) | copy-start | bytes 6291460
  84.5 49.4 %all-to-all-start.1 = ((bf16[256,16,128]{2,1,0:T(8,128)(2,1)}), bf16[256,16,128]{2,1,0:T(8,128)(2,1)S(1)}, u32[]{:S(2)}, u32[]{:S(2)}) async-start(bf16[256,16,128]{2,1,0:T(8,128)(2,1)} %get-tuple-element.25), calls=%async_computation.1 | async-start | bytes 2097152 | tf_op jit(solution)/shard_map/cond/branch_1_fun/all_to_all | solution.py:237
  91.1 26.9 %collective-permute-start = (bf16[256,1024]{1,0:T(8,128)(2,1)}, bf16[256,1024]{1,0:T(8,128)(2,1)S(1)}, u32[]{:S(2)}, u32[]{:S(2)}) collective-permute-start(bf16[256,1024]{1,0:T(8,128)(2,1)} %get-tuple-element.26), channel_id=1, source_target_pairs={{0,0},{1,1},{4,2},{5,3},{2,4},{3,5},{6,6},{7,7},{8,8},{9,9},{12,10... | collective-permute-start | bytes 1572872 | tf_op jit(solution)/shard_map/cond/branch_1_fun/ppermute | solution.py:236
  96.1 35.3 %collective-permute-start.1 = (bf16[256,1024]{1,0:T(8,128)(2,1)}, bf16[256,1024]{1,0:T(8,128)(2,1)S(1)}, u32[]{:S(2)}, u32[]{:S(2)}) collective-permute-start(bf16[256,1024]{1,0:T(8,128)(2,1)} %get-tuple-element.27), channel_id=1, source_target_pairs={{1,0},{0,1},{5,2},{4,3},{3,4},{2,5},{7,6},{6,7},{9,8},{8,9},{13,10... | collective-permute-start | bytes 1572872 | tf_op jit(solution)/shard_map/cond/branch_1_fun/ppermute | solution.py:236
  97.2 35.1 %collective-permute-start.2 = (bf16[256,1024]{1,0:T(8,128)(2,1)}, bf16[256,1024]{1,0:T(8,128)(2,1)S(1)}, u32[]{:S(2)}, u32[]{:S(2)}) collective-permute-start(bf16[256,1024]{1,0:T(8,128)(2,1)} %get-tuple-element.28), channel_id=1, source_target_pairs={{4,0},{5,1},{0,2},{1,3},{6,4},{7,5},{2,6},{3,7},{12,8},{13,9},{8,1... | collective-permute-start | bytes 1572872 | tf_op jit(solution)/shard_map/cond/branch_1_fun/ppermute | solution.py:236
  97.2 35.9 %collective-permute-start.3 = (bf16[256,1024]{1,0:T(8,128)(2,1)}, bf16[256,1024]{1,0:T(8,128)(2,1)S(1)}, u32[]{:S(2)}, u32[]{:S(2)}) collective-permute-start(bf16[256,1024]{1,0:T(8,128)(2,1)} %get-tuple-element.29), channel_id=1, source_target_pairs={{5,0},{4,1},{1,2},{0,3},{7,4},{6,5},{3,6},{2,7},{13,8},{12,9},{9,1... | collective-permute-start | bytes 1572872 | tf_op jit(solution)/shard_map/cond/branch_1_fun/ppermute | solution.py:236
  134.8 1.6 %copy-start.1 = (f32[2,256,1024]{2,1,0:T(8,128)S(1)}, f32[2,256,1024]{2,1,0:T(8,128)}, u32[]{:S(2)}) copy-start(f32[2,256,1024]{2,1,0:T(8,128)} %right_ref.3) | copy-start | bytes 6291460
  141.1 1.2 copy-start.6
Sparse Core Ops, SparseCore 0:
  13.9 112.1 all-gather.1

commit v6 on v4

--- a/solution.py
+++ b/solution.py
@@ -1,3 +1,5 @@
+import functools
+
 import jax
 import jax.numpy as jnp
 from jax import lax
@@ -63,15 +65,22 @@
         sent_ref[at + 4] = part[b : b + 1, :]
 
 
-def pack_kernel(spot_ref, left_ref, right_ref, *outs):
+def pack_kernel(spot_ref, left_ref, right_ref, *refs):
+    outs, sems = refs[:-1], refs[-1]
     half = left_ref.shape[1] // 2
     order = left_ref.shape[2]
+    copies = []
     for m, out in enumerate(outs):
         to = spot_ref[0] ^ m
         part = pl.ds(pl.multiple_of((to >> 1) * half, half), half)
-        out[:half, :] = left_ref[to & 1, part, :]
+        copies.append((left_ref.at[to & 1, part], out.at[pl.ds(0, half)]))
         for t in range(0, order, half):
-            out[half:, t : t + half] = right_ref[to & 1, t : t + half, part]
+            copies.append((right_ref.at[to & 1, pl.ds(t, half), part], out.at[pl.ds(half, half), pl.ds(t, half)]))
+    copies = [pltpu.make_async_copy(src, dst, sems.at[i]) for i, (src, dst) in enumerate(copies)]
+    for copy in copies:
+        copy.start()
+    for copy in copies:
+        copy.wait()
 
 
 def unpack_kernel(spot_ref, *refs):
@@ -136,14 +145,13 @@
     out_ref[...] = (update_ref[...].astype(F32) * scale[None, None]).astype(BF16)
 
 
-def stat_kernel(spot_ref, p0, p1, p2, p3, left_ref, right_ref, new_left_ref, new_right_ref):
-    half = left_ref.shape[1]
+def stat_kernel(side, spot_ref, p0, p1, p2, p3, stat_ref, new_ref):
+    half = stat_ref.shape[1]
     for m, ref in enumerate((p0, p1, p2, p3)):
 
         @pl.when(pl.program_id(0) == m)
         def _():
-            new_left_ref[0] = left_ref[0] + ref[:half, :].astype(F32)
-            new_right_ref[0] = right_ref[0] + ref[half:, :].astype(F32)
+            new_ref[0] = stat_ref[0] + ref[side * half : (side + 1) * half, :].astype(F32)
 
 
 def direction_kernel(slot_ref, values_ref, out_ref, wide):
@@ -185,30 +193,39 @@
 
     swap = [(i, i ^ 1) for i in range(owners)]
 
-    packed = local(
-        pack_kernel, [shape((2 * half, order), BF16)] * chips, (spot, root_left, root_right),
-        limit=5, moved=4 * MIB,
-    )
+    packed = pl.pallas_call(
+        pack_kernel,
+        out_shape=[shape((2 * half, order), BF16)] * chips,
+        in_specs=[SMEM] + [pl.BlockSpec(memory_space=pltpu.HBM)] * 2,
+        out_specs=[VMEM] * chips,
+        scratch_shapes=[pltpu.SemaphoreType.DMA((chips * (1 + order // half),))],
+        compiler_params=pltpu.CompilerParams(vmem_limit_bytes=4 * MIB),
+        cost_estimate=pl.CostEstimate(flops=0, bytes_accessed=4 * MIB, transcendentals=0),
+    )(spot, root_left, root_right)
     roots = [lax.ppermute(packed[m], AXES, matching(m, False)) for m in range(chips)]
-
-    new_second, sent = local(
-        moment_kernel,
-        [shape(second_moment.shape, F32), shape((devices, 1, 128), F32)],
-        (block_slot, gradient, second_moment),
-        scratch=[pltpu.VMEM((blocks, 128), F32)], limit=6, moved=MIB * 5 // 2,
-    )
-    adam = lax.all_to_all(sent, AXES, split_axis=0, concat_axis=0, tiled=True)
 
     pieces = local(
         spread_kernel, shape((devices, piece_rows, half), BF16), (block_slot, gradient),
         scratch=[pltpu.VMEM((2 * blocks * piece_rows, half), F32)], limit=6, moved=MIB * 3 // 2,
     )
-    own = lax.cond(
+
+    def spread(x, slots, g, second):
+        x = lax.all_to_all(x, AXES, split_axis=0, concat_axis=0, tiled=True)
+        new, sums = local(
+            moment_kernel,
+            [shape(second.shape, F32), shape((devices, 1, 128), F32)],
+            (slots, g, second),
+            scratch=[pltpu.VMEM((blocks, 128), F32)], limit=6, moved=MIB * 5 // 2,
+        )
+        return x, new, sums
+
+    own, new_second, sent = lax.cond(
         block_slot[0] >= 0,
-        lambda x: lax.all_to_all(x, AXES, split_axis=0, concat_axis=0, tiled=True),
-        lambda x: x,
-        pieces,
-    )
+        spread,
+        lambda x, slots, g, second: (x, second, jnp.zeros((devices, 1, 128), F32)),
+        pieces, block_slot, gradient, second_moment,
+    )
+    adam = lax.all_to_all(sent, AXES, split_axis=0, concat_axis=0, tiled=True)
 
     own, *roots = lax.optimization_barrier((own, *roots))
     left, right = local(
@@ -239,15 +256,18 @@
 
     whole = pl.BlockSpec((2 * half, order), lambda m, s: (0, 0))
     piece = pl.BlockSpec((1, half, order), lambda m, s: ((s[0] ^ m) & 1, (s[0] ^ m) >> 1, 0))
-    new_left, new_right = pl.pallas_call(
-        stat_kernel,
-        out_shape=[shape(stat_left.shape, F32), shape(stat_right.shape, F32)],
-        grid_spec=pltpu.PrefetchScalarGridSpec(
-            num_scalar_prefetch=1, grid=(chips,), in_specs=[whole] * chips + [piece] * 2, out_specs=[piece] * 2
-        ),
-        compiler_params=pltpu.CompilerParams(vmem_limit_bytes=10 * MIB),
-        cost_estimate=pl.CostEstimate(flops=0, bytes_accessed=10 * MIB, transcendentals=0),
-    )(spot, *products, stat_left, stat_right)
+    new_left, new_right = (
+        pl.pallas_call(
+            functools.partial(stat_kernel, side),
+            out_shape=shape(stat.shape, F32),
+            grid_spec=pltpu.PrefetchScalarGridSpec(
+                num_scalar_prefetch=1, grid=(chips,), in_specs=[whole] * chips + [piece], out_specs=piece
+            ),
+            compiler_params=pltpu.CompilerParams(vmem_limit_bytes=8 * MIB),
+            cost_estimate=pl.CostEstimate(flops=0, bytes_accessed=5 * MIB, transcendentals=0),
+        )(spot, *products, stat)
+        for side, stat in enumerate((stat_left, stat_right))
+    )
 
     direction = local(
         direction_kernel, shape(gradient.shape, gradient.dtype), (block_slot, returned),

time: 147 us -> 149 us (1.014)
  blocking collectives: 43.3 us -> 0 us
  waiting for transfers between devices: 30.6 us -> 56.8 us
  starting transfers between devices: 39.5 us -> 53 us
  local copies, waits for them, and re-layouts: 8.8 us -> 13.6 us
    all_to_all x1 -> x0, blocking collectives: 43.3 us -> none  [body(): lax.all_to_all(x, AXES, split_axis=0, concat_axis=0, tiled=True)]
    all_to_all x0 -> x1, waiting for transfers between devices: none -> 26.3 us  [spread(): x = lax.all_to_all(x, AXES, split_axis=0, concat_axis=0, tiled=True)]
    all_to_all x0 -> x1, starting transfers between devices: none -> 13.4 us  [spread(): x = lax.all_to_all(x, AXES, split_axis=0, concat_axis=0, tiled=True)]
    pallas_call x1 -> x3, Pallas kernels: 3.08 us -> 7.15 us  [the longest x2 4.89 us: body(): pl.pallas_call(functools.partial(stat_kernel, side), out_shape=shape(stat...]
    pallas_call x8 -> x7, Pallas kernels: 20.4 us -> 17 us  [local(): pl.pallas_call(kernel, out_shape=outs, in_specs=[SMEM] + [VMEM] * (len(in...]
    unnamed x26 -> x31, local copies, waits for them, and re-layouts: 7.57 us -> 10.3 us
    cond x1 -> x2, local copies, waits for them, and re-layouts: 1.23 us -> 3.34 us
  transfers between devices with their start and end apart: 13 -> 14, of which waited for: 3 -> 4; matrix products, arithmetic and copies ran while one was open for 1% -> 2% of each run, Pallas kernels for 11% -> 12%
where the time goes in v6:
time: 149 us
  waiting for transfers between devices  56.8 us (38%)
  starting transfers between devices  53 us (36%)
  Pallas kernels  24.2 us (16%)
  local copies, waits for them, and re-layouts  13.6 us (9%)
    ppermute x4, waiting for transfers between devices, body(): lax.ppermute(products[m], AXES, matching(m, True))  30.6 us
    all_to_all x1, waiting for transfers between devices, spread(): x = lax.all_to_all(x, AXES, split_axis=0, concat_axis=0, tiled=True)  26.3 us
    pallas_call x7, Pallas kernels, local(): pl.pallas_call(kernel, out_shape=outs, in_specs=[SMEM] + [VMEM] * (len(in...  17 us
    all_to_all x1, starting transfers between devices, spread(): x = lax.all_to_all(x, AXES, split_axis=0, concat_axis=0, tiled=True)  13.4 us
    all_to_all x1, starting transfers between devices, body(): lax.all_to_all(back.reshape(devices, piece_rows, half), AXES, split_axis=...  11.7 us
    unnamed x31, local copies, waits for them, and re-layouts  10.3 us
    ppermute x4, starting transfers between devices, body(): lax.ppermute(packed[m], AXES, matching(m, False))  9.37 us
    ppermute x4, starting transfers between devices, body(): lax.ppermute(products[m], AXES, matching(m, True))  9.08 us
  transfers between devices with their start and end apart: 14, of which 4 were waited for; matrix products, arithmetic and copies ran while one was open for 2% of the time, Pallas kernels for 12%

profile of v6, /device:TPU:1, one launch (start us, length us, event | category | flops | bytes accessed | tf_op | source)
XLA Modules:
  0.0 148.7 jit_solution(13845643381522292967)
XLA Ops:
  0.7 2.4 %copy.18 = f32[8,16,8,256]{3,2,1,0:T(8,128)} copy(f32[8,16,8,256]{3,2,1,0:T(8,128)} %param.10) | data formatting | bytes 2097152
  3.2 2.3 %shard_map.103 = (bf16[256,1024]{1,0:T(8,128)(2,1)}, bf16[256,1024]{1,0:T(8,128)(2,1)}, bf16[256,1024]{1,0:T(8,128)(2,1)S(1)}, bf16[256,1024]{1,0:T(8,128)(2,1)S(1)}) custom-call(s32[3]{0:T(128)S(1)} %pad_add_fusion.spot_ref, bf16[2,256,1024]{2,1,0:T(8,128)(2,1)S(1)} %copy-done.2, bf16[2,1024,256]{2,1,0:T(8,128)(2,1)S(1)} %copy-done.3), custom_call_target="tpu_custom_call" | custom-call | bytes 4194304 | tf_op jit(solution)/shard_map/pallas_call | solution.py:196
  5.4 6.2 %collective-permute-start = (bf16[256,1024]{1,0:T(8,128)(2,1)}, bf16[256,1024]{1,0:T(8,128)(2,1)S(1)}, u32[]{:S(2)}, u32[]{:S(2)}) collective-permute-start(bf16[256,1024]{1,0:T(8,128)(2,1)} %get-tuple-element.51), channel_id=1, source_target_pairs={{0,0},{1,1},{2,4},{3,5},{4,2},{5,3},{6,6},{7,7},{8,8},{9,9},{10,12... | collective-permute-start | bytes 1572872 | tf_op jit(solution)/shard_map/ppermute | solution.py:205
  12.2 2.6 %collective-permute-start.3 = (bf16[256,1024]{1,0:T(8,128)(2,1)S(1)}, bf16[256,1024]{1,0:T(8,128)(2,1)S(1)}, u32[]{:S(2)}, u32[]{:S(2)}) collective-permute-start(bf16[256,1024]{1,0:T(8,128)(2,1)S(1)} %get-tuple-element.54), channel_id=1, source_target_pairs={{0,5},{1,4},{2,1},{3,0},{4,7},{5,6},{6,3},{7,2},{8,13},{9,12},{10,... | collective-permute-start | bytes 1572872 | tf_op jit(solution)/shard_map/ppermute | solution.py:205
  14.8 2.4 %shard_map.102 = bf16[256,16,128]{2,1,0:T(8,128)(2,1)} custom-call(s32[64]{0:T(128)S(1)} %copy-done.14, bf16[8,16,8,256]{3,2,1,0:T(8,128)(2,1)} %grad_ref.1), custom_call_target="tpu_custom_call" | custom-call | bytes 1572864 | tf_op jit(solution)/shard_map/pallas_call | solution.py:19
  17.2 45.9 %conditional.1 = (bf16[256,16,128]{2,1,0:T(8,128)(2,1)}, f32[8,16,8,256]{3,2,1,0:T(8,128)}, f32[256,1,128]{2,1,0:T(1,128)}) conditional(s32[]{:T(128)} %bitcast.3, (bf16[256,16,128]{2,1,0:T(8,128)(2,1)}, f32[8,16,8,256]{3,2,1,0:T(8,128)}) %tuple.18, (bf16[256,16,128]{2,1,0:T(8,128)(2,1)}, s32[64]{0:T(128)S(1)}, bf16[8,16,8,256]{3,2,1,0:T(8,128)(2,1)}, ...), branch_computations={%region_0.1_spmd, %region_1.2_spmd} | conditional | bytes 9961528 | solution.py:222
  17.3 13.4 %all-to-all-start = ((bf16[256,16,128]{2,1,0:T(8,128)(2,1)}), bf16[256,16,128]{2,1,0:T(8,128)(2,1)}, u32[]{:S(2)}, u32[]{:S(2)}) async-start(bf16[256,16,128]{2,1,0:T(8,128)(2,1)} %get-tuple-element.14), calls=%async_computation | async-start | bytes 2097152 | tf_op jit(solution)/shard_map/cond/branch_1_fun/all_to_all | solution.py:213
  30.7 2.8 %branch_1_fun.1 = (f32[8,16,8,256]{3,2,1,0:T(8,128)S(1)}, f32[256,1,128]{2,1,0:T(1,128)}) custom-call(s32[64]{0:T(128)S(1)} %get-tuple-element.15.slot_ref, bf16[8,16,8,256]{3,2,1,0:T(8,128)(2,1)} %get-tuple-element.16.grad_ref, f32[8,16,8,256]{3,2,1,0:T(8,128)} %get-tuple-element.17.second_ref), custom_call_target="tpu_custom_call" | custom-call | bytes 2621440 | tf_op jit(solution)/shard_map/cond/branch_1_fun/pallas_call | solution.py:19
  34.5 26.3 %all-to-all-done = bf16[256,16,128]{2,1,0:T(8,128)(2,1)} async-done(((bf16[256,16,128]{2,1,0:T(8,128)(2,1)}), bf16[256,16,128]{2,1,0:T(8,128)(2,1)}, u32[]{:S(2)}, u32[]{:S(2)}) %all-to-all-start) | async-done | bytes 1048608 | tf_op jit(solution)/shard_map/cond/branch_1_fun/all_to_all | solution.py:213
  60.7 2.4 %copy.14 = bf16[256,16,128]{2,1,0:T(8,128)(2,1)} copy(bf16[256,16,128]{2,1,0:T(8,128)(2,1)} %all-to-all-done) | data formatting | bytes 2097152 | tf_op jit(solution)/shard_map/cond
  65.3 6.6 %all-to-all-start.1 = ((f32[256,1,128]{2,1,0:T(1,128)}), f32[256,1,128]{2,1,0:T(1,128)S(1)}, u32[]{:S(2)}, u32[]{:S(2)}) async-start(f32[256,1,128]{2,1,0:T(1,128)} %get-tuple-element.75), calls=%async_computation.1 | async-start | bytes 262144 | tf_op jit(solution)/shard_map/all_to_all | solution.py:228
  73.9 1.2 copy-done.5
  77.5 4.6 %shard_map.105 = (bf16[1024,1024]{1,0:T(8,128)(2,1)S(1)}, bf16[64,4,16,128]{3,2,1,0:T(8,128)(2,1)S(1)}, f32[8,128]{1,0:T(8,128)S(1)}) custom-call(s32[3]{0:T(128)S(1)} %pad_add_fusion.spot_ref, bf16[64,4,16,128]{3,2,1,0:T(8,128)(2,1)} %bitcast.4.own_ref, bf16[64,4,16,128]{3,2,1,0:T(8,128)(2,1)S(1)} %bitcast.8, ...), custom_call_target="tpu_custom_call" | custom-call | flops 2147483648 | bytes 8388608 | tf_op jit(solution)/shard_map/pallas_call | solution.py:19
  82.1 2.4 %collective-permute-start.10 = (f32[8,128]{1,0:T(8,128)S(1)}, f32[8,128]{1,0:T(8,128)S(1)}, u32[]{:S(2)}, u32[]{:S(2)}) collective-permute-start(f32[8,128]{1,0:T(8,128)S(1)} %get-tuple-element.74.norm_ref), channel_id=1, source_target_pairs={{0,4},{4,0},{8,12},{12,8},{16,20},{20,16},{24,28},{28,24},{32,36},... | collective-permute-start | bytes 12296 | tf_op jit(solution)/shard_map/ppermute | solution.py:246
  84.5 3.0 %shard_map.106 = (bf16[256,1024]{1,0:T(8,128)(2,1)S(1)}, bf16[256,1024]{1,0:T(8,128)(2,1)S(1)}, bf16[256,1024]{1,0:T(8,128)(2,1)S(1)}, bf16[256,1024]{1,0:T(8,128)(2,1)S(1)}) custom-call(s32[3]{0:T(128)S(1)} %pad_add_fusion.spot_ref, bf16[1024,1024]{1,0:T(8,128)(2,1)S(1)} %get-tuple-element.63.grad), custom_call_target="tpu_custom_call" | custom-call | flops 2147483648 | bytes 4194304 | tf_op jit(solution)/shard_map/pallas_call | solution.py:19
  88.8 2.0 %shard_map.109 = bf16[64,4,16,128]{3,2,1,0:T(8,128)(2,1)} custom-call(s32[3]{0:T(128)S(1)} %pad_add_fusion.spot_ref, bf16[64,4,16,128]{3,2,1,0:T(8,128)(2,1)S(1)} %get-tuple-element.73.update_ref, f32[8,128]{1,0:T(8,128)S(1)} %get-tuple-element.74.norm_ref, f32[8,128]{1,0:T(8,128)S(1)} %collective-permute-done.10.norm2_ref, ...), custom_call_target="tpu_custom_call" | custom-call | bytes 2097152 | tf_op jit(solution)/shard_map/pallas_call | solution.py:19
  90.7 11.7 %all-to-all-start.2 = ((bf16[256,16,128]{2,1,0:T(8,128)(2,1)}), bf16[256,16,128]{2,1,0:T(8,128)(2,1)S(1)}, u32[]{:S(2)}, u32[]{:S(2)}) async-start(bf16[256,16,128]{2,1,0:T(8,128)(2,1)} %bitcast.6), calls=%async_computation.2 | async-start | bytes 2097152 | tf_op jit(solution)/shard_map/all_to_all | solution.py:255
  102.5 5.2 %collective-permute-start.6 = (bf16[256,1024]{1,0:T(8,128)(2,1)}, bf16[256,1024]{1,0:T(8,128)(2,1)S(1)}, u32[]{:S(2)}, u32[]{:S(2)}) collective-permute-start(bf16[256,1024]{1,0:T(8,128)(2,1)} %copy-done.13), channel_id=1, source_target_pairs={{0,0},{1,1},{4,2},{5,3},{2,4},{3,5},{6,6},{7,7},{8,8},{9,9},{12,10... | collective-permute-start | bytes 1572872 | tf_op jit(solution)/shard_map/ppermute | solution.py:254
  108.7 2.9 %collective-permute-start.9 = (bf16[256,1024]{1,0:T(8,128)(2,1)}, bf16[256,1024]{1,0:T(8,128)(2,1)S(1)}, u32[]{:S(2)}, u32[]{:S(2)}) collective-permute-start(bf16[256,1024]{1,0:T(8,128)(2,1)} %copy-done.10), channel_id=1, source_target_pairs={{5,0},{4,1},{1,2},{0,3},{7,4},{6,5},{3,6},{2,7},{13,8},{12,9},{9,1... | collective-permute-start | bytes 1572872 | tf_op jit(solution)/shard_map/ppermute | solution.py:254
  111.6 17.3 %collective-permute-done.6.p0 = bf16[256,1024]{1,0:T(8,128)(2,1)S(1)} collective-permute-done((bf16[256,1024]{1,0:T(8,128)(2,1)}, bf16[256,1024]{1,0:T(8,128)(2,1)S(1)}, u32[]{:S(2)}, u32[]{:S(2)}) %collective-permute-start.6) | collective-permute-done | bytes 524320 | tf_op jit(solution)/shard_map/ppermute | solution.py:254
  128.9 13.2 %collective-permute-done.7.p1 = bf16[256,1024]{1,0:T(8,128)(2,1)S(1)} collective-permute-done((bf16[256,1024]{1,0:T(8,128)(2,1)}, bf16[256,1024]{1,0:T(8,128)(2,1)S(1)}, u32[]{:S(2)}, u32[]{:S(2)}) %collective-permute-start.7) | collective-permute-done | bytes 524320 | tf_op jit(solution)/shard_map/ppermute | solution.py:254
  142.1 2.4 %shard_map.108 = f32[2,256,1024]{2,1,0:T(8,128)} custom-call(s32[3]{0:T(128)S(1)} %pad_add_fusion.spot_ref, bf16[256,1024]{1,0:T(8,128)(2,1)S(1)} %collective-permute-done.6.p0, bf16[256,1024]{1,0:T(8,128)(2,1)S(1)} %collective-permute-done.7.p1, bf16[256,1024]{1,0:T(8,128)(2,1)S(1)} %collective-permute-done.8.p2, ...), custom_call_target="tpu_custom_call" | custom-call | bytes 5242880 | tf_op jit(solution)/shard_map/pallas_call | solution.py:260
  144.6 2.4 %shard_map.107 = f32[2,256,1024]{2,1,0:T(8,128)} custom-call(s32[3]{0:T(128)S(1)} %pad_add_fusion.spot_ref, bf16[256,1024]{1,0:T(8,128)(2,1)S(1)} %collective-permute-done.6.p0, bf16[256,1024]{1,0:T(8,128)(2,1)S(1)} %collective-permute-done.7.p1, bf16[256,1024]{1,0:T(8,128)(2,1)S(1)} %collective-permute-done.8.p2, ...), custom_call_target="tpu_custom_call" | custom-call | bytes 5242880 | tf_op jit(solution)/shard_map/pallas_call | solution.py:260
  147.0 1.6 %shard_map.110 = bf16[8,16,8,256]{3,2,1,0:T(8,128)(2,1)} custom-call(s32[64]{0:T(128)S(1)} %copy-done.14, bf16[256,16,128]{2,1,0:T(8,128)(2,1)S(1)} %all-to-all-done.2.values_ref), custom_call_target="tpu_custom_call" | custom-call | bytes 2097152 | tf_op jit(solution)/shard_map/pallas_call | solution.py:19
  (49 shorter events, 10.6 us)
Async XLA Ops:
  0.6 2.5 %copy-start.2 = (bf16[2,256,1024]{2,1,0:T(8,128)(2,1)S(1)}, bf16[2,256,1024]{2,1,0:T(8,128)(2,1)}, u32[]{:S(2)}) copy-start(bf16[2,256,1024]{2,1,0:T(8,128)(2,1)} %left_ref.1) | copy-start | bytes 3145732
  0.6 2.5 %copy-start.3 = (bf16[2,1024,256]{2,1,0:T(8,128)(2,1)S(1)}, bf16[2,1024,256]{2,1,0:T(8,128)(2,1)}, u32[]{:S(2)}) copy-start(bf16[2,1024,256]{2,1,0:T(8,128)(2,1)} %right_ref.1) | copy-start | bytes 3145732
  0.7 14.2 %copy-start.14 = (s32[64]{0:T(128)S(1)}, s32[64]{0:T(128)}, u32[]{:S(2)}) copy-start(s32[64]{0:T(128)} %slot_ref.3) | copy-start | bytes 772
  5.4 57.7 %collective-permute-start = (bf16[256,1024]{1,0:T(8,128)(2,1)}, bf16[256,1024]{1,0:T(8,128)(2,1)S(1)}, u32[]{:S(2)}, u32[]{:S(2)}) collective-permute-start(bf16[256,1024]{1,0:T(8,128)(2,1)} %get-tuple-element.51), channel_id=1, source_target_pairs={{0,0},{1,1},{2,4},{3,5},{4,2},{5,3},{6,6},{7,7},{8,8},{9,9},{10,12... | collective-permute-start | bytes 1572872 | tf_op jit(solution)/shard_map/ppermute | solution.py:205
  11.6 51.5 %collective-permute-start.1 = (bf16[256,1024]{1,0:T(8,128)(2,1)}, bf16[256,1024]{1,0:T(8,128)(2,1)S(1)}, u32[]{:S(2)}, u32[]{:S(2)}) collective-permute-start(bf16[256,1024]{1,0:T(8,128)(2,1)} %get-tuple-element.52), channel_id=1, source_target_pairs={{0,1},{1,0},{2,5},{3,4},{4,3},{5,2},{6,7},{7,6},{8,9},{9,8},{10,13... | collective-permute-start | bytes 1572872 | tf_op jit(solution)/shard_map/ppermute | solution.py:205
  12.2 50.9 %collective-permute-start.2 = (bf16[256,1024]{1,0:T(8,128)(2,1)S(1)}, bf16[256,1024]{1,0:T(8,128)(2,1)S(1)}, u32[]{:S(2)}, u32[]{:S(2)}) collective-permute-start(bf16[256,1024]{1,0:T(8,128)(2,1)S(1)} %get-tuple-element.53), channel_id=1, source_target_pairs={{0,4},{1,5},{2,0},{3,1},{4,6},{5,7},{6,2},{7,3},{8,12},{9,13},{10,... | collective-permute-start | bytes 1572872 | tf_op jit(solution)/shard_map/ppermute | solution.py:205
  12.2 50.9 %collective-permute-start.3 = (bf16[256,1024]{1,0:T(8,128)(2,1)S(1)}, bf16[256,1024]{1,0:T(8,128)(2,1)S(1)}, u32[]{:S(2)}, u32[]{:S(2)}) collective-permute-start(bf16[256,1024]{1,0:T(8,128)(2,1)S(1)} %get-tuple-element.54), channel_id=1, source_target_pairs={{0,5},{1,4},{2,1},{3,0},{4,7},{5,6},{6,3},{7,2},{8,13},{9,12},{10,... | collective-permute-start | bytes 1572872 | tf_op jit(solution)/shard_map/ppermute | solution.py:205
  17.3 43.5 %all-to-all-start = ((bf16[256,16,128]{2,1,0:T(8,128)(2,1)}), bf16[256,16,128]{2,1,0:T(8,128)(2,1)}, u32[]{:S(2)}, u32[]{:S(2)}) async-start(bf16[256,16,128]{2,1,0:T(8,128)(2,1)} %get-tuple-element.14), calls=%async_computation | async-start | bytes 2097152 | tf_op jit(solution)/shard_map/cond/branch_1_fun/all_to_all | solution.py:213
  64.8 7.1 %collective-permute-start.5 = (bf16[512,1024]{1,0:T(8,128)(2,1)S(1)}, bf16[512,1024]{1,0:T(8,128)(2,1)S(1)}, u32[]{:S(2)}, u32[]{:S(2)}) collective-permute-start(bf16[512,1024]{1,0:T(8,128)(2,1)S(1)} %get-tuple-element.60.left_ref), channel_id=1, source_target_pairs={{0,4},{4,0},{8,12},{12,8},{16,20},{20,16},{24,28},{28,24},{32,36},... | collective-permute-start | bytes 3145736 | tf_op jit(solution)/shard_map/ppermute | solution.py:235
  64.8 8.1 %collective-permute-start.4 = (bf16[256,16,128]{2,1,0:T(8,128)(2,1)}, bf16[256,16,128]{2,1,0:T(8,128)(2,1)S(1)}, u32[]{:S(2)}, u32[]{:S(2)}) collective-permute-start(bf16[256,16,128]{2,1,0:T(8,128)(2,1)} %get-tuple-element.55), channel_id=1, source_target_pairs={{0,4},{4,0},{8,12},{12,8},{16,20},{20,16},{24,28},{28,24},{32,36},... | collective-permute-start | bytes 3145736 | tf_op jit(solution)/shard_map/ppermute | solution.py:236
  65.3 23.4 %all-to-all-start.1 = ((f32[256,1,128]{2,1,0:T(1,128)}), f32[256,1,128]{2,1,0:T(1,128)S(1)}, u32[]{:S(2)}, u32[]{:S(2)}) async-start(f32[256,1,128]{2,1,0:T(1,128)} %get-tuple-element.75), calls=%async_computation.1 | async-start | bytes 262144 | tf_op jit(solution)/shard_map/all_to_all | solution.py:228
  73.9 1.2 copy-start.5
  75.1 1.2 copy-start.7
  76.3 1.2 copy-start.9
  82.1 6.6 %collective-permute-start.10 = (f32[8,128]{1,0:T(8,128)S(1)}, f32[8,128]{1,0:T(8,128)S(1)}, u32[]{:S(2)}, u32[]{:S(2)}) collective-permute-start(f32[8,128]{1,0:T(8,128)S(1)} %get-tuple-element.74.norm_ref), channel_id=1, source_target_pairs={{0,4},{4,0},{8,12},{12,8},{16,20},{20,16},{24,28},{28,24},{32,36},... | collective-permute-start | bytes 12296 | tf_op jit(solution)/shard_map/ppermute | solution.py:246
  87.5 1.1 copy-start.12
  87.5 1.3 copy-start.13
  88.8 53.4 %copy-start = (f32[2,256,1024]{2,1,0:T(8,128)S(1)}, f32[2,256,1024]{2,1,0:T(8,128)}, u32[]{:S(2)}) copy-start(f32[2,256,1024]{2,1,0:T(8,128)} %stat_ref.3) | copy-start | bytes 6291460
  90.7 56.3 %all-to-all-start.2 = ((bf16[256,16,128]{2,1,0:T(8,128)(2,1)}), bf16[256,16,128]{2,1,0:T(8,128)(2,1)S(1)}, u32[]{:S(2)}, u32[]{:S(2)}) async-start(bf16[256,16,128]{2,1,0:T(8,128)(2,1)} %bitcast.6), calls=%async_computation.2 | async-start | bytes 2097152 | tf_op jit(solution)/shard_map/all_to_all | solution.py:255
  102.5 42.1 %copy-start.1 = (f32[2,256,1024]{2,1,0:T(8,128)S(1)}, f32[2,256,1024]{2,1,0:T(8,128)}, u32[]{:S(2)}) copy-start(f32[2,256,1024]{2,1,0:T(8,128)} %stat_ref.2) | copy-start | bytes 6291460
  102.5 26.4 %collective-permute-start.6 = (bf16[256,1024]{1,0:T(8,128)(2,1)}, bf16[256,1024]{1,0:T(8,128)(2,1)S(1)}, u32[]{:S(2)}, u32[]{:S(2)}) collective-permute-start(bf16[256,1024]{1,0:T(8,128)(2,1)} %copy-done.13), channel_id=1, source_target_pairs={{0,0},{1,1},{4,2},{5,3},{2,4},{3,5},{6,6},{7,7},{8,8},{9,9},{12,10... | collective-permute-start | bytes 1572872 | tf_op jit(solution)/shard_map/ppermute | solution.py:254
  107.7 34.4 %collective-permute-start.7 = (bf16[256,1024]{1,0:T(8,128)(2,1)}, bf16[256,1024]{1,0:T(8,128)(2,1)S(1)}, u32[]{:S(2)}, u32[]{:S(2)}) collective-permute-start(bf16[256,1024]{1,0:T(8,128)(2,1)} %copy-done.12), channel_id=1, source_target_pairs={{1,0},{0,1},{5,2},{4,3},{3,4},{2,5},{7,6},{6,7},{9,8},{8,9},{13,10... | collective-permute-start | bytes 1572872 | tf_op jit(solution)/shard_map/ppermute | solution.py:254
  108.7 33.4 %collective-permute-start.8 = (bf16[256,1024]{1,0:T(8,128)(2,1)}, bf16[256,1024]{1,0:T(8,128)(2,1)S(1)}, u32[]{:S(2)}, u32[]{:S(2)}) collective-permute-start(bf16[256,1024]{1,0:T(8,128)(2,1)} %copy-done.11), channel_id=1, source_target_pairs={{4,0},{5,1},{0,2},{1,3},{6,4},{7,5},{2,6},{3,7},{12,8},{13,9},{8,1... | collective-permute-start | bytes 1572872 | tf_op jit(solution)/shard_map/ppermute | solution.py:254
  108.7 33.4 %collective-permute-start.9 = (bf16[256,1024]{1,0:T(8,128)(2,1)}, bf16[256,1024]{1,0:T(8,128)(2,1)S(1)}, u32[]{:S(2)}, u32[]{:S(2)}) collective-permute-start(bf16[256,1024]{1,0:T(8,128)(2,1)} %copy-done.10), channel_id=1, source_target_pairs={{5,0},{4,1},{1,2},{0,3},{7,4},{6,5},{3,6},{2,7},{13,8},{12,9},{9,1... | collective-permute-start | bytes 1572872 | tf_op jit(solution)/shard_map/ppermute | solution.py:254
  (5 other events, 4.7 us)

commit v7 on v4

--- a/solution.py
+++ b/solution.py
@@ -57,21 +57,31 @@
         adam = g / (jnp.sqrt(new) + 1e-08)
         sums = jnp.sum(jnp.sum(adam * adam, axis=0), axis=1, keepdims=True)
         part[r * column_blocks : (r + 1) * column_blocks, :] = jnp.broadcast_to(sums, (column_blocks, 128))
+    owner = lax.broadcasted_iota(jnp.int32, (1, 128), 1) >> 5
     for b in range(row_blocks * column_blocks):
-        at = spread_row(slot_ref[b])
-        sent_ref[at] = part[b : b + 1, :]
-        sent_ref[at + 4] = part[b : b + 1, :]
-
-
-def pack_kernel(spot_ref, left_ref, right_ref, *outs):
+        slot = slot_ref[b]
+        at = (slot >> 2) * 2
+        row = sent_ref[at] + jnp.where(owner == (slot & 3), part[b : b + 1, :], 0.0)
+        sent_ref[at] = row
+        sent_ref[at + 1] = row
+
+
+def pack_kernel(spot_ref, left_ref, right_ref, *refs):
+    outs, sems = refs[:-1], refs[-1]
     half = left_ref.shape[1] // 2
     order = left_ref.shape[2]
+    copies = []
     for m, out in enumerate(outs):
         to = spot_ref[0] ^ m
         part = pl.ds(pl.multiple_of((to >> 1) * half, half), half)
-        out[:half, :] = left_ref[to & 1, part, :]
+        copies.append((left_ref.at[to & 1, part], out.at[pl.ds(0, half)]))
         for t in range(0, order, half):
-            out[half:, t : t + half] = right_ref[to & 1, t : t + half, part]
+            copies.append((right_ref.at[to & 1, pl.ds(t, half), part], out.at[pl.ds(half, half), pl.ds(t, half)]))
+    copies = [pltpu.make_async_copy(src, dst, sems.at[i]) for i, (src, dst) in enumerate(copies)]
+    for copy in copies:
+        copy.start()
+    for copy in copies:
+        copy.wait()
 
 
 def unpack_kernel(spot_ref, *refs):
@@ -130,8 +140,10 @@
             out[half:, n : n + 256] = right[m * half : (m + 1) * half].astype(BF16)
 
 
-def graft_kernel(spot_ref, update_ref, norm_ref, norm2_ref, adam_ref, out_ref):
-    adam = jnp.sum(adam_ref[...], axis=0)
+def graft_kernel(spot_ref, update_ref, norm_ref, norm2_ref, adam0, adam1, adam2, adam3, out_ref):
+    adam = adam0[...] + adam1[...] + adam2[...] + adam3[...]
+    owner = lax.broadcasted_iota(jnp.int32, (1, 128), 1) >> 5
+    adam = jnp.max(jnp.where(owner == spot_ref[0], adam, 0.0), axis=1, keepdims=True)
     scale = jnp.sqrt(adam / (norm_ref[0:1, :] + norm2_ref[0:1, :] + 1e-06))
     out_ref[...] = (update_ref[...].astype(F32) * scale[None, None]).astype(BF16)
 
@@ -185,19 +197,24 @@
 
     swap = [(i, i ^ 1) for i in range(owners)]
 
-    packed = local(
-        pack_kernel, [shape((2 * half, order), BF16)] * chips, (spot, root_left, root_right),
-        limit=5, moved=4 * MIB,
-    )
+    packed = pl.pallas_call(
+        pack_kernel,
+        out_shape=[shape((2 * half, order), BF16)] * chips,
+        in_specs=[SMEM] + [pl.BlockSpec(memory_space=pl.ANY)] * 2,
+        out_specs=[VMEM] * chips,
+        scratch_shapes=[pltpu.SemaphoreType.DMA((chips * (1 + order // half),))],
+        compiler_params=pltpu.CompilerParams(vmem_limit_bytes=4 * MIB),
+        cost_estimate=pl.CostEstimate(flops=0, bytes_accessed=4 * MIB, transcendentals=0),
+    )(spot, root_left, root_right)
     roots = [lax.ppermute(packed[m], AXES, matching(m, False)) for m in range(chips)]
 
     new_second, sent = local(
         moment_kernel,
-        [shape(second_moment.shape, F32), shape((devices, 1, 128), F32)],
+        [shape(second_moment.shape, F32), shape((owners, 1, 128), F32)],
         (block_slot, gradient, second_moment),
         scratch=[pltpu.VMEM((blocks, 128), F32)], limit=6, moved=MIB * 5 // 2,
     )
-    adam = lax.all_to_all(sent, AXES, split_axis=0, concat_axis=0, tiled=True)
+    adam = lax.all_to_all(sent, "fsdp", split_axis=0, concat_axis=0, tiled=True)
 
     pieces = local(
         spread_kernel, shape((devices, piece_rows, half), BF16), (block_slot, gradient),
@@ -226,14 +243,17 @@
         scratch=[pltpu.VMEM((order, order // 2), BF16)] * 2,
         flops=2 * order * order * order, limit=18, moved=8 * MIB,
     )
+    norm, adam = lax.optimization_barrier((norm, adam))
     norm2 = lax.ppermute(norm, "fsdp", swap)
+    adam = adam.sum(axis=0)
+    adams = [adam] + [lax.ppermute(adam, "dp", [(i, (i + k) % chips) for i in range(chips)]) for k in range(1, chips)]
     products = local(
         product_kernel, [shape((2 * half, order), BF16)] * chips, (spot, grad),
         scratch=[pltpu.VMEM((order // 2, order), BF16)] * 2,
         flops=2 * order * order * order, limit=11, moved=4 * MIB,
     )
     update, *products = lax.optimization_barrier((update, *products))
-    back = local(graft_kernel, shape(cut, BF16), (spot, update, norm, norm2, adam), limit=5, moved=2 * MIB)
+    back = local(graft_kernel, shape(cut, BF16), (spot, update, norm, norm2, *adams), limit=5, moved=2 * MIB)
     products = [lax.ppermute(products[m], AXES, matching(m, True)) for m in range(chips)]
     returned = lax.all_to_all(back.reshape(devices, piece_rows, half), AXES, split_axis=0, concat_axis=0, tiled=True)
 

time: 147 us -> 150 us (1.020)
  local copies, waits for them, and re-layouts: 8.8 us -> 10.5 us
  waiting for transfers between devices: 30.6 us -> 32.2 us
    ppermute x0 -> x3, starting transfers between devices: none -> 3.47 us  [body(): lax.ppermute(adam, 'dp', [(i, (i + k) % chips) for i in range(chips)])]
    pallas_call x0 -> x1, Pallas kernels: none -> 2.6 us  [body(): pl.pallas_call(pack_kernel, out_shape=[shape((2 * half, order), BF16)] *...]
    pallas_call x8 -> x7, Pallas kernels: 20.4 us -> 18.1 us  [local(): pl.pallas_call(kernel, out_shape=outs, in_specs=[SMEM] + [VMEM] * (len(in...]
    all_to_all x1, starting transfers between devices: 11.7 us -> 9.59 us  [body(): lax.all_to_all(back.reshape(devices, piece_rows, half), AXES, split_axis=...]
    unnamed x26 -> x30, local copies, waits for them, and re-layouts: 7.57 us -> 9.24 us
    all_to_all x1, waiting for transfers between devices: 0.01 us -> 1.55 us  [body(): adam = lax.all_to_all(sent, 'fsdp', split_axis=0, concat_axis=0, tiled=True)]
  transfers between devices with their start and end apart: 13 -> 16, of which waited for: 3 -> 4; matrix products, arithmetic and copies ran while one was open for 1% -> 1% of each run, Pallas kernels for 11% -> 10%
where the time goes in v7:
time: 150 us
  blocking collectives  43.3 us (29%)
  starting transfers between devices  38.9 us (26%)
  waiting for transfers between devices  32.2 us (21%)
  Pallas kernels  23.8 us (16%)
  local copies, waits for them, and re-layouts  10.5 us (7%)
    all_to_all x1, blocking collectives, body(): lax.all_to_all(x, AXES, split_axis=0, concat_axis=0, tiled=True)  43.3 us
    ppermute x4, waiting for transfers between devices, body(): lax.ppermute(products[m], AXES, matching(m, True))  30.6 us
    pallas_call x7, Pallas kernels, local(): pl.pallas_call(kernel, out_shape=outs, in_specs=[SMEM] + [VMEM] * (len(in...  18.1 us
    all_to_all x1, starting transfers between devices, body(): lax.all_to_all(back.reshape(devices, piece_rows, half), AXES, split_axis=...  9.59 us
    ppermute x4, starting transfers between devices, body(): lax.ppermute(packed[m], AXES, matching(m, False))  9.37 us
    unnamed x30, local copies, waits for them, and re-layouts  9.24 us
    ppermute x4, starting transfers between devices, body(): lax.ppermute(products[m], AXES, matching(m, True))  8.95 us
    all_to_all x1, starting transfers between devices, body(): adam = lax.all_to_all(sent, 'fsdp', split_axis=0, concat_axis=0, tiled=True)  5.48 us
  transfers between devices with their start and end apart: 16, of which 4 were waited for; matrix products, arithmetic and copies ran while one was open for 1% of the time, Pallas kernels for 10%

profile of v7, /device:TPU:1, one launch (start us, length us, event | category | flops | bytes accessed | tf_op | source)
XLA Modules:
  0.0 149.7 jit_solution(6026850225961617174)
XLA Ops:
  3.2 2.6 %shard_map.103 = (bf16[256,1024]{1,0:T(8,128)(2,1)}, bf16[256,1024]{1,0:T(8,128)(2,1)}, bf16[256,1024]{1,0:T(8,128)(2,1)}, bf16[256,1024]{1,0:T(8,128)(2,1)}) custom-call(s32[3]{0:T(128)S(1)} %pad_add_fusion.spot_ref, bf16[2,256,1024]{2,1,0:T(8,128)(2,1)S(1)} %copy-done.3, bf16[2,1024,256]{2,1,0:T(8,128)(2,1)S(1)} %copy-done.4), custom_call_target="tpu_custom_call" | custom-call | bytes 4194304 | tf_op jit(solution)/shard_map/pallas_call | solution.py:200
  5.8 6.2 %collective-permute-start = (bf16[256,1024]{1,0:T(8,128)(2,1)}, bf16[256,1024]{1,0:T(8,128)(2,1)S(1)}, u32[]{:S(2)}, u32[]{:S(2)}) collective-permute-start(bf16[256,1024]{1,0:T(8,128)(2,1)} %get-tuple-element.38), channel_id=1, source_target_pairs={{0,0},{1,1},{2,4},{3,5},{4,2},{5,3},{6,6},{7,7},{8,8},{9,9},{10,12... | collective-permute-start | bytes 1572872 | tf_op jit(solution)/shard_map/ppermute | solution.py:209
  12.7 2.6 %collective-permute-start.3 = (bf16[256,1024]{1,0:T(8,128)(2,1)}, bf16[256,1024]{1,0:T(8,128)(2,1)}, u32[]{:S(2)}, u32[]{:S(2)}) collective-permute-start(bf16[256,1024]{1,0:T(8,128)(2,1)} %get-tuple-element.41), channel_id=1, source_target_pairs={{0,5},{1,4},{2,1},{3,0},{4,7},{5,6},{6,3},{7,2},{8,13},{9,12},{10,... | collective-permute-start | bytes 1572872 | tf_op jit(solution)/shard_map/ppermute | solution.py:209
  15.2 1.9 %shard_map.102 = bf16[256,16,128]{2,1,0:T(8,128)(2,1)} custom-call(s32[64]{0:T(128)S(1)} %copy-done.6, bf16[8,16,8,256]{3,2,1,0:T(8,128)(2,1)S(1)} %copy-done.2), custom_call_target="tpu_custom_call" | custom-call | bytes 1572864 | tf_op jit(solution)/shard_map/pallas_call | solution.py:17
  17.2 44.5 %conditional.1 = (bf16[256,16,128]{2,1,0:T(8,128)(2,1)}) conditional(s32[]{:T(128)} %bitcast.3, bf16[256,16,128]{2,1,0:T(8,128)(2,1)} %shard_map.102, bf16[256,16,128]{2,1,0:T(8,128)(2,1)} %shard_map.102), branch_computations={%region_0.1_spmd, %region_1.2_spmd} | conditional | bytes 4194312 | solution.py:223
  18.4 43.3 %all_to_all.14 = bf16[256,16,128]{2,1,0:T(8,128)(2,1)} all-to-all(bf16[256,16,128]{2,1,0:T(8,128)(2,1)S(1)} %copy.13), channel_id=1, replica_groups=mesh['fsdp'=64,'dp'=4] {'fsdp','dp'}, dimensions={0} | all-to-all | bytes 2097152 | tf_op jit(solution)/shard_map/cond/branch_1_fun/all_to_all | solution.py:225
  61.7 2.2 %shard_map.104 = (bf16[512,1024]{1,0:T(8,128)(2,1)}, bf16[4,128,1024]{2,1,0:T(8,128)(2,1)S(1)}) custom-call(s32[3]{0:T(128)S(1)} %pad_add_fusion.spot_ref, bf16[256,1024]{1,0:T(8,128)(2,1)S(1)} %collective-permute-done.refs_0_, bf16[256,1024]{1,0:T(8,128)(2,1)S(1)} %collective-permute-done.1.refs_1_, bf16[256,1024]{1,0:T(8,128)(2,1)S(1)} %collective-permute-done.2.refs_2_, ...), custom_call_target="tpu_custom_call" | custom-call | bytes 4194304 | tf_op jit(solution)/shard_map/pallas_call | solution.py:17
  65.4 2.3 %shard_map.108 = (f32[8,16,8,256]{3,2,1,0:T(8,128)}, f32[64,1,128]{2,1,0:T(1,128)}) custom-call(s32[64]{0:T(128)S(1)} %copy-done.6, bf16[8,16,8,256]{3,2,1,0:T(8,128)(2,1)S(1)} %copy-done.2, f32[8,16,8,256]{3,2,1,0:T(8,128)S(1)} %copy-done.5), custom_call_target="tpu_custom_call" | custom-call | bytes 2621440 | tf_op jit(solution)/shard_map/pallas_call | solution.py:17
  67.7 5.5 %all-to-all-start.1 = ((f32[64,1,128]{2,1,0:T(1,128)}), f32[64,1,128]{2,1,0:T(1,128)S(1)}, u32[]{:S(2)}, u32[]{:S(2)}) async-start(f32[64,1,128]{2,1,0:T(1,128)} %get-tuple-element.64), calls=%async_computation.1 | async-start | bytes 65536 | tf_op jit(solution)/shard_map/all_to_all | solution.py:217
  74.5 5.2 %shard_map.105 = (bf16[1024,1024]{1,0:T(8,128)(2,1)S(1)}, bf16[64,4,16,128]{3,2,1,0:T(8,128)(2,1)S(1)}, f32[8,128]{1,0:T(8,128)S(1)}) custom-call(s32[3]{0:T(128)S(1)} %pad_add_fusion.spot_ref, bf16[64,4,16,128]{3,2,1,0:T(8,128)(2,1)} %bitcast.4.own_ref, bf16[64,4,16,128]{3,2,1,0:T(8,128)(2,1)} %bitcast.5.other_ref, ...), custom_call_target="tpu_custom_call" | custom-call | flops 2147483648 | bytes 8388608 | tf_op jit(solution)/shard_map/pallas_call | solution.py:17
  81.0 1.6 %all-to-all-done.1 = f32[64,1,128]{2,1,0:T(1,128)S(1)} async-done(((f32[64,1,128]{2,1,0:T(1,128)}), f32[64,1,128]{2,1,0:T(1,128)S(1)}, u32[]{:S(2)}, u32[]{:S(2)}) %all-to-all-start.1) | async-done | bytes 32800 | tf_op jit(solution)/shard_map/all_to_all | solution.py:217
  82.9 2.2 %collective-permute-start.12 = (f32[1,128]{1,0:T(1,128)S(1)}, f32[1,128]{1,0:T(1,128)S(1)}, u32[]{:S(2)}, u32[]{:S(2)}) collective-permute-start(f32[1,128]{1,0:T(1,128)S(1)} %bitcast.11), channel_id=1, source_target_pairs={{0,2},{1,3},{2,0},{3,1},{4,6},{5,7},{6,4},{7,5},{8,10},{9,11},{10,... | collective-permute-start | bytes 1544 | tf_op jit(solution)/shard_map/ppermute | solution.py:249
  86.1 1.5 %collective-permute-start.10 = (f32[8,128]{1,0:T(8,128)S(1)}, f32[8,128]{1,0:T(8,128)S(1)}, u32[]{:S(2)}, u32[]{:S(2)}) collective-permute-start(f32[8,128]{1,0:T(8,128)S(1)} %get-tuple-element.65.norm_ref), channel_id=1, source_target_pairs={{0,4},{4,0},{8,12},{12,8},{16,20},{20,16},{24,28},{28,24},{32,36},... | collective-permute-start | bytes 12296 | tf_op jit(solution)/shard_map/ppermute | solution.py:247
  87.6 1.6 %copy-done.14 = bf16[1024,1024]{1,0:T(8,128)(2,1)S(1)} copy-done((bf16[1024,1024]{1,0:T(8,128)(2,1)S(1)}, bf16[1024,1024]{1,0:T(8,128)(2,1)}, u32[]{:S(2)}) %copy-start.14) | copy-done | bytes 2097176
  89.2 3.0 %shard_map.106 = (bf16[256,1024]{1,0:T(8,128)(2,1)S(1)}, bf16[256,1024]{1,0:T(8,128)(2,1)S(1)}, bf16[256,1024]{1,0:T(8,128)(2,1)S(1)}, bf16[256,1024]{1,0:T(8,128)(2,1)S(1)}) custom-call(s32[3]{0:T(128)S(1)} %pad_add_fusion.spot_ref, bf16[1024,1024]{1,0:T(8,128)(2,1)S(1)} %copy-done.14), custom_call_target="tpu_custom_call" | custom-call | flops 2147483648 | bytes 4194304 | tf_op jit(solution)/shard_map/pallas_call | solution.py:17
  92.3 1.9 %shard_map.109 = bf16[64,4,16,128]{3,2,1,0:T(8,128)(2,1)} custom-call(s32[3]{0:T(128)S(1)} %pad_add_fusion.spot_ref, bf16[64,4,16,128]{3,2,1,0:T(8,128)(2,1)S(1)} %get-tuple-element.62.update_ref, f32[8,128]{1,0:T(8,128)S(1)} %get-tuple-element.65.norm_ref, f32[8,128]{1,0:T(8,128)S(1)} %collective-permute-done.10.norm2_ref, f32[1,128]{1,0:T(1,128)S(1)} %bitcast.13, ...), custom_call_target="tpu_custom_call" | custom-call | bytes 2097152 | tf_op jit(solution)/shard_map/pallas_call | solution.py:17
  94.2 9.6 %all-to-all-start.2 = ((bf16[256,16,128]{2,1,0:T(8,128)(2,1)}), bf16[256,16,128]{2,1,0:T(8,128)(2,1)S(1)}, u32[]{:S(2)}, u32[]{:S(2)}) async-start(bf16[256,16,128]{2,1,0:T(8,128)(2,1)} %bitcast.7), calls=%async_computation.2 | async-start | bytes 2097152 | tf_op jit(solution)/shard_map/all_to_all | solution.py:258
  103.8 5.1 %collective-permute-start.6 = (bf16[256,1024]{1,0:T(8,128)(2,1)}, bf16[256,1024]{1,0:T(8,128)(2,1)S(1)}, u32[]{:S(2)}, u32[]{:S(2)}) collective-permute-start(bf16[256,1024]{1,0:T(8,128)(2,1)} %copy-done.12), channel_id=1, source_target_pairs={{0,0},{1,1},{4,2},{5,3},{2,4},{3,5},{6,6},{7,7},{8,8},{9,9},{12,10... | collective-permute-start | bytes 1572872 | tf_op jit(solution)/shard_map/ppermute | solution.py:257
  109.9 2.9 %collective-permute-start.9 = (bf16[256,1024]{1,0:T(8,128)(2,1)}, bf16[256,1024]{1,0:T(8,128)(2,1)S(1)}, u32[]{:S(2)}, u32[]{:S(2)}) collective-permute-start(bf16[256,1024]{1,0:T(8,128)(2,1)} %copy-done.9), channel_id=1, source_target_pairs={{5,0},{4,1},{1,2},{0,3},{7,4},{6,5},{3,6},{2,7},{13,8},{12,9},{9,1... | collective-permute-start | bytes 1572872 | tf_op jit(solution)/shard_map/ppermute | solution.py:257
  112.8 17.0 %collective-permute-done.6.p0 = bf16[256,1024]{1,0:T(8,128)(2,1)S(1)} collective-permute-done((bf16[256,1024]{1,0:T(8,128)(2,1)}, bf16[256,1024]{1,0:T(8,128)(2,1)S(1)}, u32[]{:S(2)}, u32[]{:S(2)}) %collective-permute-start.6) | collective-permute-done | bytes 524320 | tf_op jit(solution)/shard_map/ppermute | solution.py:257
  129.8 13.5 %collective-permute-done.7.p1 = bf16[256,1024]{1,0:T(8,128)(2,1)S(1)} collective-permute-done((bf16[256,1024]{1,0:T(8,128)(2,1)}, bf16[256,1024]{1,0:T(8,128)(2,1)S(1)}, u32[]{:S(2)}, u32[]{:S(2)}) %collective-permute-start.7) | collective-permute-done | bytes 524320 | tf_op jit(solution)/shard_map/ppermute | solution.py:257
  143.3 1.6 %copy-done.1 = f32[2,256,1024]{2,1,0:T(8,128)S(1)} copy-done((f32[2,256,1024]{2,1,0:T(8,128)S(1)}, f32[2,256,1024]{2,1,0:T(8,128)}, u32[]{:S(2)}) %copy-start.1) | copy-done | bytes 2097176
  144.9 3.1 %shard_map.107 = (f32[2,256,1024]{2,1,0:T(8,128)}, f32[2,256,1024]{2,1,0:T(8,128)}) custom-call(s32[3]{0:T(128)S(1)} %pad_add_fusion.spot_ref, bf16[256,1024]{1,0:T(8,128)(2,1)S(1)} %collective-permute-done.6.p0, bf16[256,1024]{1,0:T(8,128)(2,1)S(1)} %collective-permute-done.7.p1, bf16[256,1024]{1,0:T(8,128)(2,1)S(1)} %collective-permute-done.8.p2, ...), custom_call_target="tpu_custom_call" | custom-call | bytes 10485760 | tf_op jit(solution)/shard_map/pallas_call | solution.py:262
  148.0 1.6 %shard_map.110 = bf16[8,16,8,256]{3,2,1,0:T(8,128)(2,1)} custom-call(s32[64]{0:T(128)S(1)} %copy-done.6, bf16[256,16,128]{2,1,0:T(8,128)(2,1)S(1)} %all-to-all-done.2.values_ref), custom_call_target="tpu_custom_call" | custom-call | bytes 2097152 | tf_op jit(solution)/shard_map/pallas_call | solution.py:17
  (52 shorter events, 10.9 us)
Async XLA Ops:
  0.6 14.6 %copy-start.2 = (bf16[8,16,8,256]{3,2,1,0:T(8,128)(2,1)S(1)}, bf16[8,16,8,256]{3,2,1,0:T(8,128)(2,1)}, u32[]{:S(2)}) copy-start(bf16[8,16,8,256]{3,2,1,0:T(8,128)(2,1)} %grad_ref.3) | copy-start | bytes 1572868
  3.2 12.0 %copy-start.6 = (s32[64]{0:T(128)S(1)}, s32[64]{0:T(128)}, u32[]{:S(2)}) copy-start(s32[64]{0:T(128)} %slot_ref.5) | copy-start | bytes 772
  5.8 55.8 %collective-permute-start = (bf16[256,1024]{1,0:T(8,128)(2,1)}, bf16[256,1024]{1,0:T(8,128)(2,1)S(1)}, u32[]{:S(2)}, u32[]{:S(2)}) collective-permute-start(bf16[256,1024]{1,0:T(8,128)(2,1)} %get-tuple-element.38), channel_id=1, source_target_pairs={{0,0},{1,1},{2,4},{3,5},{4,2},{5,3},{6,6},{7,7},{8,8},{9,9},{10,12... | collective-permute-start | bytes 1572872 | tf_op jit(solution)/shard_map/ppermute | solution.py:209
  12.1 49.6 %collective-permute-start.1 = (bf16[256,1024]{1,0:T(8,128)(2,1)}, bf16[256,1024]{1,0:T(8,128)(2,1)S(1)}, u32[]{:S(2)}, u32[]{:S(2)}) collective-permute-start(bf16[256,1024]{1,0:T(8,128)(2,1)} %get-tuple-element.39), channel_id=1, source_target_pairs={{0,1},{1,0},{2,5},{3,4},{4,3},{5,2},{6,7},{7,6},{8,9},{9,8},{10,13... | collective-permute-start | bytes 1572872 | tf_op jit(solution)/shard_map/ppermute | solution.py:209
  12.6 49.0 %collective-permute-start.2 = (bf16[256,1024]{1,0:T(8,128)(2,1)}, bf16[256,1024]{1,0:T(8,128)(2,1)S(1)}, u32[]{:S(2)}, u32[]{:S(2)}) collective-permute-start(bf16[256,1024]{1,0:T(8,128)(2,1)} %get-tuple-element.40), channel_id=1, source_target_pairs={{0,4},{1,5},{2,0},{3,1},{4,6},{5,7},{6,2},{7,3},{8,12},{9,13},{10,... | collective-permute-start | bytes 1572872 | tf_op jit(solution)/shard_map/ppermute | solution.py:209
  12.7 49.0 %collective-permute-start.3 = (bf16[256,1024]{1,0:T(8,128)(2,1)}, bf16[256,1024]{1,0:T(8,128)(2,1)}, u32[]{:S(2)}, u32[]{:S(2)}) collective-permute-start(bf16[256,1024]{1,0:T(8,128)(2,1)} %get-tuple-element.41), channel_id=1, source_target_pairs={{0,5},{1,4},{2,1},{3,0},{4,7},{5,6},{6,3},{7,2},{8,13},{9,12},{10,... | collective-permute-start | bytes 1572872 | tf_op jit(solution)/shard_map/ppermute | solution.py:209
  61.7 3.7 %copy-start.5 = (f32[8,16,8,256]{3,2,1,0:T(8,128)S(1)}, f32[8,16,8,256]{3,2,1,0:T(8,128)}, u32[]{:S(2)}) copy-start(f32[8,16,8,256]{3,2,1,0:T(8,128)} %second_ref.1) | copy-start | bytes 3145732
  64.9 8.3 %collective-permute-start.5 = (bf16[512,1024]{1,0:T(8,128)(2,1)}, bf16[512,1024]{1,0:T(8,128)(2,1)S(1)}, u32[]{:S(2)}, u32[]{:S(2)}) collective-permute-start(bf16[512,1024]{1,0:T(8,128)(2,1)} %get-tuple-element.47.left_ref), channel_id=1, source_target_pairs={{0,4},{4,0},{8,12},{12,8},{16,20},{20,16},{24,28},{28,24},{32,36},... | collective-permute-start | bytes 3145736 | tf_op jit(solution)/shard_map/ppermute | solution.py:235
  64.9 8.3 %collective-permute-start.4 = (bf16[256,16,128]{2,1,0:T(8,128)(2,1)}, bf16[256,16,128]{2,1,0:T(8,128)(2,1)}, u32[]{:S(2)}, u32[]{:S(2)}) collective-permute-start(bf16[256,16,128]{2,1,0:T(8,128)(2,1)} %get-tuple-element.67), channel_id=1, source_target_pairs={{0,4},{4,0},{8,12},{12,8},{16,20},{20,16},{24,28},{28,24},{32,36},... | collective-permute-start | bytes 3145736 | tf_op jit(solution)/shard_map/ppermute | solution.py:236
  67.7 14.8 %all-to-all-start.1 = ((f32[64,1,128]{2,1,0:T(1,128)}), f32[64,1,128]{2,1,0:T(1,128)S(1)}, u32[]{:S(2)}, u32[]{:S(2)}) async-start(f32[64,1,128]{2,1,0:T(1,128)} %get-tuple-element.64), calls=%async_computation.1 | async-start | bytes 65536 | tf_op jit(solution)/shard_map/all_to_all | solution.py:217
  82.6 9.6 %collective-permute-start.11 = (f32[1,128]{1,0:T(1,128)S(1)}, f32[1,128]{1,0:T(1,128)S(1)}, u32[]{:S(2)}, u32[]{:S(2)}) collective-permute-start(f32[1,128]{1,0:T(1,128)S(1)} %bitcast.10), channel_id=1, source_target_pairs={{0,1},{1,2},{2,3},{3,0},{4,5},{5,6},{6,7},{7,4},{8,9},{9,10},{10,1... | collective-permute-start | bytes 1544 | tf_op jit(solution)/shard_map/ppermute | solution.py:249
  82.9 9.3 %collective-permute-start.12 = (f32[1,128]{1,0:T(1,128)S(1)}, f32[1,128]{1,0:T(1,128)S(1)}, u32[]{:S(2)}, u32[]{:S(2)}) collective-permute-start(f32[1,128]{1,0:T(1,128)S(1)} %bitcast.11), channel_id=1, source_target_pairs={{0,2},{1,3},{2,0},{3,1},{4,6},{5,7},{6,4},{7,5},{8,10},{9,11},{10,... | collective-permute-start | bytes 1544 | tf_op jit(solution)/shard_map/ppermute | solution.py:249
  85.2 7.1 %collective-permute-start.13 = (f32[1,128]{1,0:T(1,128)S(1)}, f32[1,128]{1,0:T(1,128)S(1)}, u32[]{:S(2)}, u32[]{:S(2)}) collective-permute-start(f32[1,128]{1,0:T(1,128)S(1)} %bitcast.12), channel_id=1, source_target_pairs={{0,3},{1,0},{2,1},{3,2},{4,7},{5,4},{6,5},{7,6},{8,11},{9,8},{10,9... | collective-permute-start | bytes 1544 | tf_op jit(solution)/shard_map/ppermute | solution.py:249
  86.1 6.2 %collective-permute-start.10 = (f32[8,128]{1,0:T(8,128)S(1)}, f32[8,128]{1,0:T(8,128)S(1)}, u32[]{:S(2)}, u32[]{:S(2)}) collective-permute-start(f32[8,128]{1,0:T(8,128)S(1)} %get-tuple-element.65.norm_ref), channel_id=1, source_target_pairs={{0,4},{4,0},{8,12},{12,8},{16,20},{20,16},{24,28},{28,24},{32,36},... | collective-permute-start | bytes 12296 | tf_op jit(solution)/shard_map/ppermute | solution.py:247
  92.2 2.0 %copy-start.9 = (bf16[256,1024]{1,0:T(8,128)(2,1)}, bf16[256,1024]{1,0:T(8,128)(2,1)S(1)}, u32[]{:S(2)}) copy-start(bf16[256,1024]{1,0:T(8,128)(2,1)S(1)} %get-tuple-element.58) | copy-start | bytes 1572868
  92.2 2.0 %copy-start.10 = (bf16[256,1024]{1,0:T(8,128)(2,1)}, bf16[256,1024]{1,0:T(8,128)(2,1)S(1)}, u32[]{:S(2)}) copy-start(bf16[256,1024]{1,0:T(8,128)(2,1)S(1)} %get-tuple-element.57) | copy-start | bytes 1572868
  92.2 2.0 %copy-start.11 = (bf16[256,1024]{1,0:T(8,128)(2,1)}, bf16[256,1024]{1,0:T(8,128)(2,1)S(1)}, u32[]{:S(2)}) copy-start(bf16[256,1024]{1,0:T(8,128)(2,1)S(1)} %get-tuple-element.56) | copy-start | bytes 1572868
  92.2 2.0 %copy-start.12 = (bf16[256,1024]{1,0:T(8,128)(2,1)}, bf16[256,1024]{1,0:T(8,128)(2,1)S(1)}, u32[]{:S(2)}) copy-start(bf16[256,1024]{1,0:T(8,128)(2,1)S(1)} %get-tuple-element.55) | copy-start | bytes 1572868
  92.2 51.1 %copy-start = (f32[2,256,1024]{2,1,0:T(8,128)S(1)}, f32[2,256,1024]{2,1,0:T(8,128)}, u32[]{:S(2)}) copy-start(f32[2,256,1024]{2,1,0:T(8,128)} %left_ref.3) | copy-start | bytes 6291460
  94.2 53.8 %all-to-all-start.2 = ((bf16[256,16,128]{2,1,0:T(8,128)(2,1)}), bf16[256,16,128]{2,1,0:T(8,128)(2,1)S(1)}, u32[]{:S(2)}, u32[]{:S(2)}) async-start(bf16[256,16,128]{2,1,0:T(8,128)(2,1)} %bitcast.7), calls=%async_computation.2 | async-start | bytes 2097152 | tf_op jit(solution)/shard_map/all_to_all | solution.py:258
  103.8 26.0 %collective-permute-start.6 = (bf16[256,1024]{1,0:T(8,128)(2,1)}, bf16[256,1024]{1,0:T(8,128)(2,1)S(1)}, u32[]{:S(2)}, u32[]{:S(2)}) collective-permute-start(bf16[256,1024]{1,0:T(8,128)(2,1)} %copy-done.12), channel_id=1, source_target_pairs={{0,0},{1,1},{4,2},{5,3},{2,4},{3,5},{6,6},{7,7},{8,8},{9,9},{12,10... | collective-permute-start | bytes 1572872 | tf_op jit(solution)/shard_map/ppermute | solution.py:257
  108.8 34.4 %collective-permute-start.7 = (bf16[256,1024]{1,0:T(8,128)(2,1)}, bf16[256,1024]{1,0:T(8,128)(2,1)S(1)}, u32[]{:S(2)}, u32[]{:S(2)}) collective-permute-start(bf16[256,1024]{1,0:T(8,128)(2,1)} %copy-done.11), channel_id=1, source_target_pairs={{1,0},{0,1},{5,2},{4,3},{3,4},{2,5},{7,6},{6,7},{9,8},{8,9},{13,10... | collective-permute-start | bytes 1572872 | tf_op jit(solution)/shard_map/ppermute | solution.py:257
  109.9 33.4 %collective-permute-start.8 = (bf16[256,1024]{1,0:T(8,128)(2,1)}, bf16[256,1024]{1,0:T(8,128)(2,1)S(1)}, u32[]{:S(2)}, u32[]{:S(2)}) collective-permute-start(bf16[256,1024]{1,0:T(8,128)(2,1)} %copy-done.10), channel_id=1, source_target_pairs={{4,0},{5,1},{0,2},{1,3},{6,4},{7,5},{2,6},{3,7},{12,8},{13,9},{8,1... | collective-permute-start | bytes 1572872 | tf_op jit(solution)/shard_map/ppermute | solution.py:257
  109.9 33.5 %collective-permute-start.9 = (bf16[256,1024]{1,0:T(8,128)(2,1)}, bf16[256,1024]{1,0:T(8,128)(2,1)S(1)}, u32[]{:S(2)}, u32[]{:S(2)}) collective-permute-start(bf16[256,1024]{1,0:T(8,128)(2,1)} %copy-done.9), channel_id=1, source_target_pairs={{5,0},{4,1},{1,2},{0,3},{7,4},{6,5},{3,6},{2,7},{13,8},{12,9},{9,1... | collective-permute-start | bytes 1572872 | tf_op jit(solution)/shard_map/ppermute | solution.py:257
  (7 other events, 9.2 us)

commit v8 on v6

--- a/solution.py
+++ b/solution.py
@@ -1,5 +1,3 @@
-import functools
-
 import jax
 import jax.numpy as jnp
 from jax import lax
@@ -145,13 +143,14 @@
     out_ref[...] = (update_ref[...].astype(F32) * scale[None, None]).astype(BF16)
 
 
-def stat_kernel(side, spot_ref, p0, p1, p2, p3, stat_ref, new_ref):
-    half = stat_ref.shape[1]
+def stat_kernel(spot_ref, p0, p1, p2, p3, left_ref, right_ref, new_left_ref, new_right_ref):
+    half = left_ref.shape[1]
     for m, ref in enumerate((p0, p1, p2, p3)):
 
         @pl.when(pl.program_id(0) == m)
         def _():
-            new_ref[0] = stat_ref[0] + ref[side * half : (side + 1) * half, :].astype(F32)
+            new_left_ref[0] = left_ref[0] + ref[:half, :].astype(F32)
+            new_right_ref[0] = right_ref[0] + ref[half:, :].astype(F32)
 
 
 def direction_kernel(slot_ref, values_ref, out_ref, wide):
@@ -196,7 +195,7 @@
     packed = pl.pallas_call(
         pack_kernel,
         out_shape=[shape((2 * half, order), BF16)] * chips,
-        in_specs=[SMEM] + [pl.BlockSpec(memory_space=pltpu.HBM)] * 2,
+        in_specs=[SMEM] + [pl.BlockSpec(memory_space=pl.ANY)] * 2,
         out_specs=[VMEM] * chips,
         scratch_shapes=[pltpu.SemaphoreType.DMA((chips * (1 + order // half),))],
         compiler_params=pltpu.CompilerParams(vmem_limit_bytes=4 * MIB),
@@ -222,7 +221,7 @@
     own, new_second, sent = lax.cond(
         block_slot[0] >= 0,
         spread,
-        lambda x, slots, g, second: (x, second, jnp.zeros((devices, 1, 128), F32)),
+        lambda x, slots, g, second: (jnp.zeros_like(x), jnp.zeros_like(second), jnp.zeros((devices, 1, 128), F32)),
         pieces, block_slot, gradient, second_moment,
     )
     adam = lax.all_to_all(sent, AXES, split_axis=0, concat_axis=0, tiled=True)
@@ -256,18 +255,15 @@
 
     whole = pl.BlockSpec((2 * half, order), lambda m, s: (0, 0))
     piece = pl.BlockSpec((1, half, order), lambda m, s: ((s[0] ^ m) & 1, (s[0] ^ m) >> 1, 0))
-    new_left, new_right = (
-        pl.pallas_call(
-            functools.partial(stat_kernel, side),
-            out_shape=shape(stat.shape, F32),
-            grid_spec=pltpu.PrefetchScalarGridSpec(
-                num_scalar_prefetch=1, grid=(chips,), in_specs=[whole] * chips + [piece], out_specs=piece
-            ),
-            compiler_params=pltpu.CompilerParams(vmem_limit_bytes=8 * MIB),
-            cost_estimate=pl.CostEstimate(flops=0, bytes_accessed=5 * MIB, transcendentals=0),
-        )(spot, *products, stat)
-        for side, stat in enumerate((stat_left, stat_right))
-    )
+    new_left, new_right = pl.pallas_call(
+        stat_kernel,
+        out_shape=[shape(stat_left.shape, F32), shape(stat_right.shape, F32)],
+        grid_spec=pltpu.PrefetchScalarGridSpec(
+            num_scalar_prefetch=1, grid=(chips,), in_specs=[whole] * chips + [piece] * 2, out_specs=[piece] * 2
+        ),
+        compiler_params=pltpu.CompilerParams(vmem_limit_bytes=10 * MIB),
+        cost_estimate=pl.CostEstimate(flops=0, bytes_accessed=10 * MIB, transcendentals=0),
+    )(spot, *products, stat_left, stat_right)
 
     direction = local(
         direction_kernel, shape(gradient.shape, gradient.dtype), (block_slot, returned),

time: 149 us -> 147 us (0.987)
  local copies, waits for them, and re-layouts: 13.6 us -> 11.9 us
  Pallas kernels: 24.2 us -> 22.7 us
    cond x2 -> x0, local copies, waits for them, and re-layouts: 3.34 us -> none
    pallas_call x2 -> x1, Pallas kernels: 4.89 us -> 3.08 us  [body(): pl.pallas_call(stat_kernel, out_shape=[shape(stat_left.shape, F32), shape...]
    unnamed x31 -> x30, local copies, waits for them, and re-layouts: 10.3 us -> 11.9 us
  transfers between devices with their start and end apart: 14 -> 14, of which waited for: 4 -> 4; matrix products, arithmetic and copies ran while one was open for 2% -> 0% of each run, Pallas kernels for 12% -> 11%
where the time goes in v8:
time: 147 us; the launch traced here: 146 us
  waiting for transfers between devices  57.5 us (39%)
  starting transfers between devices  52.9 us (36%)
  Pallas kernels  22.7 us (15%)
  local copies, waits for them, and re-layouts  11.9 us (8%)
    ppermute x4, waiting for transfers between devices, body(): lax.ppermute(products[m], AXES, matching(m, True))  30.6 us
    all_to_all x1, waiting for transfers between devices, spread(): x = lax.all_to_all(x, AXES, split_axis=0, concat_axis=0, tiled=True)  26.9 us
    pallas_call x7, Pallas kernels, local(): pl.pallas_call(kernel, out_shape=outs, in_specs=[SMEM] + [VMEM] * (len(in...  17.4 us
    all_to_all x1, starting transfers between devices, spread(): x = lax.all_to_all(x, AXES, split_axis=0, concat_axis=0, tiled=True)  13.4 us
    unnamed x30, local copies, waits for them, and re-layouts  11.9 us
    all_to_all x1, starting transfers between devices, body(): lax.all_to_all(back.reshape(devices, piece_rows, half), AXES, split_axis=...  11.7 us
    ppermute x4, starting transfers between devices, body(): lax.ppermute(packed[m], AXES, matching(m, False))  9.37 us
    ppermute x4, starting transfers between devices, body(): lax.ppermute(products[m], AXES, matching(m, True))  8.95 us
  transfers between devices with their start and end apart: 14, of which 4 were waited for; matrix products, arithmetic and copies ran while one was open for 0% of the time, Pallas kernels for 11%

profile of v8, /device:TPU:1, one launch (start us, length us, event | category | flops | bytes accessed | tf_op | source)
XLA Modules:
  0.0 146.0 jit_solution(17852721928916781206)
XLA Ops:
  0.7 1.2 copy-done.2
  2.0 1.2 copy-done.3
  3.2 2.3 %shard_map.104 = (bf16[256,1024]{1,0:T(8,128)(2,1)}, bf16[256,1024]{1,0:T(8,128)(2,1)}, bf16[256,1024]{1,0:T(8,128)(2,1)S(1)}, bf16[256,1024]{1,0:T(8,128)(2,1)S(1)}) custom-call(s32[3]{0:T(128)S(1)} %pad_add_fusion.spot_ref, bf16[2,256,1024]{2,1,0:T(8,128)(2,1)S(1)} %copy-done.2, bf16[2,1024,256]{2,1,0:T(8,128)(2,1)S(1)} %copy-done.3), custom_call_target="tpu_custom_call" | custom-call | bytes 4194304 | tf_op jit(solution)/shard_map/pallas_call | solution.py:195
  5.4 6.2 %collective-permute-start = (bf16[256,1024]{1,0:T(8,128)(2,1)}, bf16[256,1024]{1,0:T(8,128)(2,1)S(1)}, u32[]{:S(2)}, u32[]{:S(2)}) collective-permute-start(bf16[256,1024]{1,0:T(8,128)(2,1)} %get-tuple-element.47), channel_id=1, source_target_pairs={{0,0},{1,1},{2,4},{3,5},{4,2},{5,3},{6,6},{7,7},{8,8},{9,9},{10,12... | collective-permute-start | bytes 1572872 | tf_op jit(solution)/shard_map/ppermute | solution.py:204
  12.3 2.6 %collective-permute-start.3 = (bf16[256,1024]{1,0:T(8,128)(2,1)S(1)}, bf16[256,1024]{1,0:T(8,128)(2,1)S(1)}, u32[]{:S(2)}, u32[]{:S(2)}) collective-permute-start(bf16[256,1024]{1,0:T(8,128)(2,1)S(1)} %get-tuple-element.50), channel_id=1, source_target_pairs={{0,5},{1,4},{2,1},{3,0},{4,7},{5,6},{6,3},{7,2},{8,13},{9,12},{10,... | collective-permute-start | bytes 1572872 | tf_op jit(solution)/shard_map/ppermute | solution.py:204
  14.9 2.4 %shard_map.103 = bf16[256,16,128]{2,1,0:T(8,128)(2,1)} custom-call(s32[64]{0:T(128)S(1)} %copy-done.14, bf16[8,16,8,256]{3,2,1,0:T(8,128)(2,1)} %grad_ref.1), custom_call_target="tpu_custom_call" | custom-call | bytes 1572864 | tf_op jit(solution)/shard_map/pallas_call | solution.py:17
  17.3 43.5 %conditional.1 = (bf16[256,16,128]{2,1,0:T(8,128)(2,1)}, f32[8,16,8,256]{3,2,1,0:T(8,128)}, f32[256,1,128]{2,1,0:T(1,128)}) conditional(s32[]{:T(128)} %bitcast.3, () %tuple.18, (bf16[256,16,128]{2,1,0:T(8,128)(2,1)}, s32[64]{0:T(128)S(1)}, bf16[8,16,8,256]{3,2,1,0:T(8,128)(2,1)}, f32[8,16,8,256]{3,2,1,0:T(8,128)}) %tuple.25), branch_computations={%region_0.1_spmd, %region_1.2_spmd} | conditional | bytes 5767224 | solution.py:221
  17.3 13.4 %all-to-all-start = ((bf16[256,16,128]{2,1,0:T(8,128)(2,1)}), bf16[256,16,128]{2,1,0:T(8,128)(2,1)}, u32[]{:S(2)}, u32[]{:S(2)}) async-start(bf16[256,16,128]{2,1,0:T(8,128)(2,1)} %get-tuple-element.8), calls=%async_computation | async-start | bytes 2097152 | tf_op jit(solution)/shard_map/cond/branch_1_fun/all_to_all | solution.py:212
  30.7 3.1 %branch_1_fun.1 = (f32[8,16,8,256]{3,2,1,0:T(8,128)}, f32[256,1,128]{2,1,0:T(1,128)}) custom-call(s32[64]{0:T(128)S(1)} %get-tuple-element.9.slot_ref, bf16[8,16,8,256]{3,2,1,0:T(8,128)(2,1)} %get-tuple-element.10.grad_ref, f32[8,16,8,256]{3,2,1,0:T(8,128)} %get-tuple-element.75.second_ref), custom_call_target="tpu_custom_call" | custom-call | bytes 2621440 | tf_op jit(solution)/shard_map/cond/branch_1_fun/pallas_call | solution.py:17
  33.9 26.9 %all-to-all-done = bf16[256,16,128]{2,1,0:T(8,128)(2,1)} async-done(((bf16[256,16,128]{2,1,0:T(8,128)(2,1)}), bf16[256,16,128]{2,1,0:T(8,128)(2,1)}, u32[]{:S(2)}, u32[]{:S(2)}) %all-to-all-start) | async-done | bytes 1048608 | tf_op jit(solution)/shard_map/cond/branch_1_fun/all_to_all | solution.py:212
  63.0 6.6 %all-to-all-start.1 = ((f32[256,1,128]{2,1,0:T(1,128)}), f32[256,1,128]{2,1,0:T(1,128)S(1)}, u32[]{:S(2)}, u32[]{:S(2)}) async-start(f32[256,1,128]{2,1,0:T(1,128)} %get-tuple-element.73), calls=%async_computation.1 | async-start | bytes 262144 | tf_op jit(solution)/shard_map/all_to_all | solution.py:227
  71.5 1.2 copy-done.5
  75.2 4.6 %shard_map.106 = (bf16[1024,1024]{1,0:T(8,128)(2,1)S(1)}, bf16[64,4,16,128]{3,2,1,0:T(8,128)(2,1)S(1)}, f32[8,128]{1,0:T(8,128)S(1)}) custom-call(s32[3]{0:T(128)S(1)} %pad_add_fusion.spot_ref, bf16[64,4,16,128]{3,2,1,0:T(8,128)(2,1)} %bitcast.4.own_ref, bf16[64,4,16,128]{3,2,1,0:T(8,128)(2,1)S(1)} %bitcast.8, ...), custom_call_target="tpu_custom_call" | custom-call | flops 2147483648 | bytes 8388608 | tf_op jit(solution)/shard_map/pallas_call | solution.py:17
  79.8 2.4 %collective-permute-start.10 = (f32[8,128]{1,0:T(8,128)S(1)}, f32[8,128]{1,0:T(8,128)S(1)}, u32[]{:S(2)}, u32[]{:S(2)}) collective-permute-start(f32[8,128]{1,0:T(8,128)S(1)} %get-tuple-element.72.norm_ref), channel_id=1, source_target_pairs={{0,4},{4,0},{8,12},{12,8},{16,20},{20,16},{24,28},{28,24},{32,36},... | collective-permute-start | bytes 12296 | tf_op jit(solution)/shard_map/ppermute | solution.py:245
  82.1 3.0 %shard_map.107 = (bf16[256,1024]{1,0:T(8,128)(2,1)S(1)}, bf16[256,1024]{1,0:T(8,128)(2,1)S(1)}, bf16[256,1024]{1,0:T(8,128)(2,1)S(1)}, bf16[256,1024]{1,0:T(8,128)(2,1)S(1)}) custom-call(s32[3]{0:T(128)S(1)} %pad_add_fusion.spot_ref, bf16[1024,1024]{1,0:T(8,128)(2,1)S(1)} %get-tuple-element.59.grad), custom_call_target="tpu_custom_call" | custom-call | flops 2147483648 | bytes 4194304 | tf_op jit(solution)/shard_map/pallas_call | solution.py:17
  86.4 2.0 %shard_map.109 = bf16[64,4,16,128]{3,2,1,0:T(8,128)(2,1)} custom-call(s32[3]{0:T(128)S(1)} %pad_add_fusion.spot_ref, bf16[64,4,16,128]{3,2,1,0:T(8,128)(2,1)S(1)} %get-tuple-element.71.update_ref, f32[8,128]{1,0:T(8,128)S(1)} %get-tuple-element.72.norm_ref, f32[8,128]{1,0:T(8,128)S(1)} %collective-permute-done.10.norm2_ref, ...), custom_call_target="tpu_custom_call" | custom-call | bytes 2097152 | tf_op jit(solution)/shard_map/pallas_call | solution.py:17
  88.4 11.7 %all-to-all-start.2 = ((bf16[256,16,128]{2,1,0:T(8,128)(2,1)}), bf16[256,16,128]{2,1,0:T(8,128)(2,1)S(1)}, u32[]{:S(2)}, u32[]{:S(2)}) async-start(bf16[256,16,128]{2,1,0:T(8,128)(2,1)} %bitcast.6), calls=%async_computation.2 | async-start | bytes 2097152 | tf_op jit(solution)/shard_map/all_to_all | solution.py:254
  100.1 5.1 %collective-permute-start.6 = (bf16[256,1024]{1,0:T(8,128)(2,1)}, bf16[256,1024]{1,0:T(8,128)(2,1)S(1)}, u32[]{:S(2)}, u32[]{:S(2)}) collective-permute-start(bf16[256,1024]{1,0:T(8,128)(2,1)} %copy-done.13), channel_id=1, source_target_pairs={{0,0},{1,1},{4,2},{5,3},{2,4},{3,5},{6,6},{7,7},{8,8},{9,9},{12,10... | collective-permute-start | bytes 1572872 | tf_op jit(solution)/shard_map/ppermute | solution.py:253
  106.2 2.9 %collective-permute-start.9 = (bf16[256,1024]{1,0:T(8,128)(2,1)}, bf16[256,1024]{1,0:T(8,128)(2,1)S(1)}, u32[]{:S(2)}, u32[]{:S(2)}) collective-permute-start(bf16[256,1024]{1,0:T(8,128)(2,1)} %copy-done.10), channel_id=1, source_target_pairs={{5,0},{4,1},{1,2},{0,3},{7,4},{6,5},{3,6},{2,7},{13,8},{12,9},{9,1... | collective-permute-start | bytes 1572872 | tf_op jit(solution)/shard_map/ppermute | solution.py:253
  109.1 17.0 %collective-permute-done.6.p0 = bf16[256,1024]{1,0:T(8,128)(2,1)S(1)} collective-permute-done((bf16[256,1024]{1,0:T(8,128)(2,1)}, bf16[256,1024]{1,0:T(8,128)(2,1)S(1)}, u32[]{:S(2)}, u32[]{:S(2)}) %collective-permute-start.6) | collective-permute-done | bytes 524320 | tf_op jit(solution)/shard_map/ppermute | solution.py:253
  126.1 13.5 %collective-permute-done.7.p1 = bf16[256,1024]{1,0:T(8,128)(2,1)S(1)} collective-permute-done((bf16[256,1024]{1,0:T(8,128)(2,1)}, bf16[256,1024]{1,0:T(8,128)(2,1)S(1)}, u32[]{:S(2)}, u32[]{:S(2)}) %collective-permute-start.7) | collective-permute-done | bytes 524320 | tf_op jit(solution)/shard_map/ppermute | solution.py:253
  139.7 1.6 %copy-done.1 = f32[2,256,1024]{2,1,0:T(8,128)S(1)} copy-done((f32[2,256,1024]{2,1,0:T(8,128)S(1)}, f32[2,256,1024]{2,1,0:T(8,128)}, u32[]{:S(2)}) %copy-start.1) | copy-done | bytes 2097176
  141.2 3.1 %shard_map.108 = (f32[2,256,1024]{2,1,0:T(8,128)}, f32[2,256,1024]{2,1,0:T(8,128)}) custom-call(s32[3]{0:T(128)S(1)} %pad_add_fusion.spot_ref, bf16[256,1024]{1,0:T(8,128)(2,1)S(1)} %collective-permute-done.6.p0, bf16[256,1024]{1,0:T(8,128)(2,1)S(1)} %collective-permute-done.7.p1, bf16[256,1024]{1,0:T(8,128)(2,1)S(1)} %collective-permute-done.8.p2, ...), custom_call_target="tpu_custom_call" | custom-call | bytes 10485760 | tf_op jit(solution)/shard_map/pallas_call | solution.py:258
  144.3 1.6 %shard_map.110 = bf16[8,16,8,256]{3,2,1,0:T(8,128)(2,1)} custom-call(s32[64]{0:T(128)S(1)} %copy-done.14, bf16[256,16,128]{2,1,0:T(8,128)(2,1)S(1)} %all-to-all-done.2.values_ref), custom_call_target="tpu_custom_call" | custom-call | bytes 2097152 | tf_op jit(solution)/shard_map/pallas_call | solution.py:17
  (45 shorter events, 9.6 us)
Async XLA Ops:
  0.6 14.2 %copy-start.14 = (s32[64]{0:T(128)S(1)}, s32[64]{0:T(128)}, u32[]{:S(2)}) copy-start(s32[64]{0:T(128)} %slot_ref.3) | copy-start | bytes 772
  0.7 1.2 copy-start.2
  2.0 1.2 copy-start.3
  5.4 55.3 %collective-permute-start = (bf16[256,1024]{1,0:T(8,128)(2,1)}, bf16[256,1024]{1,0:T(8,128)(2,1)S(1)}, u32[]{:S(2)}, u32[]{:S(2)}) collective-permute-start(bf16[256,1024]{1,0:T(8,128)(2,1)} %get-tuple-element.47), channel_id=1, source_target_pairs={{0,0},{1,1},{2,4},{3,5},{4,2},{5,3},{6,6},{7,7},{8,8},{9,9},{10,12... | collective-permute-start | bytes 1572872 | tf_op jit(solution)/shard_map/ppermute | solution.py:204
  11.7 49.1 %collective-permute-start.1 = (bf16[256,1024]{1,0:T(8,128)(2,1)}, bf16[256,1024]{1,0:T(8,128)(2,1)S(1)}, u32[]{:S(2)}, u32[]{:S(2)}) collective-permute-start(bf16[256,1024]{1,0:T(8,128)(2,1)} %get-tuple-element.48), channel_id=1, source_target_pairs={{0,1},{1,0},{2,5},{3,4},{4,3},{5,2},{6,7},{7,6},{8,9},{9,8},{10,13... | collective-permute-start | bytes 1572872 | tf_op jit(solution)/shard_map/ppermute | solution.py:204
  12.2 48.5 %collective-permute-start.2 = (bf16[256,1024]{1,0:T(8,128)(2,1)S(1)}, bf16[256,1024]{1,0:T(8,128)(2,1)S(1)}, u32[]{:S(2)}, u32[]{:S(2)}) collective-permute-start(bf16[256,1024]{1,0:T(8,128)(2,1)S(1)} %get-tuple-element.49), channel_id=1, source_target_pairs={{0,4},{1,5},{2,0},{3,1},{4,6},{5,7},{6,2},{7,3},{8,12},{9,13},{10,... | collective-permute-start | bytes 1572872 | tf_op jit(solution)/shard_map/ppermute | solution.py:204
  12.3 48.5 %collective-permute-start.3 = (bf16[256,1024]{1,0:T(8,128)(2,1)S(1)}, bf16[256,1024]{1,0:T(8,128)(2,1)S(1)}, u32[]{:S(2)}, u32[]{:S(2)}) collective-permute-start(bf16[256,1024]{1,0:T(8,128)(2,1)S(1)} %get-tuple-element.50), channel_id=1, source_target_pairs={{0,5},{1,4},{2,1},{3,0},{4,7},{5,6},{6,3},{7,2},{8,13},{9,12},{10,... | collective-permute-start | bytes 1572872 | tf_op jit(solution)/shard_map/ppermute | solution.py:204
  17.3 43.5 %all-to-all-start = ((bf16[256,16,128]{2,1,0:T(8,128)(2,1)}), bf16[256,16,128]{2,1,0:T(8,128)(2,1)}, u32[]{:S(2)}, u32[]{:S(2)}) async-start(bf16[256,16,128]{2,1,0:T(8,128)(2,1)} %get-tuple-element.8), calls=%async_computation | async-start | bytes 2097152 | tf_op jit(solution)/shard_map/cond/branch_1_fun/all_to_all | solution.py:212
  62.4 7.1 %collective-permute-start.5 = (bf16[512,1024]{1,0:T(8,128)(2,1)S(1)}, bf16[512,1024]{1,0:T(8,128)(2,1)S(1)}, u32[]{:S(2)}, u32[]{:S(2)}) collective-permute-start(bf16[512,1024]{1,0:T(8,128)(2,1)S(1)} %get-tuple-element.56.left_ref), channel_id=1, source_target_pairs={{0,4},{4,0},{8,12},{12,8},{16,20},{20,16},{24,28},{28,24},{32,36},... | collective-permute-start | bytes 3145736 | tf_op jit(solution)/shard_map/ppermute | solution.py:234
  62.4 8.1 %collective-permute-start.4 = (bf16[256,16,128]{2,1,0:T(8,128)(2,1)}, bf16[256,16,128]{2,1,0:T(8,128)(2,1)S(1)}, u32[]{:S(2)}, u32[]{:S(2)}) collective-permute-start(bf16[256,16,128]{2,1,0:T(8,128)(2,1)} %get-tuple-element.51), channel_id=1, source_target_pairs={{0,4},{4,0},{8,12},{12,8},{16,20},{20,16},{24,28},{28,24},{32,36},... | collective-permute-start | bytes 3145736 | tf_op jit(solution)/shard_map/ppermute | solution.py:235
  63.0 23.4 %all-to-all-start.1 = ((f32[256,1,128]{2,1,0:T(1,128)}), f32[256,1,128]{2,1,0:T(1,128)S(1)}, u32[]{:S(2)}, u32[]{:S(2)}) async-start(f32[256,1,128]{2,1,0:T(1,128)} %get-tuple-element.73), calls=%async_computation.1 | async-start | bytes 262144 | tf_op jit(solution)/shard_map/all_to_all | solution.py:227
  71.5 1.2 copy-start.5
  72.7 1.2 copy-start.7
  73.9 1.2 copy-start.9
  79.8 6.6 %collective-permute-start.10 = (f32[8,128]{1,0:T(8,128)S(1)}, f32[8,128]{1,0:T(8,128)S(1)}, u32[]{:S(2)}, u32[]{:S(2)}) collective-permute-start(f32[8,128]{1,0:T(8,128)S(1)} %get-tuple-element.72.norm_ref), channel_id=1, source_target_pairs={{0,4},{4,0},{8,12},{12,8},{16,20},{20,16},{24,28},{28,24},{32,36},... | collective-permute-start | bytes 12296 | tf_op jit(solution)/shard_map/ppermute | solution.py:245
  85.1 1.1 copy-start.12
  85.1 1.3 copy-start.13
  86.4 53.3 %copy-start = (f32[2,256,1024]{2,1,0:T(8,128)S(1)}, f32[2,256,1024]{2,1,0:T(8,128)}, u32[]{:S(2)}) copy-start(f32[2,256,1024]{2,1,0:T(8,128)} %left_ref.3) | copy-start | bytes 6291460
  88.4 56.0 %all-to-all-start.2 = ((bf16[256,16,128]{2,1,0:T(8,128)(2,1)}), bf16[256,16,128]{2,1,0:T(8,128)(2,1)S(1)}, u32[]{:S(2)}, u32[]{:S(2)}) async-start(bf16[256,16,128]{2,1,0:T(8,128)(2,1)} %bitcast.6), calls=%async_computation.2 | async-start | bytes 2097152 | tf_op jit(solution)/shard_map/all_to_all | solution.py:254
  100.1 26.0 %collective-permute-start.6 = (bf16[256,1024]{1,0:T(8,128)(2,1)}, bf16[256,1024]{1,0:T(8,128)(2,1)S(1)}, u32[]{:S(2)}, u32[]{:S(2)}) collective-permute-start(bf16[256,1024]{1,0:T(8,128)(2,1)} %copy-done.13), channel_id=1, source_target_pairs={{0,0},{1,1},{4,2},{5,3},{2,4},{3,5},{6,6},{7,7},{8,8},{9,9},{12,10... | collective-permute-start | bytes 1572872 | tf_op jit(solution)/shard_map/ppermute | solution.py:253
  105.2 34.4 %collective-permute-start.7 = (bf16[256,1024]{1,0:T(8,128)(2,1)}, bf16[256,1024]{1,0:T(8,128)(2,1)S(1)}, u32[]{:S(2)}, u32[]{:S(2)}) collective-permute-start(bf16[256,1024]{1,0:T(8,128)(2,1)} %copy-done.12), channel_id=1, source_target_pairs={{1,0},{0,1},{5,2},{4,3},{3,4},{2,5},{7,6},{6,7},{9,8},{8,9},{13,10... | collective-permute-start | bytes 1572872 | tf_op jit(solution)/shard_map/ppermute | solution.py:253
  106.2 33.4 %collective-permute-start.8 = (bf16[256,1024]{1,0:T(8,128)(2,1)}, bf16[256,1024]{1,0:T(8,128)(2,1)S(1)}, u32[]{:S(2)}, u32[]{:S(2)}) collective-permute-start(bf16[256,1024]{1,0:T(8,128)(2,1)} %copy-done.11), channel_id=1, source_target_pairs={{4,0},{5,1},{0,2},{1,3},{6,4},{7,5},{2,6},{3,7},{12,8},{13,9},{8,1... | collective-permute-start | bytes 1572872 | tf_op jit(solution)/shard_map/ppermute | solution.py:253
  106.2 33.5 %collective-permute-start.9 = (bf16[256,1024]{1,0:T(8,128)(2,1)}, bf16[256,1024]{1,0:T(8,128)(2,1)S(1)}, u32[]{:S(2)}, u32[]{:S(2)}) collective-permute-start(bf16[256,1024]{1,0:T(8,128)(2,1)} %copy-done.10), channel_id=1, source_target_pairs={{5,0},{4,1},{1,2},{0,3},{7,4},{6,5},{3,6},{2,7},{13,8},{12,9},{9,1... | collective-permute-start | bytes 1572872 | tf_op jit(solution)/shard_map/ppermute | solution.py:253
  139.7 1.6 %copy-start.1 = (f32[2,256,1024]{2,1,0:T(8,128)S(1)}, f32[2,256,1024]{2,1,0:T(8,128)}, u32[]{:S(2)}) copy-start(f32[2,256,1024]{2,1,0:T(8,128)} %right_ref.3) | copy-start | bytes 6291460
  (5 other events, 4.7 us)

commit v9 on v8

--- a/solution.py
+++ b/solution.py
@@ -143,14 +143,27 @@
     out_ref[...] = (update_ref[...].astype(F32) * scale[None, None]).astype(BF16)
 
 
-def stat_kernel(spot_ref, p0, p1, p2, p3, left_ref, right_ref, new_left_ref, new_right_ref):
-    half = left_ref.shape[1]
+def stat_kernel(spot_ref, p0, p1, p2, p3, left_ref, right_ref, new_left_ref, new_right_ref, held, sems):
+    half = held.shape[1]
+    moves = []
     for m, ref in enumerate((p0, p1, p2, p3)):
-
-        @pl.when(pl.program_id(0) == m)
-        def _():
-            new_left_ref[0] = left_ref[0] + ref[:half, :].astype(F32)
-            new_right_ref[0] = right_ref[0] + ref[half:, :].astype(F32)
+        to = spot_ref[0] ^ m
+        part = pl.ds(pl.multiple_of((to >> 1) * half, half), half)
+        for side, (old, new) in enumerate(((left_ref, new_left_ref), (right_ref, new_right_ref))):
+            i = 2 * m + side
+            moves.append((
+                pltpu.make_async_copy(old.at[to & 1, part], held.at[i], sems.at[0, i]),
+                ref.at[pl.ds(side * half, half)],
+                pltpu.make_async_copy(held.at[i], new.at[to & 1, part], sems.at[1, i]),
+            ))
+    for read, _, _ in moves:
+        read.start()
+    for i, (read, term, write) in enumerate(moves):
+        read.wait()
+        held[i] = held[i] + term[...].astype(F32)
+        write.start()
+    for _, _, write in moves:
+        write.wait()
 
 
 def direction_kernel(slot_ref, values_ref, out_ref, wide):
@@ -196,9 +209,9 @@
         pack_kernel,
         out_shape=[shape((2 * half, order), BF16)] * chips,
         in_specs=[SMEM] + [pl.BlockSpec(memory_space=pl.ANY)] * 2,
-        out_specs=[VMEM] * chips,
+        out_specs=[pl.BlockSpec(memory_space=pl.ANY)] * chips,
         scratch_shapes=[pltpu.SemaphoreType.DMA((chips * (1 + order // half),))],
-        compiler_params=pltpu.CompilerParams(vmem_limit_bytes=4 * MIB),
+        compiler_params=pltpu.CompilerParams(vmem_limit_bytes=60 * MIB),
         cost_estimate=pl.CostEstimate(flops=0, bytes_accessed=4 * MIB, transcendentals=0),
     )(spot, root_left, root_right)
     roots = [lax.ppermute(packed[m], AXES, matching(m, False)) for m in range(chips)]
@@ -253,14 +266,13 @@
     products = [lax.ppermute(products[m], AXES, matching(m, True)) for m in range(chips)]
     returned = lax.all_to_all(back.reshape(devices, piece_rows, half), AXES, split_axis=0, concat_axis=0, tiled=True)
 
-    whole = pl.BlockSpec((2 * half, order), lambda m, s: (0, 0))
-    piece = pl.BlockSpec((1, half, order), lambda m, s: ((s[0] ^ m) & 1, (s[0] ^ m) >> 1, 0))
+    anywhere = pl.BlockSpec(memory_space=pl.ANY)
     new_left, new_right = pl.pallas_call(
         stat_kernel,
         out_shape=[shape(stat_left.shape, F32), shape(stat_right.shape, F32)],
-        grid_spec=pltpu.PrefetchScalarGridSpec(
-            num_scalar_prefetch=1, grid=(chips,), in_specs=[whole] * chips + [piece] * 2, out_specs=[piece] * 2
-        ),
+        in_specs=[SMEM] + [VMEM] * chips + [anywhere] * 2,
+        out_specs=[anywhere] * 2,
+        scratch_shapes=[pltpu.VMEM((2 * chips, half, order), F32), pltpu.SemaphoreType.DMA((2, 2 * chips))],
         compiler_params=pltpu.CompilerParams(vmem_limit_bytes=10 * MIB),
         cost_estimate=pl.CostEstimate(flops=0, bytes_accessed=10 * MIB, transcendentals=0),
     )(spot, *products, stat_left, stat_right)

time: 147 us -> 208 us (1.41)
  Pallas kernels: 22.7 us -> 85.4 us
  local copies, waits for them, and re-layouts: 11.9 us -> 9.46 us
    pallas_call x1, Pallas kernels: 2.25 us -> 65.6 us  [body(): pl.pallas_call(pack_kernel, out_shape=[shape((2 * half, order), BF16)] *...]
    unnamed x30, local copies, waits for them, and re-layouts: 11.9 us -> 9.46 us
  transfers between devices with their start and end apart: 14 -> 14, of which waited for: 4 -> 4; matrix products, arithmetic and copies ran while one was open for 0% -> 0% of each run, Pallas kernels for 11% -> 7%
where the time goes in v9:
time: 208 us; the launch traced here: 207 us
  Pallas kernels  85.4 us (41%)
  waiting for transfers between devices  57.7 us (28%)
  starting transfers between devices  52.9 us (25%)
  local copies, waits for them, and re-layouts  9.46 us (5%)
    pallas_call x1, Pallas kernels, body(): pl.pallas_call(pack_kernel, out_shape=[shape((2 * half, order), BF16)] *...  65.6 us
    ppermute x4, waiting for transfers between devices, body(): lax.ppermute(products[m], AXES, matching(m, True))  30.6 us
    all_to_all x1, waiting for transfers between devices, spread(): x = lax.all_to_all(x, AXES, split_axis=0, concat_axis=0, tiled=True)  27.1 us
    pallas_call x7, Pallas kernels, local(): pl.pallas_call(kernel, out_shape=outs, in_specs=[SMEM] + [VMEM] * (len(in...  16.7 us
    all_to_all x1, starting transfers between devices, spread(): x = lax.all_to_all(x, AXES, split_axis=0, concat_axis=0, tiled=True)  13.4 us
    all_to_all x1, starting transfers between devices, body(): lax.all_to_all(back.reshape(devices, piece_rows, half), AXES, split_axis=...  11.7 us
    unnamed x30, local copies, waits for them, and re-layouts  9.46 us
    ppermute x4, starting transfers between devices, body(): lax.ppermute(packed[m], AXES, matching(m, False))  9.37 us
  transfers between devices with their start and end apart: 14, of which 4 were waited for; matrix products, arithmetic and copies ran while one was open for 0% of the time, Pallas kernels for 7%

profile of v9, /device:TPU:1, one launch (start us, length us, event | category | flops | bytes accessed | tf_op | source)
XLA Modules:
  0.0 206.9 jit_solution(11408527414543590790)
XLA Ops:
  1.3 65.6 %shard_map.104 = (bf16[256,1024]{1,0:T(8,128)(2,1)}, bf16[256,1024]{1,0:T(8,128)(2,1)}, bf16[256,1024]{1,0:T(8,128)(2,1)}, bf16[256,1024]{1,0:T(8,128)(2,1)}) custom-call(s32[3]{0:T(128)} %pad_add_fusion.spot_ref, bf16[2,256,1024]{2,1,0:T(8,128)(2,1)} %left_ref.2, bf16[2,1024,256]{2,1,0:T(8,128)(2,1)} %right_ref.2), custom_call_target="tpu_custom_call" | custom-call | bytes 4194304 | tf_op jit(solution)/shard_map/pallas_call | solution.py:208
  66.9 6.2 %collective-permute-start = (bf16[256,1024]{1,0:T(8,128)(2,1)}, bf16[256,1024]{1,0:T(8,128)(2,1)S(1)}, u32[]{:S(2)}, u32[]{:S(2)}) collective-permute-start(bf16[256,1024]{1,0:T(8,128)(2,1)} %get-tuple-element.47), channel_id=1, source_target_pairs={{0,0},{1,1},{2,4},{3,5},{4,2},{5,3},{6,6},{7,7},{8,8},{9,9},{10,12... | collective-permute-start | bytes 1572872 | tf_op jit(solution)/shard_map/ppermute | solution.py:217
  73.7 2.6 %collective-permute-start.3 = (bf16[256,1024]{1,0:T(8,128)(2,1)}, bf16[256,1024]{1,0:T(8,128)(2,1)S(1)}, u32[]{:S(2)}, u32[]{:S(2)}) collective-permute-start(bf16[256,1024]{1,0:T(8,128)(2,1)} %get-tuple-element.50), channel_id=1, source_target_pairs={{0,5},{1,4},{2,1},{3,0},{4,7},{5,6},{6,3},{7,2},{8,13},{9,12},{10,... | collective-permute-start | bytes 1572872 | tf_op jit(solution)/shard_map/ppermute | solution.py:217
  76.4 1.9 shard_map.103
  78.3 43.5 %conditional.1 = (bf16[256,16,128]{2,1,0:T(8,128)(2,1)}, f32[8,16,8,256]{3,2,1,0:T(8,128)}, f32[256,1,128]{2,1,0:T(1,128)}) conditional(s32[]{:T(128)} %bitcast.3, () %tuple.18, (bf16[256,16,128]{2,1,0:T(8,128)(2,1)}, s32[64]{0:T(128)S(1)}, bf16[8,16,8,256]{3,2,1,0:T(8,128)(2,1)S(1)}, f32[8,16,8,256]{3,2,1,0:T(8,128)}) %tuple.26), branch_computations={%region_0.1_spmd, %region_1.2_spmd} | conditional | bytes 5767224 | solution.py:234
  78.3 13.4 %all-to-all-start = ((bf16[256,16,128]{2,1,0:T(8,128)(2,1)}), bf16[256,16,128]{2,1,0:T(8,128)(2,1)}, u32[]{:S(2)}, u32[]{:S(2)}) async-start(bf16[256,16,128]{2,1,0:T(8,128)(2,1)} %get-tuple-element.8), calls=%async_computation | async-start | bytes 2097152 | tf_op jit(solution)/shard_map/cond/branch_1_fun/all_to_all | solution.py:225
  91.7 3.0 %branch_1_fun.1 = (f32[8,16,8,256]{3,2,1,0:T(8,128)}, f32[256,1,128]{2,1,0:T(1,128)}) custom-call(s32[64]{0:T(128)S(1)} %get-tuple-element.9.slot_ref, bf16[8,16,8,256]{3,2,1,0:T(8,128)(2,1)S(1)} %get-tuple-element.10.grad_ref, f32[8,16,8,256]{3,2,1,0:T(8,128)} %get-tuple-element.75.second_ref), custom_call_target="tpu_custom_call" | custom-call | bytes 2621440 | tf_op jit(solution)/shard_map/cond/branch_1_fun/pallas_call | solution.py:17
  94.7 27.1 %all-to-all-done = bf16[256,16,128]{2,1,0:T(8,128)(2,1)} async-done(((bf16[256,16,128]{2,1,0:T(8,128)(2,1)}), bf16[256,16,128]{2,1,0:T(8,128)(2,1)}, u32[]{:S(2)}, u32[]{:S(2)}) %all-to-all-start) | async-done | bytes 1048608 | tf_op jit(solution)/shard_map/cond/branch_1_fun/all_to_all | solution.py:225
  124.0 6.6 %all-to-all-start.1 = ((f32[256,1,128]{2,1,0:T(1,128)}), f32[256,1,128]{2,1,0:T(1,128)S(1)}, u32[]{:S(2)}, u32[]{:S(2)}) async-start(f32[256,1,128]{2,1,0:T(1,128)} %get-tuple-element.73), calls=%async_computation.1 | async-start | bytes 262144 | tf_op jit(solution)/shard_map/all_to_all | solution.py:240
  132.5 1.2 copy-done.4
  133.7 1.2 copy-done.6
  134.9 1.2 copy-done.8
  136.2 4.6 %shard_map.106 = (bf16[1024,1024]{1,0:T(8,128)(2,1)S(1)}, bf16[64,4,16,128]{3,2,1,0:T(8,128)(2,1)S(1)}, f32[8,128]{1,0:T(8,128)S(1)}) custom-call(s32[3]{0:T(128)S(1)} %copy-done.2, bf16[64,4,16,128]{3,2,1,0:T(8,128)(2,1)} %bitcast.4.own_ref, bf16[64,4,16,128]{3,2,1,0:T(8,128)(2,1)S(1)} %bitcast.8, bf16[512,1024]{1,0:T(8,128)(2,1)S(1)} %get-tuple-element.56.left_ref, ...), custom_call_target="tpu_custom_call" | custom-call | flops 2147483648 | bytes 8388608 | tf_op jit(solution)/shard_map/pallas_call | solution.py:17
  140.8 2.4 %collective-permute-start.10 = (f32[8,128]{1,0:T(8,128)S(1)}, f32[8,128]{1,0:T(8,128)S(1)}, u32[]{:S(2)}, u32[]{:S(2)}) collective-permute-start(f32[8,128]{1,0:T(8,128)S(1)} %get-tuple-element.72.norm_ref), channel_id=1, source_target_pairs={{0,4},{4,0},{8,12},{12,8},{16,20},{20,16},{24,28},{28,24},{32,36},... | collective-permute-start | bytes 12296 | tf_op jit(solution)/shard_map/ppermute | solution.py:258
  143.1 3.0 %shard_map.107 = (bf16[256,1024]{1,0:T(8,128)(2,1)S(1)}, bf16[256,1024]{1,0:T(8,128)(2,1)S(1)}, bf16[256,1024]{1,0:T(8,128)(2,1)S(1)}, bf16[256,1024]{1,0:T(8,128)(2,1)S(1)}) custom-call(s32[3]{0:T(128)S(1)} %copy-done.2, bf16[1024,1024]{1,0:T(8,128)(2,1)S(1)} %get-tuple-element.59.grad), custom_call_target="tpu_custom_call" | custom-call | flops 2147483648 | bytes 4194304 | tf_op jit(solution)/shard_map/pallas_call | solution.py:17
  147.4 2.0 shard_map.109
  149.4 11.7 %all-to-all-start.2 = ((bf16[256,16,128]{2,1,0:T(8,128)(2,1)}), bf16[256,16,128]{2,1,0:T(8,128)(2,1)S(1)}, u32[]{:S(2)}, u32[]{:S(2)}) async-start(bf16[256,16,128]{2,1,0:T(8,128)(2,1)} %bitcast.6), calls=%async_computation.2 | async-start | bytes 2097152 | tf_op jit(solution)/shard_map/all_to_all | solution.py:267
  161.1 5.1 %collective-permute-start.6 = (bf16[256,1024]{1,0:T(8,128)(2,1)}, bf16[256,1024]{1,0:T(8,128)(2,1)S(1)}, u32[]{:S(2)}, u32[]{:S(2)}) collective-permute-start(bf16[256,1024]{1,0:T(8,128)(2,1)} %copy-done.12), channel_id=1, source_target_pairs={{0,0},{1,1},{4,2},{5,3},{2,4},{3,5},{6,6},{7,7},{8,8},{9,9},{12,10... | collective-permute-start | bytes 1572872 | tf_op jit(solution)/shard_map/ppermute | solution.py:266
  167.2 2.9 %collective-permute-start.9 = (bf16[256,1024]{1,0:T(8,128)(2,1)}, bf16[256,1024]{1,0:T(8,128)(2,1)S(1)}, u32[]{:S(2)}, u32[]{:S(2)}) collective-permute-start(bf16[256,1024]{1,0:T(8,128)(2,1)} %copy-done.9), channel_id=1, source_target_pairs={{5,0},{4,1},{1,2},{0,3},{7,4},{6,5},{3,6},{2,7},{13,8},{12,9},{9,1... | collective-permute-start | bytes 1572872 | tf_op jit(solution)/shard_map/ppermute | solution.py:266
  170.1 17.0 %collective-permute-done.6.p0 = bf16[256,1024]{1,0:T(8,128)(2,1)S(1)} collective-permute-done((bf16[256,1024]{1,0:T(8,128)(2,1)}, bf16[256,1024]{1,0:T(8,128)(2,1)S(1)}, u32[]{:S(2)}, u32[]{:S(2)}) %collective-permute-start.6) | collective-permute-done | bytes 524320 | tf_op jit(solution)/shard_map/ppermute | solution.py:266
  187.1 13.5 %collective-permute-done.7.p1 = bf16[256,1024]{1,0:T(8,128)(2,1)S(1)} collective-permute-done((bf16[256,1024]{1,0:T(8,128)(2,1)}, bf16[256,1024]{1,0:T(8,128)(2,1)S(1)}, u32[]{:S(2)}, u32[]{:S(2)}) %collective-permute-start.7) | collective-permute-done | bytes 524320 | tf_op jit(solution)/shard_map/ppermute | solution.py:266
  200.7 1.6 copy-done.1
  202.3 3.0 %shard_map.108 = (f32[2,256,1024]{2,1,0:T(8,128)}, f32[2,256,1024]{2,1,0:T(8,128)}) custom-call(s32[3]{0:T(128)S(1)} %copy-done.2, bf16[256,1024]{1,0:T(8,128)(2,1)S(1)} %collective-permute-done.6.p0, bf16[256,1024]{1,0:T(8,128)(2,1)S(1)} %collective-permute-done.7.p1, bf16[256,1024]{1,0:T(8,128)(2,1)S(1)} %collective-permute-done.8.p2, ...), custom_call_target="tpu_custom_call" | custom-call | bytes 10485760 | tf_op jit(solution)/shard_map/pallas_call | solution.py:270
  205.3 1.6 shard_map.110
  (45 shorter events, 7.8 us)
Async XLA Ops:
  0.6 75.7 %copy-start.14 = (s32[64]{0:T(128)S(1)}, s32[64]{0:T(128)}, u32[]{:S(2)}) copy-start(s32[64]{0:T(128)} %slot_ref.3) | copy-start | bytes 772
  0.6 75.7 %copy-start.13 = (bf16[8,16,8,256]{3,2,1,0:T(8,128)(2,1)S(1)}, bf16[8,16,8,256]{3,2,1,0:T(8,128)(2,1)}, u32[]{:S(2)}) copy-start(bf16[8,16,8,256]{3,2,1,0:T(8,128)(2,1)} %grad_ref.1) | copy-start | bytes 1572868
  66.9 54.8 %collective-permute-start = (bf16[256,1024]{1,0:T(8,128)(2,1)}, bf16[256,1024]{1,0:T(8,128)(2,1)S(1)}, u32[]{:S(2)}, u32[]{:S(2)}) collective-permute-start(bf16[256,1024]{1,0:T(8,128)(2,1)} %get-tuple-element.47), channel_id=1, source_target_pairs={{0,0},{1,1},{2,4},{3,5},{4,2},{5,3},{6,6},{7,7},{8,8},{9,9},{10,12... | collective-permute-start | bytes 1572872 | tf_op jit(solution)/shard_map/ppermute | solution.py:217
  73.2 48.6 %collective-permute-start.1 = (bf16[256,1024]{1,0:T(8,128)(2,1)}, bf16[256,1024]{1,0:T(8,128)(2,1)S(1)}, u32[]{:S(2)}, u32[]{:S(2)}) collective-permute-start(bf16[256,1024]{1,0:T(8,128)(2,1)} %get-tuple-element.48), channel_id=1, source_target_pairs={{0,1},{1,0},{2,5},{3,4},{4,3},{5,2},{6,7},{7,6},{8,9},{9,8},{10,13... | collective-permute-start | bytes 1572872 | tf_op jit(solution)/shard_map/ppermute | solution.py:217
  73.7 48.0 %collective-permute-start.2 = (bf16[256,1024]{1,0:T(8,128)(2,1)}, bf16[256,1024]{1,0:T(8,128)(2,1)S(1)}, u32[]{:S(2)}, u32[]{:S(2)}) collective-permute-start(bf16[256,1024]{1,0:T(8,128)(2,1)} %get-tuple-element.49), channel_id=1, source_target_pairs={{0,4},{1,5},{2,0},{3,1},{4,6},{5,7},{6,2},{7,3},{8,12},{9,13},{10,... | collective-permute-start | bytes 1572872 | tf_op jit(solution)/shard_map/ppermute | solution.py:217
  73.7 48.0 %collective-permute-start.3 = (bf16[256,1024]{1,0:T(8,128)(2,1)}, bf16[256,1024]{1,0:T(8,128)(2,1)S(1)}, u32[]{:S(2)}, u32[]{:S(2)}) collective-permute-start(bf16[256,1024]{1,0:T(8,128)(2,1)} %get-tuple-element.50), channel_id=1, source_target_pairs={{0,5},{1,4},{2,1},{3,0},{4,7},{5,6},{6,3},{7,2},{8,13},{9,12},{10,... | collective-permute-start | bytes 1572872 | tf_op jit(solution)/shard_map/ppermute | solution.py:217
  78.3 43.5 %copy-start.2 = (s32[3]{0:T(128)S(1)}, s32[3]{0:T(128)}, u32[]{:S(2)}) copy-start(s32[3]{0:T(128)} %pad_add_fusion.spot_ref) | copy-start | bytes 40
  78.3 43.5 %all-to-all-start = ((bf16[256,16,128]{2,1,0:T(8,128)(2,1)}), bf16[256,16,128]{2,1,0:T(8,128)(2,1)}, u32[]{:S(2)}, u32[]{:S(2)}) async-start(bf16[256,16,128]{2,1,0:T(8,128)(2,1)} %get-tuple-element.8), calls=%async_computation | async-start | bytes 2097152 | tf_op jit(solution)/shard_map/cond/branch_1_fun/all_to_all | solution.py:225
  123.4 7.1 %collective-permute-start.5 = (bf16[512,1024]{1,0:T(8,128)(2,1)S(1)}, bf16[512,1024]{1,0:T(8,128)(2,1)S(1)}, u32[]{:S(2)}, u32[]{:S(2)}) collective-permute-start(bf16[512,1024]{1,0:T(8,128)(2,1)S(1)} %get-tuple-element.56.left_ref), channel_id=1, source_target_pairs={{0,4},{4,0},{8,12},{12,8},{16,20},{20,16},{24,28},{28,24},{32,36},... | collective-permute-start | bytes 3145736 | tf_op jit(solution)/shard_map/ppermute | solution.py:247
  123.5 8.1 %collective-permute-start.4 = (bf16[256,16,128]{2,1,0:T(8,128)(2,1)}, bf16[256,16,128]{2,1,0:T(8,128)(2,1)S(1)}, u32[]{:S(2)}, u32[]{:S(2)}) collective-permute-start(bf16[256,16,128]{2,1,0:T(8,128)(2,1)} %get-tuple-element.51), channel_id=1, source_target_pairs={{0,4},{4,0},{8,12},{12,8},{16,20},{20,16},{24,28},{28,24},{32,36},... | collective-permute-start | bytes 3145736 | tf_op jit(solution)/shard_map/ppermute | solution.py:248
  124.0 23.4 %all-to-all-start.1 = ((f32[256,1,128]{2,1,0:T(1,128)}), f32[256,1,128]{2,1,0:T(1,128)S(1)}, u32[]{:S(2)}, u32[]{:S(2)}) async-start(f32[256,1,128]{2,1,0:T(1,128)} %get-tuple-element.73), calls=%async_computation.1 | async-start | bytes 262144 | tf_op jit(solution)/shard_map/all_to_all | solution.py:240
  132.5 1.2 copy-start.4
  133.7 1.2 copy-start.6
  134.9 1.2 copy-start.8
  140.8 6.6 %collective-permute-start.10 = (f32[8,128]{1,0:T(8,128)S(1)}, f32[8,128]{1,0:T(8,128)S(1)}, u32[]{:S(2)}, u32[]{:S(2)}) collective-permute-start(f32[8,128]{1,0:T(8,128)S(1)} %get-tuple-element.72.norm_ref), channel_id=1, source_target_pairs={{0,4},{4,0},{8,12},{12,8},{16,20},{20,16},{24,28},{28,24},{32,36},... | collective-permute-start | bytes 12296 | tf_op jit(solution)/shard_map/ppermute | solution.py:258
  146.1 1.1 copy-start.11
  146.1 1.3 copy-start.12
  147.4 53.3 %copy-start = (f32[2,256,1024]{2,1,0:T(8,128)S(1)}, f32[2,256,1024]{2,1,0:T(8,128)}, u32[]{:S(2)}) copy-start(f32[2,256,1024]{2,1,0:T(8,128)} %left_ref.3) | copy-start | bytes 6291460
  149.4 55.9 %all-to-all-start.2 = ((bf16[256,16,128]{2,1,0:T(8,128)(2,1)}), bf16[256,16,128]{2,1,0:T(8,128)(2,1)S(1)}, u32[]{:S(2)}, u32[]{:S(2)}) async-start(bf16[256,16,128]{2,1,0:T(8,128)(2,1)} %bitcast.6), calls=%async_computation.2 | async-start | bytes 2097152 | tf_op jit(solution)/shard_map/all_to_all | solution.py:267
  161.1 26.0 %collective-permute-start.6 = (bf16[256,1024]{1,0:T(8,128)(2,1)}, bf16[256,1024]{1,0:T(8,128)(2,1)S(1)}, u32[]{:S(2)}, u32[]{:S(2)}) collective-permute-start(bf16[256,1024]{1,0:T(8,128)(2,1)} %copy-done.12), channel_id=1, source_target_pairs={{0,0},{1,1},{4,2},{5,3},{2,4},{3,5},{6,6},{7,7},{8,8},{9,9},{12,10... | collective-permute-start | bytes 1572872 | tf_op jit(solution)/shard_map/ppermute | solution.py:266
  166.2 34.4 %collective-permute-start.7 = (bf16[256,1024]{1,0:T(8,128)(2,1)}, bf16[256,1024]{1,0:T(8,128)(2,1)S(1)}, u32[]{:S(2)}, u32[]{:S(2)}) collective-permute-start(bf16[256,1024]{1,0:T(8,128)(2,1)} %copy-done.11), channel_id=1, source_target_pairs={{1,0},{0,1},{5,2},{4,3},{3,4},{2,5},{7,6},{6,7},{9,8},{8,9},{13,10... | collective-permute-start | bytes 1572872 | tf_op jit(solution)/shard_map/ppermute | solution.py:266
  167.2 33.4 %collective-permute-start.8 = (bf16[256,1024]{1,0:T(8,128)(2,1)}, bf16[256,1024]{1,0:T(8,128)(2,1)S(1)}, u32[]{:S(2)}, u32[]{:S(2)}) collective-permute-start(bf16[256,1024]{1,0:T(8,128)(2,1)} %copy-done.10), channel_id=1, source_target_pairs={{4,0},{5,1},{0,2},{1,3},{6,4},{7,5},{2,6},{3,7},{12,8},{13,9},{8,1... | collective-permute-start | bytes 1572872 | tf_op jit(solution)/shard_map/ppermute | solution.py:266
  167.2 33.5 %collective-permute-start.9 = (bf16[256,1024]{1,0:T(8,128)(2,1)}, bf16[256,1024]{1,0:T(8,128)(2,1)S(1)}, u32[]{:S(2)}, u32[]{:S(2)}) collective-permute-start(bf16[256,1024]{1,0:T(8,128)(2,1)} %copy-done.9), channel_id=1, source_target_pairs={{5,0},{4,1},{1,2},{0,3},{7,4},{6,5},{3,6},{2,7},{13,8},{12,9},{9,1... | collective-permute-start | bytes 1572872 | tf_op jit(solution)/shard_map/ppermute | solution.py:266
  200.7 1.6 copy-start.1
  (5 other events, 4.7 us)
